TPU v7x, 512 devices: a whole 4x4x16 slice. The times are simulated.
512 devices in a mesh: group: 8 (over y, core), loop: 16 (over x, z_hi), mp: 4 (over z_lo).
Axes of the slice: x: 4, y: 4, z: 16 (z_hi: 4, z_lo: 4; z = z_hi * 4 + z_lo), core: 2. Of those that a mesh axis runs over, the one named last changes fastest.
Arguments:
- hidden_in: bfloat16 [16384, 8192], P(('group', 'loop'), 'mp'), may hold values from -11 to 11
- norm_gain: float32 [8192], P('mp'), may hold values from 0.5 to 1.5
- key_cotangent: bfloat16 [16384, 1024], P(('group', 'loop'), 'mp'), may hold values from -0.046875 to 0.046875
- value_cotangent: bfloat16 [16384, 1024], P(('group', 'loop'), 'mp'), may hold values from -0.046875 to 0.046875
- union_ids: int32 [128], replicated, may hold values from 0 to 8191, as said below
Outputs:
- grad_key: float32 [4, 2048, 1024], P('mp', ('group', 'loop'))
- grad_value: float32 [4, 2048, 1024], P('mp', ('group', 'loop'))
- union_key: float32 [128, 1024], replicated
- union_value: float32 [128, 1024], replicated
Inputs may be any that keep to these rules, and one draw needn't show every extreme that they name: `union_ids`: 128 distinct row indices in increasing order, the first 0 and the last 8191.
All inputs are finite; a program needn't handle non-finite values.
Results may differ from a plain program's by a relative error of at most 0.0041.
Values may be sent and summed in bfloat16 or wider, within the bound.
No kernel may reach another device: no remote copies, remote signals or barrier semaphores. Data moves between devices by JAX's collectives and lax.ppermute only.
A program may use at most 128 MiB of HBM per device.

v0:
```python
import jax
import jax.numpy as jnp
from jax import lax
from jax.sharding import PartitionSpec as P


def per_device(hidden_in, norm_gain, key_cotangent, value_cotangent, union_ids):
    local_width = hidden_in.shape[1]
    head_cols = key_cotangent.shape[1] * lax.axis_size("mp")
    full_width = local_width * lax.axis_size("mp")
    hidden_f = hidden_in.astype(jnp.float32)
    local_squares = jnp.sum(hidden_f * hidden_f, axis=-1)
    total_squares = lax.psum(local_squares, "mp")
    mean_square = (total_squares / full_width)[:, None]
    normed = (hidden_f * lax.rsqrt(mean_square + 1e-05) * norm_gain).astype(jnp.bfloat16)
    stacked = jnp.stack([key_cotangent, value_cotangent], axis=0)
    partial_value = jnp.einsum(
        "tr,ktn->rkn",
        normed,
        lax.all_gather(stacked, "mp", axis=2, tiled=True),
        preferred_element_type=jnp.float32,
    )
    partial_value = partial_value.reshape(local_width, 2 * head_cols)
    first_row = lax.axis_index("mp") * local_width
    local_ids = union_ids - first_row
    inside = (local_ids >= 0) & (local_ids < local_width)
    safe_ids = jnp.clip(local_ids, 0, local_width - 1)
    union_part = jnp.where(inside[:, None], jnp.take(partial_value, safe_ids, axis=0), 0.0)
    union_sum = lax.psum(union_part, ("group", "loop", "mp"))
    row_index = lax.iota(jnp.int32, local_width) + first_row
    in_union = jnp.any(row_index[:, None] == union_ids[None, :], axis=1)
    bulk = jnp.where(in_union[:, None], 0.0, partial_value).astype(jnp.bfloat16)
    all_cols = bulk.shape[1]
    count = lax.axis_size(("group", "loop"))
    pieces = bulk.reshape(count, local_width // count, all_cols)
    received = lax.all_to_all(pieces, ("group", "loop"), split_axis=0, concat_axis=0, tiled=True)
    total_rows = jnp.sum(received, axis=0, dtype=jnp.float32)
    grad_key = total_rows[None, :, :head_cols]
    grad_value = total_rows[None, :, head_cols:]
    union_key = union_sum[:, :head_cols]
    union_value = union_sum[:, head_cols:]
    return (grad_key, grad_value, union_key, union_value)


def solution(mesh):
    return jax.shard_map(
        per_device,
        mesh=mesh,
        in_specs=(
            P(("group", "loop"), "mp"),
            P("mp"),
            P(("group", "loop"), "mp"),
            P(("group", "loop"), "mp"),
            P(),
        ),
        out_specs=(P("mp", ("group", "loop"), None), P("mp", ("group", "loop"), None), P(), P()),
        check_vma=False,
    )
```

profile of v0, /device:TPU:1, one launch (start us, length us, event | category | flops | bytes accessed | tf_op | source)
XLA Modules:
  0.0 880.8 jit_solution(7301884601444834069)
XLA Ops:
  7.2 0.9 copy.17
  8.1 1.0 copy.16
  9.1 16.3 %all_gather.3 = bf16[2,128,1024]{1,2,0:T(8,128)(2,1)S(1)} all-gather(bf16[2,128,256]{1,2,0:T(8,128)(2,1)S(1)} %pad_maximum_fusion), channel_id=1, replica_groups=mesh['group'=8,'loop'=16,'mp'=4] {'mp'}, dimensions={2}, use_global_device_ids=true | all-gather | bytes 655360 | tf_op jit(solution)/shard_map/all_gather | solution.py:20
  25.4 1.2 fusion
  26.6 8.9 %psum.14 = f32[128]{0:T(128)S(1)} all-reduce(f32[128]{0:T(128)S(1)} %fusion), channel_id=1, replica_groups=mesh['group'=8,'loop'=16,'mp'=4] {'mp'}, use_global_device_ids=true, to_apply=%region_2.3 | all-reduce | flops 128 | bytes 1024 | tf_op jit(solution)/shard_map/psum | solution.py:13
  35.5 9.2 %fusion.4 = f32[2048,2,1024]{0,2,1:T(8,128)} fusion(bf16[2,128,1024]{1,2,0:T(8,128)(2,1)S(1)} %all_gather.3, bf16[128,2048]{1,0:T(8,128)(2,1)} %param.5, f32[2048]{0:T(1024)} %param.6, f32[128]{0:T(128)S(1)} %add_rsqrt_fusion), kind=kOutput, calls=%fused_computation.11 | convolution fusion | flops 1074790400 | bytes 17834496 | tf_op jit(solution)/shard_map/tr,ktn->rkn/dot_general | solution.py:17
  44.7 24.1 %copy.18 = bf16[2048,2,1024]{2,1,0:T(2,128)(2,1)} copy(f32[2048,2,1024]{0,2,1:T(8,128)} %fusion.4) | data formatting | bytes 25165824 | tf_op jit(solution)/shard_map/tr,ktn->rkn/dot_general | solution.py:17
  68.8 0.0 copy-start
  68.8 14.4 %reshape.36 = bf16[128,16,2048]{2,1,0:T(8,128)(2,1)} reshape(bf16[2048,2,1024]{2,1,0:T(2,128)(2,1)} %copy.18) | data formatting | bytes 16777216 | tf_op jit(solution)/shard_map/reshape | solution.py:23
  83.3 0.0 copy-done
  83.3 0.6 compare_reduce_fusion
  83.9 0.1 broadcast_in_dim.50
  84.0 8.1 select_convert_fusion
  92.1 24.7 %all-to-all-start = ((bf16[128,16,2048]{2,1,0:T(8,128)(2,1)}), bf16[128,16,2048]{2,1,0:T(8,128)(2,1)}, u32[]{:S(2)}, u32[]{:S(2)}) async-start(bf16[128,16,2048]{2,1,0:T(8,128)(2,1)} %select_convert_fusion), calls=%async_computation | async-start | bytes 16777216 | tf_op jit(solution)/shard_map/all_to_all | solution.py:36
  116.7 0.0 all-reduce.2.cloned.1.call-start
  116.8 17.6 %copy.19 = f32[2048,2048]{1,0:T(8,128)} copy(f32[2048,2048]{0,1:T(8,128)} %bitcast.11) | data formatting | bytes 33554432 | tf_op jit(solution)/shard_map/reshape | solution.py:23
  134.4 7.2 gather_fusion
  141.7 1.2 select_select_fusion
  142.9 0.0 all-reduce.2.cloned.1.call-update
  142.9 723.5 %all-reduce.2.cloned.1.call-done = f32[128,2048]{1,0:T(8,128)} async-done(((f32[128,2048]{1,0:T(8,128)}), f32[128,2048]{1,0:T(8,128)}) %all-reduce.2.cloned.1.call-update) | async-done | bytes 1048592 | tf_op jit(solution)/shard_map/psum | solution.py:29
  866.5 2.3 fusion.8
  868.7 0.0 all-to-all-done
  868.7 4.6 convert_reduce_fusion
  873.3 0.7 slice_bitcast_fusion
  (5 shorter events, 0.0 us)
Async XLA Ops:
  68.8 14.5 %copy-start = (s32[128]{0:T(128)S(1)}, s32[128]{0:T(128)}, u32[]{:S(2)}) copy-start(s32[128]{0:T(128)} %param.9) | copy-start | bytes 1540
  92.1 776.7 %all-to-all-start = ((bf16[128,16,2048]{2,1,0:T(8,128)(2,1)}), bf16[128,16,2048]{2,1,0:T(8,128)(2,1)}, u32[]{:S(2)}, u32[]{:S(2)}) async-start(bf16[128,16,2048]{2,1,0:T(8,128)(2,1)} %select_convert_fusion), calls=%async_computation | async-start | bytes 16777216 | tf_op jit(solution)/shard_map/all_to_all | solution.py:36
  116.7 749.7 %all-reduce.2.cloned.1.call-start = ((), (), s32[]{:S(2)}) async-start(), calls=%async_computation.1 | async-start | bytes 2097152 | tf_op jit(solution)/shard_map/psum | solution.py:29
Sparse Core Ops, SparseCore 0:
  143.0 723.3 all-reduce.1
where the time goes:
time: 882 us; the launch traced here: 881 us
  waiting for transfers between devices  724 us (82%)
  local copies, waits for them, and re-layouts  68.3 us (8%)
  blocking collectives  25.2 us (3%)
  starting transfers between devices  24.7 us (3%)
  other arithmetic  15.8 us (2%)
  between operations  14.1 us (2%)
  matrix products  9.18 us (1%)
    psum x1, waiting for transfers between devices, per_device(): union_sum = lax.psum(union_part, ('group', 'loop', 'mp'))  724 us
    reshape x2, local copies, waits for them, and re-layouts, per_device(): partial_value = partial_value.reshape(local_width, 2 * head_cols)  32 us
    all_to_all x1, starting transfers between devices, per_device(): lax.all_to_all(pieces, ('group', 'loop'), split_axis=0, concat_axis=0, ti...  24.7 us
    dot_general x1, local copies, waits for them, and re-layouts, per_device(): jnp.einsum('tr,ktn->rkn', normed, lax.all_gather(stacked, 'mp', axis=2, t...  24.1 us
  transfers between devices with their start and end apart: 2, of which 1 were waited for; matrix products, arithmetic and copies ran while one was open for 3% of the time, Pallas kernels for 0%

commit v1 on v0

v1 whole, which is shorter than its diff:
```python
import jax
import jax.numpy as jnp
from jax import lax
from jax.experimental import pallas as pl
from jax.experimental.pallas import tpu as pltpu
from jax.sharding import Mesh, PartitionSpec as P

AXES = ("y", "core", "x", "zh", "zl")
LANES = 128
VMEM = pl.BlockSpec(memory_space=pltpu.VMEM)
PARAMS = pltpu.CompilerParams(vmem_limit_bytes=40 * 1024 * 1024)


def split3(v):
    hi = v.astype(jnp.bfloat16).astype(jnp.float32)
    mid = (v - hi).astype(jnp.bfloat16).astype(jnp.float32)
    low = (v - hi - mid).astype(jnp.bfloat16).astype(jnp.float32)
    return hi, mid, low


def prepare(hidden_ref, key_ref, value_ref, ids_ref, gain_ref, out_ref):
    n_x, n_zl, _, _ = out_ref.shape
    toks, width = hidden_ref.shape
    n_union = ids_ref.shape[0]
    hidden = hidden_ref[...]
    hidden_f = hidden.astype(jnp.float32)
    squares = jnp.sum(hidden_f * hidden_f, axis=1, keepdims=True)
    hit = lax.broadcasted_iota(jnp.int32, (n_union, width), 1) == ids_ref[...]
    gains = jnp.sum(jnp.where(hit, gain_ref[...], 0.0), axis=1, keepdims=True)
    picked = lax.dot_general(
        jnp.where(hit, 1.0, 0.0).astype(jnp.bfloat16),
        hidden,
        (((1,), (1,)), ((), ())),
        preferred_element_type=jnp.float32,
    ).astype(jnp.bfloat16)
    lane = lax.broadcasted_iota(jnp.int32, (toks, LANES), 1)
    table = jnp.zeros((toks, LANES), jnp.float32)
    for place, part in enumerate(split3(squares) + split3(gains)):
        table = jnp.where(lane == place, part, table)
    extra = table.T[:16].astype(jnp.bfloat16)
    per = n_union // n_zl
    for x in range(n_x):
        source = key_ref if x < n_x // 2 else value_ref
        at = LANES * (x % (n_x // 2))
        block = source[:, at : at + LANES]
        for z in range(n_zl):
            out_ref[x, z, :toks] = block
            out_ref[x, z, toks : toks + per] = picked[per * z : per * (z + 1)]
            out_ref[x, z, toks + per :] = extra


def scale(features, in_ref, zl_ref, out_ref, union_ref, gain_ref):
    n_x, n_zl, rows, _ = in_ref.shape
    toks = LANES
    per = rows - toks - 16
    copies = out_ref.shape[0]
    zl = zl_ref[0]
    total = jnp.zeros((per, n_zl * LANES), jnp.float32)
    for x in range(n_x):
        extra = in_ref[x, 0, toks + per :].astype(jnp.float32)
        picked = in_ref[x, 0, toks : toks + per].astype(jnp.float32)
        for z in range(1, n_zl):
            extra = extra + in_ref[x, z, toks + per :].astype(jnp.float32)
            picked = picked + in_ref[x, z, toks : toks + per].astype(jnp.float32)
        if x == 0:
            gain = extra[3:4] + extra[4:5] + extra[5:6]
            gain_ref[...] = jnp.broadcast_to(gain, (LANES, LANES)).T
        squares = extra[0:1] + extra[1:2] + extra[2:3]
        inverse = lax.rsqrt(squares / features + 1e-05)
        column = jnp.broadcast_to(inverse, (LANES, LANES)).T
        gain_rows = gain_ref[pl.ds(pl.multiple_of(zl * per, 8), per), :]
        normed = (picked * inverse * gain_rows).astype(jnp.bfloat16)
        raw = jnp.concatenate([in_ref[x, z, :toks] for z in range(n_zl)], axis=1)
        total = total + jnp.dot(normed, raw, preferred_element_type=jnp.float32)
        for z in range(n_zl):
            scaled = (in_ref[x, z, :toks].astype(jnp.float32) * column).astype(jnp.bfloat16)
            for y in range(copies):
                out_ref[y, x, :, z * LANES : (z + 1) * LANES] = scaled
    for z in range(n_zl):
        union_ref[:, z, :] = total[:, z * LANES : (z + 1) * LANES]


def multiply(a_ref, b_ref, out_ref):
    rows = a_ref.shape[3]
    depth = a_ref.shape[1] * a_ref.shape[2]
    part = lax.dot_general(
        a_ref[0].reshape(depth, rows),
        b_ref[:, 0].reshape(depth, b_ref.shape[3]),
        (((0,), (0,)), ((), ())),
        preferred_element_type=jnp.float32,
    ).reshape(out_ref.shape)

    @pl.when(pl.program_id(0) == 0)
    def _():
        out_ref[...] = part

    @pl.when(pl.program_id(0) > 0)
    def _():
        out_ref[...] += part


def exchange(v, axes):
    return lax.all_to_all(v, axes, split_axis=0, concat_axis=0, tiled=True)


def gather(v, axes):
    count = lax.axis_size(axes)
    return exchange(jnp.broadcast_to(v[None], (count,) + v.shape), axes)


def per_device(hidden_in, norm_gain, key_cotangent, value_cotangent, union_ids):
    toks, width = hidden_in.shape
    n_y, n_core, n_x, n_zh, n_zl = (lax.axis_size(a) for a in AXES)
    y, core, x, zh, zl = (lax.axis_index(a) for a in AXES)
    n_union = union_ids.shape[0]
    heads = 2 * key_cotangent.shape[1]
    tile = width // n_y
    cols = n_zl * LANES
    per = n_union // n_zl

    a_sent = jnp.swapaxes(hidden_in.reshape(toks, n_y, tile), 0, 1)
    a_rows = exchange(a_sent, "y")

    local_ids = (union_ids - zl * width).reshape(n_union, 1)
    packed = pl.pallas_call(
        prepare,
        out_shape=jax.ShapeDtypeStruct((n_x, n_zl, toks + per + 16, LANES), jnp.bfloat16),
        in_specs=[VMEM] * 5,
        out_specs=VMEM,
        compiler_params=PARAMS,
    )(hidden_in, key_cotangent, value_cotangent, local_ids, norm_gain.reshape(1, width))
    packed = exchange(packed.reshape((n_x * n_zl,) + packed.shape[2:]), ("x", "zl"))
    packed = packed.reshape((n_x, n_zl) + packed.shape[1:])

    b_sent, union_part = pl.pallas_call(
        lambda *refs: scale(float(width * n_zl), *refs),
        out_shape=(
            jax.ShapeDtypeStruct((n_y, n_x, toks, cols), jnp.bfloat16),
            jax.ShapeDtypeStruct((per, n_zl, LANES), jnp.float32),
        ),
        in_specs=[VMEM, pl.BlockSpec(memory_space=pltpu.SMEM)],
        out_specs=(VMEM, VMEM),
        scratch_shapes=[pltpu.VMEM((LANES, LANES), jnp.float32)],
        compiler_params=PARAMS,
    )(packed, zl.astype(jnp.int32).reshape(1))

    a_all = gather(a_rows, "x")
    b_all = exchange(b_sent, "y")

    union_sum = jnp.sum(exchange(union_part, ("y", "core", "zh")), axis=0).astype(jnp.bfloat16)
    union_line = gather(union_sum, ("zh", "zl"))
    union_all = gather(union_line, ("y", "core", "x"))
    union_all = union_all.reshape(n_y * n_core, 2, n_x // 2, n_zh, n_zl, n_zl, LANES)
    union_all = jnp.transpose(union_all, (1, 4, 0, 3, 5, 2, 6)).astype(jnp.float32)
    union_all = union_all.reshape(2, n_union, heads * n_zl // 2)

    product = pl.pallas_call(
        multiply,
        grid=(n_x,),
        out_shape=jax.ShapeDtypeStruct((n_core, tile // n_core, cols), jnp.float32),
        in_specs=[
            pl.BlockSpec((1, n_y, toks, tile), lambda i: (i, 0, 0, 0)),
            pl.BlockSpec((n_y, 1, toks, cols), lambda i: (0, i, 0, 0)),
        ],
        out_specs=pl.BlockSpec((n_core, tile // n_core, cols), lambda i: (0, 0, 0)),
        compiler_params=PARAMS,
    )(a_all, b_all)
    product = jnp.sum(exchange(product, "core"), axis=0).astype(jnp.bfloat16)
    own = tile // (n_core * n_x * n_zh)
    pieces = exchange(product.reshape(n_x * n_zh, own, cols), ("x", "zh"))
    summed = jnp.sum(pieces.reshape(n_x, n_zh, own, cols).astype(jnp.float32), axis=1)
    first = own * (((y * n_core + core) * n_x + x) * n_zh + zh)
    gain = lax.dynamic_slice(norm_gain, (first,), (own,))
    row_ids = zl * width + first + lax.iota(jnp.int32, own)
    outlier = jnp.any(row_ids[:, None] == union_ids[None, :], axis=1)
    summed = jnp.where(outlier[None, :, None], 0.0, summed * gain[None, :, None])
    summed = summed.reshape(2, n_x // 2, own, n_zl, LANES)
    grads = jnp.transpose(summed, (0, 2, 3, 1, 4)).reshape(2, 1, own, heads * n_zl // 2)
    return (grads[0], grads[1], union_all[0], union_all[1])


def solution(mesh):
    sizes = dict(mesh.shape)
    split = Mesh(
        mesh.devices.reshape(sizes["group"] // 2, 2, 4, sizes["loop"] // 4, sizes["mp"]), AXES
    )
    rows = ("y", "core", "x", "zh")
    return jax.shard_map(
        per_device,
        mesh=split,
        in_specs=(P(rows, "zl"), P("zl"), P(rows, "zl"), P(rows, "zl"), P()),
        out_specs=(P("zl", rows, None), P("zl", rows, None), P(), P()),
        check_vma=False,
    )
```

time: 882 us -> 207 us (0.23)
  waiting for transfers between devices: 724 us -> 99.9 us
  local copies, waits for them, and re-layouts: 68.3 us -> 13.7 us
  blocking collectives: 25.2 us -> 52.1 us
  other arithmetic: 15.8 us -> 1.98 us
  between operations: 14.1 us -> 0.82 us
  matrix products: 9.18 us -> 0 us
    psum x1 -> x0, waiting for transfers between devices: 724 us -> none  [per_device(): union_sum = lax.psum(union_part, ('group', 'loop', 'mp'))]
    all_to_all x1 -> x6, waiting for transfers between devices: 0.01 us -> 99.9 us  [exchange(): return lax.all_to_all(v, axes, split_axis=0, concat_axis=0, tiled=True)]
    all_to_all x0 -> x3, blocking collectives: none -> 52.1 us  [exchange(): return lax.all_to_all(v, axes, split_axis=0, concat_axis=0, tiled=True)]
    reshape x2, local copies, waits for them, and re-layouts: 32 us -> 0.96 us  [the longest x1 0.84 us: per_device(): a_sent = jnp.swapaxes(hidden_in.reshape(toks, n_y, tile), 0, 1)]
    dot_general x1 -> x0, local copies, waits for them, and re-layouts: 24.1 us -> none  [per_device(): jnp.einsum('tr,ktn->rkn', normed, lax.all_gather(stacked, 'mp', axis=2, t...]
    all_gather x1 -> x0, blocking collectives: 16.3 us -> none  [per_device(): lax.all_gather(stacked, 'mp', axis=2, tiled=True)]
    dot_general x1 -> x0, matrix products: 9.18 us -> none  [per_device(): jnp.einsum('tr,ktn->rkn', normed, lax.all_gather(stacked, 'mp', axis=2, t...]
    psum x1 -> x0, blocking collectives: 8.89 us -> none  [per_device(): total_squares = lax.psum(local_squares, 'mp')]
  transfers between devices with their start and end apart: 2 -> 6, of which waited for: 1 -> 6; matrix products, arithmetic and copies ran while one was open for 3% -> 3% of each run, Pallas kernels for 0% -> 0%
where the time goes in v1:
time: 207 us; the launch traced here: 203 us
  waiting for transfers between devices  99.9 us (48%)
  blocking collectives  52.1 us (25%)
  starting transfers between devices  28.7 us (14%)
  local copies, waits for them, and re-layouts  13.7 us (7%)
  Pallas kernels  5.63 us (3%)
    all_to_all x6, waiting for transfers between devices, exchange(): return lax.all_to_all(v, axes, split_axis=0, concat_axis=0, tiled=True)  99.9 us
    all_to_all x3, blocking collectives, exchange(): return lax.all_to_all(v, axes, split_axis=0, concat_axis=0, tiled=True)  52.1 us
    all_to_all x6, starting transfers between devices, exchange(): return lax.all_to_all(v, axes, split_axis=0, concat_axis=0, tiled=True)  28.7 us
    unnamed x16, local copies, waits for them, and re-layouts  6.03 us
  transfers between devices with their start and end apart: 6, of which 6 were waited for; matrix products, arithmetic and copies ran while one was open for 3% of the time, Pallas kernels for 0%

profile of v1, /device:TPU:1, one launch (start us, length us, event | category | flops | bytes accessed | tf_op | source)
XLA Modules:
  0.0 202.9 jit_solution(6202910686342025197)
XLA Ops:
  0.6 0.7 subtract_bitcast_fusion
  1.4 1.0 copy-done.1
  2.5 0.8 copy-done.3
  3.3 0.8 copy-done.4
  4.1 0.7 copy-done.5
  4.8 1.4 shard_map.84
  6.2 9.0 %all-to-all-start.2 = ((bf16[16,176,128]{2,1,0:T(8,128)(2,1)}), bf16[16,176,128]{2,1,0:T(8,128)(2,1)S(1)}, u32[]{:S(2)}, u32[]{:S(2)}) async-start(bf16[16,176,128]{2,1,0:T(8,128)(2,1)} %bitcast.3), calls=%async_computation.2 | async-start | bytes 1441792 | tf_op jit(solution)/shard_map/all_to_all | solution.py:103
  15.3 0.8 copy.41
  16.1 19.1 %all-to-all-done.2 = bf16[16,176,128]{2,1,0:T(8,128)(2,1)S(1)} async-done(((bf16[16,176,128]{2,1,0:T(8,128)(2,1)}), bf16[16,176,128]{2,1,0:T(8,128)(2,1)S(1)}, u32[]{:S(2)}, u32[]{:S(2)}) %all-to-all-start.2) | async-done | bytes 720928 | tf_op jit(solution)/shard_map/all_to_all | solution.py:103
  35.2 4.2 %all-to-all-start = ((bf16[4,128,512]{2,1,0:T(8,128)(2,1)}), bf16[4,128,512]{2,1,0:T(8,128)(2,1)S(1)}, u32[]{:S(2)}, u32[]{:S(2)}) async-start(bf16[4,128,512]{2,1,0:T(8,128)(2,1)} %bitcast.26), calls=%async_computation | async-start | bytes 1048576 | tf_op jit(solution)/shard_map/all_to_all | solution.py:103
  39.8 1.3 copy-done
  41.1 5.4 %all-to-all-done = bf16[4,128,512]{2,1,0:T(8,128)(2,1)S(1)} async-done(((bf16[4,128,512]{2,1,0:T(8,128)(2,1)}), bf16[4,128,512]{2,1,0:T(8,128)(2,1)S(1)}, u32[]{:S(2)}, u32[]{:S(2)}) %all-to-all-start) | async-done | bytes 524320 | tf_op jit(solution)/shard_map/all_to_all | solution.py:103
  46.5 30.7 %all_to_all.45 = f32[32,4,128]{2,1,0:T(4,128)S(1)} all-to-all(f32[32,4,128]{2,1,0:T(4,128)S(1)} %get-tuple-element.7), channel_id=1, replica_groups=mesh['y'=4,'core'=2,'x'=4,'zh'=4,'zl'=4] {'y','core','zh'}, dimensions={0} | all-to-all | bytes 131072 | tf_op jit(solution)/shard_map/all_to_all | solution.py:103
  77.3 1.5 broadcast_in_dim.16
  78.8 3.6 %all-to-all-start.1 = ((bf16[4,4,128,512]{3,2,1,0:T(8,128)(2,1)}), bf16[4,4,128,512]{3,2,1,0:T(8,128)(2,1)S(1)}, u32[]{:S(2)}, u32[]{:S(2)}) async-start(bf16[4,4,128,512]{3,2,1,0:T(8,128)(2,1)} %broadcast_in_dim.16), calls=%async_computation.1 | async-start | bytes 4194304 | tf_op jit(solution)/shard_map/all_to_all | solution.py:103
  82.5 26.0 %all-to-all-done.1.a_ref = bf16[4,4,128,512]{3,2,1,0:T(8,128)(2,1)S(1)} async-done(((bf16[4,4,128,512]{3,2,1,0:T(8,128)(2,1)}), bf16[4,4,128,512]{3,2,1,0:T(8,128)(2,1)S(1)}, u32[]{:S(2)}, u32[]{:S(2)}) %all-to-all-start.1) | async-done | bytes 2097184 | tf_op jit(solution)/shard_map/all_to_all | solution.py:103
  108.4 14.1 %all_to_all.46 = bf16[16,4,128]{2,1,0:T(4,128)(2,1)S(1)} all-to-all(bf16[16,4,128]{2,1,0:T(4,128)(2,1)S(1)} %broadcast_in_dim.17), channel_id=1, replica_groups=mesh['y'=4,'core'=2,'x'=4,'zh'=4,'zl'=4] {'zh','zl'}, dimensions={0} | all-to-all | bytes 32768 | tf_op jit(solution)/shard_map/all_to_all | solution.py:103
  122.6 4.5 %all-to-all-start.3 = ((bf16[4,4,128,512]{3,2,1,0:T(8,128)(2,1)}), bf16[4,4,128,512]{3,2,1,0:T(8,128)(2,1)}, u32[]{:S(2)}, u32[]{:S(2)}) async-start(bf16[4,4,128,512]{3,2,1,0:T(8,128)(2,1)} %copy-done), calls=%async_computation.3 | async-start | bytes 4194304 | tf_op jit(solution)/shard_map/all_to_all | solution.py:103
  127.0 24.3 %all-to-all-done.3.b_ref = bf16[4,4,128,512]{3,2,1,0:T(8,128)(2,1)} async-done(((bf16[4,4,128,512]{3,2,1,0:T(8,128)(2,1)}), bf16[4,4,128,512]{3,2,1,0:T(8,128)(2,1)}, u32[]{:S(2)}, u32[]{:S(2)}) %all-to-all-start.3) | async-done | bytes 2097184 | tf_op jit(solution)/shard_map/all_to_all | solution.py:103
  151.3 3.8 %shard_map.86 = f32[2,256,512]{2,1,0:T(8,128)S(1)} custom-call(bf16[4,4,128,512]{3,2,1,0:T(8,128)(2,1)S(1)} %all-to-all-done.1.a_ref, bf16[4,4,128,512]{3,2,1,0:T(8,128)(2,1)} %all-to-all-done.3.b_ref), custom_call_target="tpu_custom_call" | custom-call | tf_op jit(solution)/shard_map/pallas_call | solution.py:157
  155.1 7.3 %all_to_all.47 = f32[2,256,512]{2,1,0:T(8,128)S(1)} all-to-all(f32[2,256,512]{2,1,0:T(8,128)S(1)} %shard_map.86), channel_id=1, replica_groups=mesh['y'=4,'core'=2,'x'=4,'zh'=4,'zl'=4] {'core'}, dimensions={0} | all-to-all | bytes 2097152 | tf_op jit(solution)/shard_map/all_to_all | solution.py:103
  162.4 0.9 broadcast_in_dim.18
  163.3 3.9 %all-to-all-start.8 = ((bf16[32,16,4,128]{3,1,2,0:T(8,128)(2,1)}), bf16[32,16,4,128]{3,1,2,0:T(8,128)(2,1)S(1)}, u32[]{:S(2)}, u32[]{:S(2)}) async-start(bf16[32,16,4,128]{3,1,2,0:T(8,128)(2,1)} %broadcast_in_dim.18), calls=%async_computation.8 | async-start | bytes 1048576 | tf_op jit(solution)/shard_map/all_to_all | solution.py:103
  167.2 0.8 reduce_sum.29
  168.1 10.6 %all-to-all-done.8 = bf16[32,16,4,128]{3,1,2,0:T(8,128)(2,1)S(1)} async-done(((bf16[32,16,4,128]{3,1,2,0:T(8,128)(2,1)}), bf16[32,16,4,128]{3,1,2,0:T(8,128)(2,1)S(1)}, u32[]{:S(2)}, u32[]{:S(2)}) %all-to-all-start.8) | async-done | bytes 524320 | tf_op jit(solution)/shard_map/all_to_all | solution.py:103
  178.7 3.5 %all-to-all-start.5 = ((bf16[16,16,512]{2,1,0:T(8,128)(2,1)}), bf16[16,16,512]{2,1,0:T(8,128)(2,1)S(1)}, u32[]{:S(2)}, u32[]{:S(2)}) async-start(bf16[16,16,512]{2,1,0:T(8,128)(2,1)} %bitcast.6), calls=%async_computation.5 | async-start | bytes 524288 | tf_op jit(solution)/shard_map/all_to_all | solution.py:103
  182.3 0.8 dynamic_slice.3
  183.9 1.2 squeeze.14
  185.5 1.2 squeeze.15
  186.7 14.6 %all-to-all-done.5 = bf16[16,16,512]{2,1,0:T(8,128)(2,1)S(1)} async-done(((bf16[16,16,512]{2,1,0:T(8,128)(2,1)}), bf16[16,16,512]{2,1,0:T(8,128)(2,1)S(1)}, u32[]{:S(2)}, u32[]{:S(2)}) %all-to-all-start.5) | async-done | bytes 262176 | tf_op jit(solution)/shard_map/all_to_all | solution.py:103
  201.6 0.6 copy.37
  202.3 0.6 copy.38
  (26 shorter events, 2.1 us)
Async XLA Ops:
  1.4 1.0 copy-start.1
  2.5 0.8 copy-start.3
  3.3 0.8 copy-start.4
  4.1 0.7 copy-start.5
  4.8 10.4 %copy-start.2 = (bf16[128,2048]{1,0:T(8,128)(2,1)S(1)}, bf16[128,2048]{1,0:T(8,128)(2,1)}, u32[]{:S(2)}) copy-start(bf16[128,2048]{1,0:T(8,128)(2,1)} %hidden_ref.1) | copy-start | bytes 1572868
  6.2 28.9 %all-to-all-start.2 = ((bf16[16,176,128]{2,1,0:T(8,128)(2,1)}), bf16[16,176,128]{2,1,0:T(8,128)(2,1)S(1)}, u32[]{:S(2)}, u32[]{:S(2)}) async-start(bf16[16,176,128]{2,1,0:T(8,128)(2,1)} %bitcast.3), calls=%async_computation.2 | async-start | bytes 1441792 | tf_op jit(solution)/shard_map/all_to_all | solution.py:103
  35.2 11.4 %all-to-all-start = ((bf16[4,128,512]{2,1,0:T(8,128)(2,1)}), bf16[4,128,512]{2,1,0:T(8,128)(2,1)S(1)}, u32[]{:S(2)}, u32[]{:S(2)}) async-start(bf16[4,128,512]{2,1,0:T(8,128)(2,1)} %bitcast.26), calls=%async_computation | async-start | bytes 1048576 | tf_op jit(solution)/shard_map/all_to_all | solution.py:103
  39.8 1.3 copy-start
  78.8 29.6 %all-to-all-start.1 = ((bf16[4,4,128,512]{3,2,1,0:T(8,128)(2,1)}), bf16[4,4,128,512]{3,2,1,0:T(8,128)(2,1)S(1)}, u32[]{:S(2)}, u32[]{:S(2)}) async-start(bf16[4,4,128,512]{3,2,1,0:T(8,128)(2,1)} %broadcast_in_dim.16), calls=%async_computation.1 | async-start | bytes 4194304 | tf_op jit(solution)/shard_map/all_to_all | solution.py:103
  122.6 28.7 %all-to-all-start.3 = ((bf16[4,4,128,512]{3,2,1,0:T(8,128)(2,1)}), bf16[4,4,128,512]{3,2,1,0:T(8,128)(2,1)}, u32[]{:S(2)}, u32[]{:S(2)}) async-start(bf16[4,4,128,512]{3,2,1,0:T(8,128)(2,1)} %copy-done), calls=%async_computation.3 | async-start | bytes 4194304 | tf_op jit(solution)/shard_map/all_to_all | solution.py:103
  162.4 20.7 %copy-start.6 = (s32[128]{0:T(128)S(1)}, s32[128]{0:T(128)}, u32[]{:S(2)}) copy-start(s32[128]{0:T(128)} %param.9) | copy-start | bytes 1540
  163.3 15.4 %all-to-all-start.8 = ((bf16[32,16,4,128]{3,1,2,0:T(8,128)(2,1)}), bf16[32,16,4,128]{3,1,2,0:T(8,128)(2,1)S(1)}, u32[]{:S(2)}, u32[]{:S(2)}) async-start(bf16[32,16,4,128]{3,1,2,0:T(8,128)(2,1)} %broadcast_in_dim.18), calls=%async_computation.8 | async-start | bytes 1048576 | tf_op jit(solution)/shard_map/all_to_all | solution.py:103
  178.7 22.6 %all-to-all-start.5 = ((bf16[16,16,512]{2,1,0:T(8,128)(2,1)}), bf16[16,16,512]{2,1,0:T(8,128)(2,1)S(1)}, u32[]{:S(2)}, u32[]{:S(2)}) async-start(bf16[16,16,512]{2,1,0:T(8,128)(2,1)} %bitcast.6), calls=%async_computation.5 | async-start | bytes 524288 | tf_op jit(solution)/shard_map/all_to_all | solution.py:103

commit v2 on v0

v2 whole, which is shorter than its diff:
```python
import jax
import jax.numpy as jnp
from jax import lax
from jax.experimental import pallas as pl
from jax.experimental.pallas import tpu as pltpu
from jax.sharding import Mesh, PartitionSpec as P

AXES = ("y", "core", "x", "zh", "zl")
LANES = 128
AUX = 16
VMEM = pl.BlockSpec(memory_space=pltpu.VMEM)
SMEM = pl.BlockSpec(memory_space=pltpu.SMEM)
PARAMS = pltpu.CompilerParams(vmem_limit_bytes=40 * 1024 * 1024)


def split3(v):
    hi = v.astype(jnp.bfloat16).astype(jnp.float32)
    mid = (v - hi).astype(jnp.bfloat16).astype(jnp.float32)
    low = (v - hi - mid).astype(jnp.bfloat16).astype(jnp.float32)
    return hi, mid, low


def column(row):
    return jnp.broadcast_to(row, (LANES, LANES)).T


def spread_cotangents(key_ref, value_ref, out_ref):
    n_x, n_zl, _, _ = out_ref.shape
    for x in range(n_x):
        source = key_ref if x < n_x // 2 else value_ref
        at = LANES * (x % (n_x // 2))
        for z in range(n_zl):
            out_ref[x, z] = source[:, at : at + LANES]


def prepare(y_ref, zl_ref, hidden_ref, ids_ref, gain_ref, *refs):
    outs, picked_ref = refs[:-1], refs[-1]
    n_y = len(outs)
    toks, width = hidden_ref.shape
    tile = width // n_y
    n_union = ids_ref.shape[1]
    per = n_union // n_y
    hidden = hidden_ref[...]
    hidden_f = hidden.astype(jnp.float32)
    squares = jnp.sum(hidden_f * hidden_f, axis=1, keepdims=True)
    ids = column(ids_ref[...].astype(jnp.float32))[:, :1].astype(jnp.int32) - zl_ref[0] * width
    hit = lax.broadcasted_iota(jnp.int32, (n_union, width), 1) == ids
    gains = jnp.sum(jnp.where(hit, gain_ref[...], 0.0), axis=1, keepdims=True)
    picked_ref[...] = lax.dot_general(
        jnp.where(hit, 1.0, 0.0).astype(jnp.bfloat16),
        hidden,
        (((1,), (1,)), ((), ())),
        preferred_element_type=jnp.float32,
    ).astype(jnp.bfloat16)
    lane = lax.broadcasted_iota(jnp.int32, (toks, LANES), 1)
    table = jnp.zeros((toks, LANES), jnp.float32)
    for place, part in enumerate(split3(squares) + split3(gains)):
        table = jnp.where(lane == place, part, table)
    extra = table.T[:AUX].astype(jnp.bfloat16)
    for k, out_ref in enumerate(outs):
        to = lax.rem(y_ref[0] + k, n_y)
        out_ref[:toks] = hidden_ref[:, pl.ds(pl.multiple_of(to * tile, tile), tile)]
        for half in range(2):
            rows = pl.ds(pl.multiple_of(to * per + half * AUX, AUX), AUX)
            out_ref[toks:, half * LANES : (half + 1) * LANES] = picked_ref[rows, :]
        out_ref[toks:, 2 * LANES : 3 * LANES] = extra
        out_ref[toks:, 3 * LANES :] = jnp.zeros((AUX, tile - 3 * LANES), jnp.bfloat16)


def complete(features, n_y, *refs):
    blocks, parts, out_ref = refs[:n_y], refs[n_y:-1], refs[-1]
    toks = blocks[0].shape[0] - AUX
    for k in range(n_y):
        out_ref[k, :toks] = blocks[k][:toks]
        rows = parts[0][k].astype(jnp.float32)
        for part in parts[1:]:
            rows = rows + part[k].astype(jnp.float32)
        extra = rows[:, 2 * LANES : 3 * LANES]
        squares = extra[0:1] + extra[1:2] + extra[2:3]
        scales = split3(lax.rsqrt(squares / features + 1e-05))
        place = lax.broadcasted_iota(jnp.int32, (AUX, LANES), 0)
        for i, part in enumerate(scales):
            extra = jnp.where(place == i, part, extra)
        out_ref[k, toks:, : 2 * LANES] = rows[:, : 2 * LANES].astype(jnp.bfloat16)
        out_ref[k, toks:, 2 * LANES : 3 * LANES] = extra.astype(jnp.bfloat16)
        out_ref[k, toks:, 3 * LANES :] = rows[:, 3 * LANES :].astype(jnp.bfloat16)


def multiply(y_ref, x_ref, core_ref, gain_ref, b_ref, *refs):
    own_ref, other_ref, bulk_ref, union_ref, gains_ref = refs[-5:]
    blocks = refs[:-5]
    n_y, n_x, toks, cols = b_ref.shape
    tile = bulk_ref.shape[0]
    per = union_ref.shape[0]
    y, x = y_ref[0], x_ref[0]
    gain = gain_ref[:, pl.ds(pl.multiple_of(y * tile, tile), tile)]
    extra = blocks[0][0, toks:, 2 * LANES : 3 * LANES].astype(jnp.float32)
    gains_ref[...] = column(extra[3:4] + extra[4:5] + extra[5:6])
    union_gain = gains_ref[pl.ds(pl.multiple_of(y * per, per), per), :]
    for j, block in enumerate(blocks):
        from_x = lax.rem(x + n_x - j, n_x)
        normed, picked, right = [], [], []
        for k in range(n_y):
            from_y = lax.rem(y + n_y - k, n_y)
            right.append(b_ref[from_y, from_x])
            extra = block[k, toks:, 2 * LANES : 3 * LANES].astype(jnp.float32)
            scale = extra[0:1] + extra[1:2] + extra[2:3]
            scales = column(scale)
            scales = jnp.concatenate([scales] * (tile // LANES), axis=1)
            normed.append((block[k, :toks].astype(jnp.float32) * scales * gain).astype(jnp.bfloat16))
            raw = block[k, toks:].astype(jnp.float32)
            raw = jnp.concatenate([raw[:, :LANES], raw[:, LANES : 2 * LANES]], axis=0)
            picked.append((raw * scale * union_gain).astype(jnp.bfloat16))
        right = jnp.concatenate(right, axis=0)
        bulk = lax.dot_general(
            jnp.concatenate(normed, axis=0),
            right,
            (((0,), (0,)), ((), ())),
            preferred_element_type=jnp.float32,
        )
        union = jnp.dot(jnp.concatenate(picked, axis=1), right, preferred_element_type=jnp.float32)
        if j == 0:
            bulk_ref[...] = bulk
            union_ref[...] = union
        else:
            bulk_ref[...] += bulk
            union_ref[...] += union
    rows, outliers = tile // 2, per // 2
    for out_ref, core in ((own_ref, core_ref[0]), (other_ref, 1 - core_ref[0])):
        out_ref[:rows] = bulk_ref[pl.ds(pl.multiple_of(core * rows, rows), rows), :]
        out_ref[rows:] = union_ref[pl.ds(pl.multiple_of(core * outliers, outliers), outliers), :]


def add_cores(own_ref, got_ref, out_ref):
    n_x, n_zh, rows, _ = out_ref.shape
    bulk = n_x * n_zh * rows
    cols = own_ref.shape[1]
    outliers = (own_ref[bulk:] + got_ref[bulk:]).astype(jnp.bfloat16)
    wide = cols // n_x
    for x in range(n_x):
        for z in range(n_zh):
            at = rows * (x * n_zh + z)
            out_ref[x, z, :, :cols] = (own_ref[at : at + rows] + got_ref[at : at + rows]).astype(jnp.bfloat16)
            out_ref[x, z, :, cols:] = outliers[:, x * wide : (x + 1) * wide]


def finish(first_ref, ids_ref, in_ref, key_ref, value_ref, union_ref):
    n_x, n_zh, rows, _ = in_ref.shape
    n_zl = key_ref.shape[2] // (2 * LANES)
    cols = n_zl * LANES
    row = lax.broadcasted_iota(jnp.int32, (rows, LANES), 0) + first_ref[0]
    hits = jnp.sum(jnp.where(row == ids_ref[...], 1.0, 0.0), axis=1, keepdims=True)
    for x in range(n_x):
        total = in_ref[x, 0].astype(jnp.float32)
        for z in range(1, n_zh):
            total = total + in_ref[x, z].astype(jnp.float32)
        kind, half = x // 2, x % 2
        out_ref = value_ref if kind else key_ref
        for z in range(n_zl):
            at = LANES * (2 * z + half)
            out_ref[0, :, at : at + LANES] = jnp.where(hits > 0.0, 0.0, total[:, z * LANES : (z + 1) * LANES])
        outliers = total[:, cols:].astype(jnp.bfloat16)
        for i in range(union_ref.shape[0]):
            union_ref[i, kind, :, half * LANES : (half + 1) * LANES] = outliers


def lay_out(in_ref, key_ref, value_ref):
    count, _, rows, cols = in_ref.shape
    n_x = key_ref.shape[1] // cols
    for i in range(count):
        at, to = rows * (i // n_x), cols * (i % n_x)
        key_ref[at : at + rows, to : to + cols] = in_ref[i, 0].astype(jnp.float32)
        value_ref[at : at + rows, to : to + cols] = in_ref[i, 1].astype(jnp.float32)


def call(body, out_shape, args, scalars=0, scratch=()):
    single = not isinstance(out_shape, tuple)
    return pl.pallas_call(
        body,
        out_shape=out_shape,
        in_specs=[SMEM] * scalars + [VMEM] * (len(args) - scalars),
        out_specs=VMEM if single else tuple(VMEM for _ in out_shape),
        scratch_shapes=scratch,
        compiler_params=PARAMS,
    )(*args)


def exchange(v, axes):
    return lax.all_to_all(v, axes, split_axis=0, concat_axis=0, tiled=True)


def shift(v, axis, by):
    count = lax.axis_size(axis)
    return lax.ppermute(v, axis, [(i, (i + by) % count) for i in range(count)])


def per_device(hidden_in, norm_gain, key_cotangent, value_cotangent, union_ids):
    bf16, f32 = jnp.bfloat16, jnp.float32
    toks, width = hidden_in.shape
    n_y, n_core, n_x, n_zh, n_zl = (lax.axis_size(a) for a in AXES)
    y, core, x, zh, zl = (lax.axis_index(a).astype(jnp.int32) for a in AXES)
    n_union = union_ids.shape[0]
    heads = key_cotangent.shape[1] * n_zl
    tile = width // n_y
    cols = n_zl * LANES
    per = n_union // n_y
    shape = jax.ShapeDtypeStruct
    ids = union_ids.reshape(1, n_union)
    gain = norm_gain.reshape(1, width)
    at_y, at_x, at_core, at_zl = (v.reshape(1) for v in (y, x, core, zl))

    spread = call(spread_cotangents, shape((n_x, n_zl, toks, LANES), bf16), (key_cotangent, value_cotangent))
    b_some = exchange(spread.reshape(n_x * n_zl, toks, LANES), ("x", "zl"))
    b_some = jnp.swapaxes(b_some.reshape(n_x, n_zl, toks, LANES), 1, 2).reshape(n_x, toks, cols)
    b_all = exchange(jnp.broadcast_to(b_some[None], (n_y,) + b_some.shape), "y")

    sent = call(
        prepare,
        tuple(shape((toks + AUX, tile), bf16) for _ in range(n_y)),
        (at_y, at_zl, hidden_in, ids, gain),
        2,
        [pltpu.VMEM((n_union, toks), bf16)],
    )
    blocks = [sent[0]] + [shift(sent[k], "y", k) for k in range(1, n_y)]
    aux = jnp.stack([block[toks:] for block in blocks])
    parts = [aux] + [shift(aux, "zl", k) for k in range(1, n_zl)]
    a_own = call(
        lambda *refs: complete(float(width * n_zl), n_y, *refs),
        shape((n_y, toks + AUX, tile), bf16),
        (*blocks, *parts),
    )
    a_all = [a_own] + [shift(a_own, "x", k) for k in range(1, n_x)]

    half = shape(((tile + per) // n_core, cols), f32)
    own, other = call(
        multiply,
        (half, half),
        (at_y, at_x, at_core, gain, b_all, *a_all),
        3,
        [pltpu.VMEM((tile, cols), f32), pltpu.VMEM((per, cols), f32), pltpu.VMEM((LANES, LANES), f32)],
    )
    got = shift(other, "core", 1)
    rows = tile // (n_core * n_x * n_zh)
    pieces = call(add_cores, shape((n_x, n_zh, rows, cols + cols // n_x), bf16), (own, got))
    pieces = exchange(pieces.reshape((n_x * n_zh,) + pieces.shape[2:]), ("x", "zh"))
    first = zl * width + rows * (((y * n_core + core) * n_x + x) * n_zh + zh)
    grad = shape((1, rows, heads), f32)
    grad_key, grad_value, outliers = call(
        finish,
        (grad, grad, shape((n_y * n_core * n_x, 2, per // n_core, 2 * LANES), bf16)),
        (first.reshape(1), ids, pieces.reshape((n_x, n_zh) + pieces.shape[1:])),
        1,
    )
    outliers = exchange(outliers, ("y", "core", "x"))
    union = shape((n_union, heads), f32)
    union_key, union_value = call(lay_out, (union, union), (outliers,))
    return (grad_key, grad_value, union_key, union_value)


def solution(mesh):
    sizes = dict(mesh.shape)
    split = Mesh(
        mesh.devices.reshape(sizes["group"] // 2, 2, 4, sizes["loop"] // 4, sizes["mp"]), AXES
    )
    rows = ("y", "core", "x", "zh")
    return jax.shard_map(
        per_device,
        mesh=split,
        in_specs=(P(rows, "zl"), P("zl"), P(rows, "zl"), P(rows, "zl"), P()),
        out_specs=(P("zl", rows, None), P("zl", rows, None), P(), P()),
        check_vma=False,
    )
```

time: 882 us -> 145 us (0.16)
  waiting for transfers between devices: 724 us -> 48 us
  local copies, waits for them, and re-layouts: 68.3 us -> 6.23 us
  starting transfers between devices: 24.7 us -> 60.5 us
  other arithmetic: 15.8 us -> 0.01 us
  between operations: 14.1 us -> 0.89 us
  matrix products: 9.18 us -> 0 us
    psum x1 -> x0, waiting for transfers between devices: 724 us -> none  [per_device(): union_sum = lax.psum(union_part, ('group', 'loop', 'mp'))]
    ppermute x0 -> x10, starting transfers between devices: none -> 32.9 us  [shift(): return lax.ppermute(v, axis, [(i, (i + by) % count) for i in range(count)])]
    reshape x2 -> x1, local copies, waits for them, and re-layouts: 32 us -> 0.41 us  [per_device(): b_some.reshape(n_x, n_zl, toks, LANES)]
    ppermute x0 -> x10, waiting for transfers between devices: none -> 26.7 us  [shift(): return lax.ppermute(v, axis, [(i, (i + by) % count) for i in range(count)])]
    dot_general x1 -> x0, local copies, waits for them, and re-layouts: 24.1 us -> none  [per_device(): jnp.einsum('tr,ktn->rkn', normed, lax.all_gather(stacked, 'mp', axis=2, t...]
    all_to_all x0 -> x1, blocking collectives: none -> 21.7 us  [exchange(): return lax.all_to_all(v, axes, split_axis=0, concat_axis=0, tiled=True)]
    all_to_all x1 -> x3, waiting for transfers between devices: 0.01 us -> 21.4 us  [exchange(): return lax.all_to_all(v, axes, split_axis=0, concat_axis=0, tiled=True)]
    all_gather x1 -> x0, blocking collectives: 16.3 us -> none  [per_device(): lax.all_gather(stacked, 'mp', axis=2, tiled=True)]
  transfers between devices with their start and end apart: 2 -> 13, of which waited for: 1 -> 7; matrix products, arithmetic and copies ran while one was open for 3% -> 2% of each run, Pallas kernels for 0% -> 0%
where the time goes in v2:
time: 145 us
  starting transfers between devices  60.5 us (42%)
  waiting for transfers between devices  48 us (33%)
  blocking collectives  21.7 us (15%)
  Pallas kernels  7.16 us (5%)
  local copies, waits for them, and re-layouts  6.23 us (4%)
    ppermute x10, starting transfers between devices, shift(): return lax.ppermute(v, axis, [(i, (i + by) % count) for i in range(count)])  32.9 us
    all_to_all x3, starting transfers between devices, exchange(): return lax.all_to_all(v, axes, split_axis=0, concat_axis=0, tiled=True)  27.6 us
    ppermute x10, waiting for transfers between devices, shift(): return lax.ppermute(v, axis, [(i, (i + by) % count) for i in range(count)])  26.7 us
    all_to_all x1, blocking collectives, exchange(): return lax.all_to_all(v, axes, split_axis=0, concat_axis=0, tiled=True)  21.7 us
    all_to_all x3, waiting for transfers between devices, exchange(): return lax.all_to_all(v, axes, split_axis=0, concat_axis=0, tiled=True)  21.4 us
    pallas_call x7, Pallas kernels, call(): pl.pallas_call(body, out_shape=out_shape, in_specs=[SMEM] * scalars + [VM...  7.16 us
    unnamed x14, local copies, waits for them, and re-layouts  4.07 us
  transfers between devices with their start and end apart: 13, of which 7 were waited for; matrix products, arithmetic and copies ran while one was open for 2% of the time, Pallas kernels for 0%

profile of v2, /device:TPU:1, one launch (start us, length us, event | category | flops | bytes accessed | tf_op | source)
XLA Modules:
  0.0 144.5 jit_solution(11956453590136989992)
XLA Ops:
  0.6 0.8 copy-done.1
  1.5 0.8 copy-done.2
  2.3 0.9 shard_map.84
  3.2 9.0 %all-to-all-start = ((bf16[16,128,128]{2,1,0:T(8,128)(2,1)}), bf16[16,128,128]{2,1,0:T(8,128)(2,1)S(1)}, u32[]{:S(2)}, u32[]{:S(2)}) async-start(bf16[16,128,128]{2,1,0:T(8,128)(2,1)} %bitcast.6), calls=%async_computation | async-start | bytes 1048576 | tf_op jit(solution)/shard_map/all_to_all | solution.py:189
  12.2 1.0 copy-done
  13.2 0.7 copy-done.3
  13.9 0.7 copy-done.5
  15.2 3.2 %collective-permute-start = (bf16[144,512]{1,0:T(8,128)(2,1)S(1)}, bf16[144,512]{1,0:T(8,128)(2,1)S(1)}, u32[]{:S(2)}, u32[]{:S(2)}) collective-permute-start(bf16[144,512]{1,0:T(8,128)(2,1)S(1)} %get-tuple-element.16), channel_id=1, source_target_pairs={{0,128},{128,256},{256,384},{384,0},{1,129},{129,257},{257,385},{3... | collective-permute-start | bytes 442376 | tf_op jit(solution)/shard_map/ppermute | solution.py:194
  18.4 4.5 %collective-permute-start.1 = (bf16[144,512]{1,0:T(8,128)(2,1)S(1)}, bf16[144,512]{1,0:T(8,128)(2,1)S(1)}, u32[]{:S(2)}, u32[]{:S(2)}) collective-permute-start(bf16[144,512]{1,0:T(8,128)(2,1)S(1)} %get-tuple-element.17), channel_id=1, source_target_pairs={{0,256},{128,384},{256,0},{384,128},{1,257},{129,385},{257,1},{385... | collective-permute-start | bytes 442376 | tf_op jit(solution)/shard_map/ppermute | solution.py:194
  22.9 3.0 %collective-permute-start.2 = (bf16[144,512]{1,0:T(8,128)(2,1)S(1)}, bf16[144,512]{1,0:T(8,128)(2,1)S(1)}, u32[]{:S(2)}, u32[]{:S(2)}) collective-permute-start(bf16[144,512]{1,0:T(8,128)(2,1)S(1)} %get-tuple-element.18), channel_id=1, source_target_pairs={{0,384},{128,0},{256,128},{384,256},{1,385},{129,1},{257,129},{385... | collective-permute-start | bytes 442376 | tf_op jit(solution)/shard_map/ppermute | solution.py:194
  25.9 2.0 %all-to-all-done = bf16[16,128,128]{2,1,0:T(8,128)(2,1)S(1)} async-done(((bf16[16,128,128]{2,1,0:T(8,128)(2,1)}), bf16[16,128,128]{2,1,0:T(8,128)(2,1)S(1)}, u32[]{:S(2)}, u32[]{:S(2)}) %all-to-all-start) | async-done | bytes 524320 | tf_op jit(solution)/shard_map/all_to_all | solution.py:189
  28.5 1.5 %broadcast_in_dim.8 = bf16[4,4,128,512]{3,2,1,0:T(8,128)(2,1)} broadcast(bf16[4,128,512]{2,1,0:T(8,128)(2,1)S(1)} %broadcast_in_dim.7), dimensions={1,2,3} | broadcast | bytes 2621440 | tf_op jit(solution)/shard_map/broadcast_in_dim | solution.py:215
  30.1 4.3 %all-to-all-start.1 = ((bf16[4,4,128,512]{3,2,1,0:T(8,128)(2,1)}), bf16[4,4,128,512]{3,2,1,0:T(8,128)(2,1)S(1)}, u32[]{:S(2)}, u32[]{:S(2)}) async-start(bf16[4,4,128,512]{3,2,1,0:T(8,128)(2,1)} %broadcast_in_dim.8), calls=%async_computation.1 | async-start | bytes 4194304 | tf_op jit(solution)/shard_map/all_to_all | solution.py:189
  34.5 1.9 %collective-permute-start.3 = (bf16[4,16,512]{2,1,0:T(8,128)(2,1)S(1)}, bf16[4,16,512]{2,1,0:T(8,128)(2,1)S(1)}, u32[]{:S(2)}, u32[]{:S(2)}) collective-permute-start(bf16[4,16,512]{2,1,0:T(8,128)(2,1)S(1)} %pad_maximum_fusion.refs_4_), channel_id=1, source_target_pairs={{0,1},{1,2},{2,3},{3,0},{4,5},{5,6},{6,7},{7,4},{8,9},{9,10},{10,1... | collective-permute-start | bytes 196616 | tf_op jit(solution)/shard_map/ppermute | solution.py:194
  36.4 2.8 %collective-permute-start.4 = (bf16[4,16,512]{2,1,0:T(8,128)(2,1)S(1)}, bf16[4,16,512]{2,1,0:T(8,128)(2,1)S(1)}, u32[]{:S(2)}, u32[]{:S(2)}) collective-permute-start(bf16[4,16,512]{2,1,0:T(8,128)(2,1)S(1)} %pad_maximum_fusion.refs_4_), channel_id=1, source_target_pairs={{0,2},{1,3},{2,0},{3,1},{4,6},{5,7},{6,4},{7,5},{8,10},{9,11},{10,... | collective-permute-start | bytes 196616 | tf_op jit(solution)/shard_map/ppermute | solution.py:194
  39.2 4.3 %collective-permute-start.5 = (bf16[4,16,512]{2,1,0:T(8,128)(2,1)S(1)}, bf16[4,16,512]{2,1,0:T(8,128)(2,1)S(1)}, u32[]{:S(2)}, u32[]{:S(2)}) collective-permute-start(bf16[4,16,512]{2,1,0:T(8,128)(2,1)S(1)} %pad_maximum_fusion.refs_4_), channel_id=1, source_target_pairs={{0,3},{1,0},{2,1},{3,2},{4,7},{5,4},{6,5},{7,6},{8,11},{9,8},{10,9... | collective-permute-start | bytes 196616 | tf_op jit(solution)/shard_map/ppermute | solution.py:194
  43.5 2.3 %collective-permute-done.5.refs_7_ = bf16[4,16,512]{2,1,0:T(8,128)(2,1)S(1)} collective-permute-done((bf16[4,16,512]{2,1,0:T(8,128)(2,1)S(1)}, bf16[4,16,512]{2,1,0:T(8,128)(2,1)S(1)}, u32[]{:S(2)}, u32[]{:S(2)}) %collective-permute-start.5) | collective-permute-done | bytes 65568 | tf_op jit(solution)/shard_map/ppermute | solution.py:194
  45.9 2.2 %collective-permute-start.6 = (bf16[4,144,512]{2,1,0:T(8,128)(2,1)S(1)}, bf16[4,144,512]{2,1,0:T(8,128)(2,1)S(1)}, u32[]{:S(2)}, u32[]{:S(2)}) collective-permute-start(bf16[4,144,512]{2,1,0:T(8,128)(2,1)S(1)} %shard_map.86.refs_0_), channel_id=1, source_target_pairs={{0,16},{16,32},{32,48},{48,0},{1,17},{17,33},{33,49},{49,1},{2,18}... | collective-permute-start | bytes 1769480 | tf_op jit(solution)/shard_map/ppermute | solution.py:194
  48.1 4.3 %collective-permute-start.7 = (bf16[4,144,512]{2,1,0:T(8,128)(2,1)S(1)}, bf16[4,144,512]{2,1,0:T(8,128)(2,1)}, u32[]{:S(2)}, u32[]{:S(2)}) collective-permute-start(bf16[4,144,512]{2,1,0:T(8,128)(2,1)S(1)} %shard_map.86.refs_0_), channel_id=1, source_target_pairs={{0,32},{16,48},{32,0},{48,16},{1,33},{17,49},{33,1},{49,17},{2,34}... | collective-permute-start | bytes 1769480 | tf_op jit(solution)/shard_map/ppermute | solution.py:194
  52.4 3.1 %collective-permute-start.8 = (bf16[4,144,512]{2,1,0:T(8,128)(2,1)S(1)}, bf16[4,144,512]{2,1,0:T(8,128)(2,1)}, u32[]{:S(2)}, u32[]{:S(2)}) collective-permute-start(bf16[4,144,512]{2,1,0:T(8,128)(2,1)S(1)} %shard_map.86.refs_0_), channel_id=1, source_target_pairs={{0,48},{16,0},{32,16},{48,32},{1,49},{17,1},{33,17},{49,33},{2,50}... | collective-permute-start | bytes 1769480 | tf_op jit(solution)/shard_map/ppermute | solution.py:194
  55.5 5.2 %collective-permute-done.6.refs_1_ = bf16[4,144,512]{2,1,0:T(8,128)(2,1)S(1)} collective-permute-done((bf16[4,144,512]{2,1,0:T(8,128)(2,1)S(1)}, bf16[4,144,512]{2,1,0:T(8,128)(2,1)S(1)}, u32[]{:S(2)}, u32[]{:S(2)}) %collective-permute-start.6) | collective-permute-done | bytes 589856 | tf_op jit(solution)/shard_map/ppermute | solution.py:194
  60.7 12.8 %collective-permute-done.7.refs_2_ = bf16[4,144,512]{2,1,0:T(8,128)(2,1)} collective-permute-done((bf16[4,144,512]{2,1,0:T(8,128)(2,1)S(1)}, bf16[4,144,512]{2,1,0:T(8,128)(2,1)}, u32[]{:S(2)}, u32[]{:S(2)}) %collective-permute-start.7) | collective-permute-done | bytes 589856 | tf_op jit(solution)/shard_map/ppermute | solution.py:194
  73.5 4.9 %collective-permute-done.8.refs_3_ = bf16[4,144,512]{2,1,0:T(8,128)(2,1)} collective-permute-done((bf16[4,144,512]{2,1,0:T(8,128)(2,1)S(1)}, bf16[4,144,512]{2,1,0:T(8,128)(2,1)}, u32[]{:S(2)}, u32[]{:S(2)}) %collective-permute-start.8) | collective-permute-done | bytes 589856 | tf_op jit(solution)/shard_map/ppermute | solution.py:194
  78.3 3.1 %shard_map.87 = (f32[272,512]{1,0:T(8,128)S(1)}, f32[272,512]{1,0:T(8,128)S(1)}) custom-call(s32[1]{0:T(128)} %bitcast.2.y_ref, s32[1]{0:T(128)} %bitcast.3.x_ref, s32[1]{0:T(128)} %bitcast.4.core_ref, f32[1,2048]{1,0:T(1,128)S(1)} %bitcast.24, bf16[4,4,128,512]{3,2,1,0:T(8,128)(2,1)S(1)} %all-to-all-done.1.b_ref, ...), custom_call_target="tpu_custom_call" | custom-call | tf_op jit(solution)/shard_map/pallas_call | solution.py:178
  81.4 3.6 %collective-permute-start.9 = (f32[272,512]{1,0:T(8,128)S(1)}, f32[272,512]{1,0:T(8,128)S(1)}, u32[]{:S(2)}, u32[]{:S(2)}) collective-permute-start(f32[272,512]{1,0:T(8,128)S(1)} %get-tuple-element.20), channel_id=1, source_target_pairs={{0,64},{64,0},{1,65},{65,1},{2,66},{66,2},{3,67},{67,3},{4,68},{68... | collective-permute-start | bytes 1671176 | tf_op jit(solution)/shard_map/ppermute | solution.py:194
  85.0 1.6 %collective-permute-done.9.got_ref = f32[272,512]{1,0:T(8,128)S(1)} collective-permute-done((f32[272,512]{1,0:T(8,128)S(1)}, f32[272,512]{1,0:T(8,128)S(1)}, u32[]{:S(2)}, u32[]{:S(2)}) %collective-permute-start.9) | collective-permute-done | bytes 557088 | tf_op jit(solution)/shard_map/ppermute | solution.py:194
  86.6 0.8 shard_map.88
  87.3 14.3 %all-to-all-start.2 = ((bf16[16,16,640]{2,1,0:T(8,128)(2,1)}), bf16[16,16,640]{2,1,0:T(8,128)(2,1)S(1)}, u32[]{:S(2)}, u32[]{:S(2)}) async-start(bf16[16,16,640]{2,1,0:T(8,128)(2,1)} %bitcast.14), calls=%async_computation.2 | async-start | bytes 655360 | tf_op jit(solution)/shard_map/all_to_all | solution.py:189
  101.7 19.3 %all-to-all-done.2 = bf16[16,16,640]{2,1,0:T(8,128)(2,1)S(1)} async-done(((bf16[16,16,640]{2,1,0:T(8,128)(2,1)}), bf16[16,16,640]{2,1,0:T(8,128)(2,1)S(1)}, u32[]{:S(2)}, u32[]{:S(2)}) %all-to-all-start.2) | async-done | bytes 327712 | tf_op jit(solution)/shard_map/all_to_all | solution.py:189
  121.0 0.8 shard_map.89
  121.8 21.7 %all_to_all.20.in_ref = bf16[32,2,16,256]{3,2,1,0:T(8,128)(2,1)S(1)} all-to-all(bf16[32,2,16,256]{3,2,1,0:T(8,128)(2,1)S(1)} %get-tuple-element.23), channel_id=1, replica_groups=mesh['y'=4,'core'=2,'x'=4,'zh'=4,'zl'=4] {'y','core','x'}, dimensions={0} | all-to-all | bytes 1048576 | tf_op jit(solution)/shard_map/all_to_all | solution.py:189
  143.5 1.0 shard_map.90
  (24 shorter events, 1.3 us)
Async XLA Ops:
  0.6 0.8 copy-start.1
  1.5 0.8 copy-start.2
  3.2 24.7 %all-to-all-start = ((bf16[16,128,128]{2,1,0:T(8,128)(2,1)}), bf16[16,128,128]{2,1,0:T(8,128)(2,1)S(1)}, u32[]{:S(2)}, u32[]{:S(2)}) async-start(bf16[16,128,128]{2,1,0:T(8,128)(2,1)} %bitcast.6), calls=%async_computation | async-start | bytes 1048576 | tf_op jit(solution)/shard_map/all_to_all | solution.py:189
  12.2 1.0 copy-start
  13.2 0.7 copy-start.3
  13.9 0.7 copy-start.5
  15.2 19.3 %collective-permute-start = (bf16[144,512]{1,0:T(8,128)(2,1)S(1)}, bf16[144,512]{1,0:T(8,128)(2,1)S(1)}, u32[]{:S(2)}, u32[]{:S(2)}) collective-permute-start(bf16[144,512]{1,0:T(8,128)(2,1)S(1)} %get-tuple-element.16), channel_id=1, source_target_pairs={{0,128},{128,256},{256,384},{384,0},{1,129},{129,257},{257,385},{3... | collective-permute-start | bytes 442376 | tf_op jit(solution)/shard_map/ppermute | solution.py:194
  18.4 16.0 %collective-permute-start.1 = (bf16[144,512]{1,0:T(8,128)(2,1)S(1)}, bf16[144,512]{1,0:T(8,128)(2,1)S(1)}, u32[]{:S(2)}, u32[]{:S(2)}) collective-permute-start(bf16[144,512]{1,0:T(8,128)(2,1)S(1)} %get-tuple-element.17), channel_id=1, source_target_pairs={{0,256},{128,384},{256,0},{384,128},{1,257},{129,385},{257,1},{385... | collective-permute-start | bytes 442376 | tf_op jit(solution)/shard_map/ppermute | solution.py:194
  22.9 11.5 %collective-permute-start.2 = (bf16[144,512]{1,0:T(8,128)(2,1)S(1)}, bf16[144,512]{1,0:T(8,128)(2,1)S(1)}, u32[]{:S(2)}, u32[]{:S(2)}) collective-permute-start(bf16[144,512]{1,0:T(8,128)(2,1)S(1)} %get-tuple-element.18), channel_id=1, source_target_pairs={{0,384},{128,0},{256,128},{384,256},{1,385},{129,1},{257,129},{385... | collective-permute-start | bytes 442376 | tf_op jit(solution)/shard_map/ppermute | solution.py:194
  30.1 48.3 %copy-start.4 = (f32[2048]{0:T(1024)S(1)}, f32[2048]{0:T(1024)}, u32[]{:S(2)}) copy-start(f32[2048]{0:T(1024)} %param.6) | copy-start | bytes 24580
  30.1 48.3 %all-to-all-start.1 = ((bf16[4,4,128,512]{3,2,1,0:T(8,128)(2,1)}), bf16[4,4,128,512]{3,2,1,0:T(8,128)(2,1)S(1)}, u32[]{:S(2)}, u32[]{:S(2)}) async-start(bf16[4,4,128,512]{3,2,1,0:T(8,128)(2,1)} %broadcast_in_dim.8), calls=%async_computation.1 | async-start | bytes 4194304 | tf_op jit(solution)/shard_map/all_to_all | solution.py:189
  34.5 9.0 %collective-permute-start.3 = (bf16[4,16,512]{2,1,0:T(8,128)(2,1)S(1)}, bf16[4,16,512]{2,1,0:T(8,128)(2,1)S(1)}, u32[]{:S(2)}, u32[]{:S(2)}) collective-permute-start(bf16[4,16,512]{2,1,0:T(8,128)(2,1)S(1)} %pad_maximum_fusion.refs_4_), channel_id=1, source_target_pairs={{0,1},{1,2},{2,3},{3,0},{4,5},{5,6},{6,7},{7,4},{8,9},{9,10},{10,1... | collective-permute-start | bytes 196616 | tf_op jit(solution)/shard_map/ppermute | solution.py:194
  36.4 7.1 %collective-permute-start.4 = (bf16[4,16,512]{2,1,0:T(8,128)(2,1)S(1)}, bf16[4,16,512]{2,1,0:T(8,128)(2,1)S(1)}, u32[]{:S(2)}, u32[]{:S(2)}) collective-permute-start(bf16[4,16,512]{2,1,0:T(8,128)(2,1)S(1)} %pad_maximum_fusion.refs_4_), channel_id=1, source_target_pairs={{0,2},{1,3},{2,0},{3,1},{4,6},{5,7},{6,4},{7,5},{8,10},{9,11},{10,... | collective-permute-start | bytes 196616 | tf_op jit(solution)/shard_map/ppermute | solution.py:194
  39.2 6.6 %collective-permute-start.5 = (bf16[4,16,512]{2,1,0:T(8,128)(2,1)S(1)}, bf16[4,16,512]{2,1,0:T(8,128)(2,1)S(1)}, u32[]{:S(2)}, u32[]{:S(2)}) collective-permute-start(bf16[4,16,512]{2,1,0:T(8,128)(2,1)S(1)} %pad_maximum_fusion.refs_4_), channel_id=1, source_target_pairs={{0,3},{1,0},{2,1},{3,2},{4,7},{5,4},{6,5},{7,6},{8,11},{9,8},{10,9... | collective-permute-start | bytes 196616 | tf_op jit(solution)/shard_map/ppermute | solution.py:194
  45.9 14.8 %collective-permute-start.6 = (bf16[4,144,512]{2,1,0:T(8,128)(2,1)S(1)}, bf16[4,144,512]{2,1,0:T(8,128)(2,1)S(1)}, u32[]{:S(2)}, u32[]{:S(2)}) collective-permute-start(bf16[4,144,512]{2,1,0:T(8,128)(2,1)S(1)} %shard_map.86.refs_0_), channel_id=1, source_target_pairs={{0,16},{16,32},{32,48},{48,0},{1,17},{17,33},{33,49},{49,1},{2,18}... | collective-permute-start | bytes 1769480 | tf_op jit(solution)/shard_map/ppermute | solution.py:194
  48.1 25.4 %collective-permute-start.7 = (bf16[4,144,512]{2,1,0:T(8,128)(2,1)S(1)}, bf16[4,144,512]{2,1,0:T(8,128)(2,1)}, u32[]{:S(2)}, u32[]{:S(2)}) collective-permute-start(bf16[4,144,512]{2,1,0:T(8,128)(2,1)S(1)} %shard_map.86.refs_0_), channel_id=1, source_target_pairs={{0,32},{16,48},{32,0},{48,16},{1,33},{17,49},{33,1},{49,17},{2,34}... | collective-permute-start | bytes 1769480 | tf_op jit(solution)/shard_map/ppermute | solution.py:194
  52.4 25.9 %collective-permute-start.8 = (bf16[4,144,512]{2,1,0:T(8,128)(2,1)S(1)}, bf16[4,144,512]{2,1,0:T(8,128)(2,1)}, u32[]{:S(2)}, u32[]{:S(2)}) collective-permute-start(bf16[4,144,512]{2,1,0:T(8,128)(2,1)S(1)} %shard_map.86.refs_0_), channel_id=1, source_target_pairs={{0,48},{16,0},{32,16},{48,32},{1,49},{17,1},{33,17},{49,33},{2,50}... | collective-permute-start | bytes 1769480 | tf_op jit(solution)/shard_map/ppermute | solution.py:194
  81.4 39.6 %copy-start.6 = (s32[128]{0:T(128)S(1)}, s32[128]{0:T(128)}, u32[]{:S(2)}) copy-start(s32[128]{0:T(128)} %param.9) | copy-start | bytes 1540
  81.4 5.1 %collective-permute-start.9 = (f32[272,512]{1,0:T(8,128)S(1)}, f32[272,512]{1,0:T(8,128)S(1)}, u32[]{:S(2)}, u32[]{:S(2)}) collective-permute-start(f32[272,512]{1,0:T(8,128)S(1)} %get-tuple-element.20), channel_id=1, source_target_pairs={{0,64},{64,0},{1,65},{65,1},{2,66},{66,2},{3,67},{67,3},{4,68},{68... | collective-permute-start | bytes 1671176 | tf_op jit(solution)/shard_map/ppermute | solution.py:194
  87.3 33.7 %all-to-all-start.2 = ((bf16[16,16,640]{2,1,0:T(8,128)(2,1)}), bf16[16,16,640]{2,1,0:T(8,128)(2,1)S(1)}, u32[]{:S(2)}, u32[]{:S(2)}) async-start(bf16[16,16,640]{2,1,0:T(8,128)(2,1)} %bitcast.14), calls=%async_computation.2 | async-start | bytes 655360 | tf_op jit(solution)/shard_map/all_to_all | solution.py:189

commit v3 on v0

v3 whole, which is shorter than its diff:
```python
import jax
import jax.numpy as jnp
from jax import lax
from jax.experimental import pallas as pl
from jax.experimental.pallas import tpu as pltpu
from jax.sharding import Mesh, PartitionSpec as P

AXES = ("y", "core", "x", "zh", "zl")
LANES = 128
AUX = 16
VMEM = pl.BlockSpec(memory_space=pltpu.VMEM)
SMEM = pl.BlockSpec(memory_space=pltpu.SMEM)
PARAMS = pltpu.CompilerParams(vmem_limit_bytes=20 * 1024 * 1024)


def split3(v):
    hi = v.astype(jnp.bfloat16).astype(jnp.float32)
    mid = (v - hi).astype(jnp.bfloat16).astype(jnp.float32)
    low = (v - hi - mid).astype(jnp.bfloat16).astype(jnp.float32)
    return hi, mid, low


def column(row):
    return jnp.broadcast_to(row, (LANES, LANES)).T


def prepare(zl_ref, hidden_in, key_in, value_in, ids_in, gain_in, *refs):
    packed_ref, hidden_ref, key_ref, value_ref, ids_ref, gain_ref, sems = refs
    copies = [
        pltpu.make_async_copy(source, target, sems.at[i])
        for i, (source, target) in enumerate(
            [
                (hidden_in, hidden_ref),
                (key_in, key_ref),
                (value_in, value_ref),
                (ids_in, ids_ref),
                (gain_in, gain_ref),
            ]
        )
    ]
    for copy in copies:
        copy.start()
    n_x, n_zl, _, _ = packed_ref.shape
    toks, width = hidden_ref.shape
    n_union = ids_ref.shape[1]
    per = n_union // n_zl
    for copy in copies[1:]:
        copy.wait()
    for x in range(n_x):
        source = key_ref if x < n_x // 2 else value_ref
        at = LANES * (x % (n_x // 2))
        for z in range(n_zl):
            packed_ref[x, z, :toks] = source[:, at : at + LANES]
    ids = column(ids_ref[...].astype(jnp.float32))[:, :1].astype(jnp.int32) - zl_ref[0] * width
    hit = lax.broadcasted_iota(jnp.int32, (n_union, width), 1) == ids
    gains = jnp.sum(jnp.where(hit, gain_ref[...], 0.0), axis=1, keepdims=True)
    copies[0].wait()
    hidden = hidden_ref[...]
    hidden_f = hidden.astype(jnp.float32)
    squares = jnp.sum(hidden_f * hidden_f, axis=1, keepdims=True)
    picked = lax.dot_general(
        jnp.where(hit, 1.0, 0.0).astype(jnp.bfloat16),
        hidden,
        (((1,), (1,)), ((), ())),
        preferred_element_type=jnp.float32,
    ).astype(jnp.bfloat16)
    lane = lax.broadcasted_iota(jnp.int32, (toks, LANES), 1)
    table = jnp.zeros((toks, LANES), jnp.float32)
    for place, part in enumerate(split3(squares) + split3(gains)):
        table = jnp.where(lane == place, part, table)
    extra = table.T[:AUX].astype(jnp.bfloat16)
    for x in range(n_x):
        for z in range(n_zl):
            packed_ref[x, z, toks : toks + per] = picked[per * z : per * (z + 1)]
            packed_ref[x, z, toks + per :] = extra


def unpack(features, zl_ref, in_ref, out_ref, scale_ref, union_ref, gain_ref):
    n_x, n_zl, rows, _ = in_ref.shape
    toks = LANES
    per = rows - toks - AUX
    total = jnp.zeros((per, n_zl * LANES), jnp.float32)
    for x in range(n_x):
        extra = in_ref[x, 0, toks + per :].astype(jnp.float32)
        picked = in_ref[x, 0, toks : toks + per].astype(jnp.float32)
        for z in range(1, n_zl):
            extra = extra + in_ref[x, z, toks + per :].astype(jnp.float32)
            picked = picked + in_ref[x, z, toks : toks + per].astype(jnp.float32)
        if x == 0:
            gain_ref[...] = column(extra[3:4] + extra[4:5] + extra[5:6])
        squares = extra[0:1] + extra[1:2] + extra[2:3]
        scale = lax.rsqrt(squares / features + 1e-05)
        gains = gain_ref[pl.ds(pl.multiple_of(zl_ref[0] * per, per), per), :]
        normed = (picked * scale * gains).astype(jnp.bfloat16)
        right = jnp.concatenate([in_ref[x, z, :toks] for z in range(n_zl)], axis=1)
        total = total + jnp.dot(normed, right, preferred_element_type=jnp.float32)
        out_ref[x] = right
        table = jnp.zeros((AUX // 2, LANES), jnp.float32) + scale
        scale_ref[:, x * LANES : (x + 1) * LANES] = table
    count, few, _ = union_ref.shape
    for i in range(count):
        union_ref[i] = total[i * few : (i + 1) * few]


def sum_spread(groups, in_ref, out_ref):
    count = in_ref.shape[0]
    rest = count // groups
    few = in_ref.shape[1]
    for j in range(rest):
        total = in_ref[j].astype(jnp.float32)
        for i in range(1, groups):
            total = total + in_ref[i * rest + j].astype(jnp.float32)
        total = total.astype(jnp.bfloat16)
        for to in range(out_ref.shape[0]):
            out_ref[to, j * few : (j + 1) * few] = total


def multiply(x_ref, core_ref, gain_ref, scale_ref, right_ref, *refs):
    own_ref, other_ref, total_ref = refs[-3:]
    lefts = refs[:-3]
    n_x, n_y = len(lefts), own_ref.shape[0]
    toks, width = lefts[0].shape
    tile = width // n_y
    columns = []
    for j in range(n_x):
        x = lax.rem(x_ref[0] + n_x - j, n_x)
        columns.append(column(scale_ref[:1, pl.ds(pl.multiple_of(x * LANES, LANES), LANES)]))
    for y in range(n_y):
        at = slice(y * tile, (y + 1) * tile)
        normed, right = [], []
        for j, left_ref in enumerate(lefts):
            x = lax.rem(x_ref[0] + n_x - j, n_x)
            scales = jnp.concatenate([columns[j]] * (tile // LANES), axis=1)
            left = left_ref[:, at].astype(jnp.float32) * scales * gain_ref[:, at]
            normed.append(left.astype(jnp.bfloat16))
            right.append(right_ref[x])
        total_ref[...] = lax.dot_general(
            jnp.concatenate(normed, axis=0),
            jnp.concatenate(right, axis=0),
            (((0,), (0,)), ((), ())),
            preferred_element_type=jnp.float32,
        )
        rows = tile // 2
        for out_ref, core in ((own_ref, core_ref[0]), (other_ref, 1 - core_ref[0])):
            out_ref[y] = total_ref[pl.ds(pl.multiple_of(core * rows, rows), rows), :]


def add_cores(own_ref, got_ref, union_ref, out_ref):
    n_y, n_x, rows, _ = out_ref.shape
    rows -= union_ref.shape[1]
    for y in range(n_y):
        for x in range(n_x):
            at = slice(x * rows, (x + 1) * rows)
            out_ref[y, x, :rows] = (own_ref[y, at] + got_ref[y, at]).astype(jnp.bfloat16)
            out_ref[y, x, rows:] = union_ref[0]


def add_y(in_ref, out_ref, union_ref):
    n_y, n_x, _, _ = in_ref.shape
    n_zh, _, rows, _ = out_ref.shape
    for x in range(n_x):
        for z in range(n_zh):
            at = slice(z * rows, (z + 1) * rows)
            total = in_ref[0, x, at].astype(jnp.float32)
            for y in range(1, n_y):
                total = total + in_ref[y, x, at].astype(jnp.float32)
            out_ref[z, x] = total.astype(jnp.bfloat16)
        for y in range(n_y):
            union_ref[y, x] = in_ref[y, x, n_zh * rows :]


def finish(first_ref, ids_ref, in_ref, key_ref, value_ref):
    n_zh, n_x, rows, cols = in_ref.shape
    row = lax.broadcasted_iota(jnp.int32, (rows, LANES), 0) + first_ref[0]
    hits = jnp.sum(jnp.where(row == ids_ref[...], 1.0, 0.0), axis=1, keepdims=True)
    for x in range(n_x):
        total = in_ref[0, x].astype(jnp.float32)
        for z in range(1, n_zh):
            total = total + in_ref[z, x].astype(jnp.float32)
        total = jnp.where(hits > 0.0, 0.0, total)
        out_ref = value_ref if x // 2 else key_ref
        for z in range(cols // LANES):
            at = LANES * (2 * z + x % 2)
            out_ref[0, :, at : at + LANES] = total[:, z * LANES : (z + 1) * LANES]


def lay_out(n_zl, core_ref, own_ref, got_ref, key_ref, value_ref):
    n_y, n_x, rows, cols = own_ref.shape
    few = rows // n_zl
    per = key_ref.shape[0] // n_zl
    first = core_ref[0] == 0
    for x in range(n_x):
        out_ref = value_ref if x // 2 else key_ref
        blocks = []
        for y in range(n_y):
            own, got = own_ref[y, x].astype(jnp.float32), got_ref[y, x].astype(jnp.float32)
            blocks += [jnp.where(first, own, got), jnp.where(first, got, own)]
        for z in range(n_zl):
            lines = jnp.concatenate([block[few * z : few * (z + 1)] for block in blocks], axis=0)
            for j in range(cols // LANES):
                at = LANES * (2 * j + x % 2)
                out_ref[per * z : per * (z + 1), at : at + LANES] = lines[:, j * LANES : (j + 1) * LANES]


def call(body, out_shape, args, scalars=0, scratch=(), cost=0):
    single = not isinstance(out_shape, tuple)
    return pl.pallas_call(
        body,
        out_shape=out_shape,
        in_specs=[SMEM] * scalars + [VMEM] * (len(args) - scalars),
        out_specs=VMEM if single else tuple(VMEM for _ in out_shape),
        scratch_shapes=scratch,
        cost_estimate=pl.CostEstimate(flops=0, bytes_accessed=cost, transcendentals=0) if cost else None,
        compiler_params=PARAMS,
    )(*args)


def exchange(v, axes):
    return lax.all_to_all(v, axes, split_axis=0, concat_axis=0, tiled=True)


def shift(v, axis, by):
    count = lax.axis_size(axis)
    return lax.ppermute(v, axis, [(i, (i + by) % count) for i in range(count)])


def per_device(hidden_in, norm_gain, key_cotangent, value_cotangent, union_ids):
    bf16, f32 = jnp.bfloat16, jnp.float32
    toks, width = hidden_in.shape
    n_y, n_core, n_x, n_zh, n_zl = (lax.axis_size(a) for a in AXES)
    y, core, x, zh, zl = (lax.axis_index(a).astype(jnp.int32) for a in AXES)
    n_union = union_ids.shape[0]
    heads = key_cotangent.shape[1] * n_zl
    cols = n_zl * LANES
    per = n_union // n_zl
    shape = jax.ShapeDtypeStruct
    ids = union_ids.reshape(1, n_union)
    gain = norm_gain.reshape(1, width)
    at_y, at_x, at_core, at_zl = (v.reshape(1) for v in (y, x, core, zl))

    inputs = (hidden_in, key_cotangent, value_cotangent, ids, gain)
    packed = pl.pallas_call(
        prepare,
        out_shape=shape((n_x, n_zl, toks + per + AUX, LANES), bf16),
        in_specs=[SMEM] + [pl.BlockSpec(memory_space=pl.ANY)] * len(inputs),
        out_specs=VMEM,
        scratch_shapes=[pltpu.VMEM(v.shape, v.dtype) for v in inputs]
        + [pltpu.SemaphoreType.DMA((len(inputs),))],
        compiler_params=pltpu.CompilerParams(vmem_limit_bytes=60 * 1024 * 1024),
    )(at_zl, *inputs)
    packed = exchange(packed.reshape((n_x * n_zl,) + packed.shape[2:]), ("x", "zl"))
    few = per // (n_y * n_core)
    right, scale, outliers = call(
        lambda *refs: unpack(float(width * n_zl), *refs),
        (
            shape((n_x, toks, cols), bf16),
            shape((AUX // 2, n_x * LANES), f32),
            shape((n_y * n_core, few, cols), f32),
        ),
        (at_zl, packed.reshape((n_x, n_zl) + packed.shape[1:])),
        1,
        [pltpu.VMEM((LANES, LANES), f32)],
    )
    left = [hidden_in] + [shift(hidden_in, "x", k) for k in range(1, n_x)]

    outliers = exchange(outliers, ("y", "core"))
    outliers = call(
        lambda *refs: sum_spread(n_y * n_core, *refs),
        shape((n_zh * n_zl, few, cols), bf16),
        (outliers,),
    )
    outliers = exchange(outliers, ("zh", "zl"))
    outliers = call(
        lambda *refs: sum_spread(n_zh, *refs),
        shape((1, n_zl * few, cols), bf16),
        (outliers,),
    )

    half = shape((n_y, width // (n_y * n_core), cols), f32)
    own, other = call(
        multiply,
        (half, half),
        (at_x, at_core, gain, scale, right, *left),
        2,
        [pltpu.VMEM((width // n_y, cols), f32)],
        cost=128 * 1024 * 1024,
    )
    other, outliers = lax.optimization_barrier((other, outliers))
    got = shift(other, "core", 1)
    rows = width // (n_y * n_core * n_x * n_zh)
    lines = n_zh * rows + n_zl * few
    pieces = call(add_cores, shape((n_y, n_x, lines, cols), bf16), (own, got, outliers))
    pieces = exchange(pieces.reshape(n_y * n_x, lines, cols), ("y", "x"))
    pieces, outliers = call(
        add_y,
        (shape((n_zh, n_x, rows, cols), bf16), shape((n_y, n_x, n_zl * few, cols), bf16)),
        (pieces.reshape(n_y, n_x, lines, cols),),
    )
    union = shape((n_union, heads), f32)
    union_key, union_value = call(
        lambda *refs: lay_out(n_zl, *refs),
        (union, union),
        (at_core, outliers, shift(outliers, "core", 1)),
        1,
    )
    pieces = exchange(pieces, "zh")
    first = zl * width + rows * (((y * n_core + core) * n_x + x) * n_zh + zh)
    grad = shape((1, rows, heads), f32)
    grad_key, grad_value = call(finish, (grad, grad), (first.reshape(1), ids, pieces), 1)
    return (grad_key, grad_value, union_key, union_value)


def solution(mesh):
    sizes = dict(mesh.shape)
    split = Mesh(
        mesh.devices.reshape(sizes["group"] // 2, 2, 4, sizes["loop"] // 4, sizes["mp"]), AXES
    )
    rows = ("y", "core", "x", "zh")
    return jax.shard_map(
        per_device,
        mesh=split,
        in_specs=(P(rows, "zl"), P("zl"), P(rows, "zl"), P(rows, "zl"), P()),
        out_specs=(P("zl", rows, None), P("zl", rows, None), P(), P()),
        check_vma=False,
    )
```

time: 882 us -> 128 us (0.15)
  waiting for transfers between devices: 724 us -> 26.4 us
  local copies, waits for them, and re-layouts: 68.3 us -> 8.71 us
  starting transfers between devices: 24.7 us -> 48.6 us
  other arithmetic: 15.8 us -> 0 us
  between operations: 14.1 us -> 0.82 us
  matrix products: 9.18 us -> 0 us
    psum x1 -> x0, waiting for transfers between devices: 724 us -> none  [per_device(): union_sum = lax.psum(union_part, ('group', 'loop', 'mp'))]
    all_to_all x0 -> x2, blocking collectives: none -> 33.3 us  [exchange(): return lax.all_to_all(v, axes, split_axis=0, concat_axis=0, tiled=True)]
    reshape x2 -> x0, local copies, waits for them, and re-layouts: 32 us -> none  [per_device(): partial_value = partial_value.reshape(local_width, 2 * head_cols)]
    dot_general x1 -> x0, local copies, waits for them, and re-layouts: 24.1 us -> none  [per_device(): jnp.einsum('tr,ktn->rkn', normed, lax.all_gather(stacked, 'mp', axis=2, t...]
    all_to_all x1 -> x3, waiting for transfers between devices: 0.01 us -> 21.3 us  [exchange(): return lax.all_to_all(v, axes, split_axis=0, concat_axis=0, tiled=True)]
    ppermute x0 -> x5, starting transfers between devices: none -> 18.9 us  [shift(): return lax.ppermute(v, axis, [(i, (i + by) % count) for i in range(count)])]
    all_gather x1 -> x0, blocking collectives: 16.3 us -> none  [per_device(): lax.all_gather(stacked, 'mp', axis=2, tiled=True)]
    dot_general x1 -> x0, matrix products: 9.18 us -> none  [per_device(): jnp.einsum('tr,ktn->rkn', normed, lax.all_gather(stacked, 'mp', axis=2, t...]
  transfers between devices with their start and end apart: 2 -> 8, of which waited for: 1 -> 5; matrix products, arithmetic and copies ran while one was open for 3% -> 0% of each run, Pallas kernels for 0% -> 3%
where the time goes in v3:
time: 128 us; the launch traced here: 126 us
  starting transfers between devices  48.6 us (38%)
  blocking collectives  33.3 us (26%)
  waiting for transfers between devices  26.4 us (21%)
  local copies, waits for them, and re-layouts  8.71 us (7%)
  Pallas kernels  8.06 us (6%)
    all_to_all x2, blocking collectives, exchange(): return lax.all_to_all(v, axes, split_axis=0, concat_axis=0, tiled=True)  33.3 us
    all_to_all x3, starting transfers between devices, exchange(): return lax.all_to_all(v, axes, split_axis=0, concat_axis=0, tiled=True)  29.7 us
    all_to_all x3, waiting for transfers between devices, exchange(): return lax.all_to_all(v, axes, split_axis=0, concat_axis=0, tiled=True)  21.3 us
    ppermute x5, starting transfers between devices, shift(): return lax.ppermute(v, axis, [(i, (i + by) % count) for i in range(count)])  18.9 us
    unnamed x24, local copies, waits for them, and re-layouts  8.71 us
    pallas_call x8, Pallas kernels, call(): pl.pallas_call(body, out_shape=out_shape, in_specs=[SMEM] * scalars + [VM...  5.32 us
    ppermute x5, waiting for transfers between devices, shift(): return lax.ppermute(v, axis, [(i, (i + by) % count) for i in range(count)])  5.1 us
    pallas_call x1, Pallas kernels, per_device(): pl.pallas_call(prepare, out_shape=shape((n_x, n_zl, toks + per + AUX, LAN...  2.74 us
  transfers between devices with their start and end apart: 8, of which 5 were waited for; matrix products, arithmetic and copies ran while one was open for 0% of the time, Pallas kernels for 3%

profile of v3, /device:TPU:1, one launch (start us, length us, event | category | flops | bytes accessed | tf_op | source)
XLA Modules:
  0.0 125.9 jit_solution(17529552575879713045)
XLA Ops:
  0.7 2.7 %shard_map.84 = bf16[4,4,176,128]{3,2,1,0:T(8,128)(2,1)} custom-call(s32[1]{0:T(128)} %bitcast.5.zl_ref.refs_0_, bf16[128,2048]{1,0:T(8,128)(2,1)} %refs_0_.1, bf16[128,256]{1,0:T(8,128)(2,1)} %key_in.1, bf16[128,256]{1,0:T(8,128)(2,1)} %value_in.1, s32[1,128]{1,0:T(1,128)} %bitcast.15, f32[1,2048]{1,0:T(1,128)} %bitcast.13), custom_call_target="tpu_custom_call" | custom-call | tf_op jit(solution)/shard_map/pallas_call | solution.py:242
  3.4 9.0 %all-to-all-start = ((bf16[16,176,128]{2,1,0:T(8,128)(2,1)}), bf16[16,176,128]{2,1,0:T(8,128)(2,1)S(1)}, u32[]{:S(2)}, u32[]{:S(2)}) async-start(bf16[16,176,128]{2,1,0:T(8,128)(2,1)} %bitcast.17), calls=%async_computation | async-start | bytes 1441792 | tf_op jit(solution)/shard_map/all_to_all | solution.py:219
  12.5 4.8 %collective-permute-start.1 = (bf16[128,2048]{1,0:T(8,128)(2,1)S(1)}, bf16[128,2048]{1,0:T(8,128)(2,1)S(1)}, u32[]{:S(2)}, u32[]{:S(2)}) collective-permute-start(bf16[128,2048]{1,0:T(8,128)(2,1)S(1)} %copy-done), channel_id=1, source_target_pairs={{0,32},{16,48},{32,0},{48,16},{1,33},{17,49},{33,1},{49,17},{2,34}... | collective-permute-start | bytes 1572872 | tf_op jit(solution)/shard_map/ppermute | solution.py:224
  17.2 2.2 %collective-permute-start = (bf16[128,2048]{1,0:T(8,128)(2,1)S(1)}, bf16[128,2048]{1,0:T(8,128)(2,1)S(1)}, u32[]{:S(2)}, u32[]{:S(2)}) collective-permute-start(bf16[128,2048]{1,0:T(8,128)(2,1)S(1)} %copy-done), channel_id=1, source_target_pairs={{0,16},{16,32},{32,48},{48,0},{1,17},{17,33},{33,49},{49,1},{2,18}... | collective-permute-start | bytes 1572872 | tf_op jit(solution)/shard_map/ppermute | solution.py:224
  19.4 4.3 %collective-permute-start.2 = (bf16[128,2048]{1,0:T(8,128)(2,1)S(1)}, bf16[128,2048]{1,0:T(8,128)(2,1)S(1)}, u32[]{:S(2)}, u32[]{:S(2)}) collective-permute-start(bf16[128,2048]{1,0:T(8,128)(2,1)S(1)} %copy-done), channel_id=1, source_target_pairs={{0,48},{16,0},{32,16},{48,32},{1,49},{17,1},{33,17},{49,33},{2,50}... | collective-permute-start | bytes 1572872 | tf_op jit(solution)/shard_map/ppermute | solution.py:224
  23.7 8.8 %all-to-all-done = bf16[16,176,128]{2,1,0:T(8,128)(2,1)S(1)} async-done(((bf16[16,176,128]{2,1,0:T(8,128)(2,1)}), bf16[16,176,128]{2,1,0:T(8,128)(2,1)S(1)}, u32[]{:S(2)}, u32[]{:S(2)}) %all-to-all-start) | async-done | bytes 720928 | tf_op jit(solution)/shard_map/all_to_all | solution.py:219
  32.6 0.3 shard_map.85
  32.9 0.8 copy-done.7
  33.7 11.1 %all_to_all.25.refs_0_ = f32[8,4,512]{2,1,0:T(4,128)S(1)} all-to-all(f32[8,4,512]{2,1,0:T(4,128)S(1)} %get-tuple-element.21), channel_id=1, replica_groups=mesh['y'=4,'core'=2,'x'=4,'zh'=4,'zl'=4] {'y','core'}, dimensions={0} | all-to-all | bytes 131072 | tf_op jit(solution)/shard_map/all_to_all | solution.py:219
  44.8 0.6 shard_map.87
  45.4 12.2 %all-to-all-start.2 = ((bf16[16,4,512]{2,1,0:T(4,128)(2,1)}), bf16[16,4,512]{2,1,0:T(4,128)(2,1)S(1)}, u32[]{:S(2)}, u32[]{:S(2)}) async-start(bf16[16,4,512]{2,1,0:T(4,128)(2,1)} %shard_map.87), calls=%async_computation.2 | async-start | bytes 131072 | tf_op jit(solution)/shard_map/all_to_all | solution.py:219
  57.7 0.8 copy-done.1
  58.5 0.8 copy-done.3
  59.3 0.8 copy-done.5
  60.1 1.0 copy-done.2
  61.1 1.0 copy-done.4
  62.2 1.0 copy-done.6
  63.2 1.0 copy-done.8
  64.3 1.6 %shard_map.86 = (f32[4,256,512]{2,1,0:T(8,128)S(1)}, f32[4,256,512]{2,1,0:T(8,128)S(1)}) custom-call(s32[1]{0:T(128)} %bitcast.2.x_ref, s32[1]{0:T(128)} %bitcast.3.core_ref.refs_0_, f32[1,2048]{1,0:T(1,128)S(1)} %bitcast.14, f32[8,512]{1,0:T(8,128)S(1)} %get-tuple-element.17.scale_ref, bf16[4,128,512]{2,1,0:T(8,128)(2,1)S(1)} %copy-done.8, ...), custom_call_target="tpu_custom_call" | custom-call | bytes 134217728 | tf_op jit(solution)/shard_map/pallas_call | solution.py:207
  65.8 1.3 %copy-done.11 = f32[4,256,512]{2,1,0:T(8,128)} copy-done((f32[4,256,512]{2,1,0:T(8,128)}, f32[4,256,512]{2,1,0:T(8,128)S(1)}, u32[]{:S(2)}) %copy-start.11) | copy-done | bytes 2097176
  67.2 2.1 %all-to-all-done.2.refs_0_ = bf16[16,4,512]{2,1,0:T(4,128)(2,1)S(1)} async-done(((bf16[16,4,512]{2,1,0:T(4,128)(2,1)}), bf16[16,4,512]{2,1,0:T(4,128)(2,1)S(1)}, u32[]{:S(2)}, u32[]{:S(2)}) %all-to-all-start.2) | async-done | bytes 65568 | tf_op jit(solution)/shard_map/all_to_all | solution.py:219
  69.2 4.1 %collective-permute-start.3 = (f32[4,256,512]{2,1,0:T(8,128)}, f32[4,256,512]{2,1,0:T(8,128)S(1)}, u32[]{:S(2)}, u32[]{:S(2)}) collective-permute-start(f32[4,256,512]{2,1,0:T(8,128)} %copy-done.11), channel_id=1, source_target_pairs={{0,64},{64,0},{1,65},{65,1},{2,66},{66,2},{3,67},{67,3},{4,68},{68... | collective-permute-start | bytes 6291464 | tf_op jit(solution)/shard_map/ppermute | solution.py:224
  73.4 4.0 %collective-permute-done.3.got_ref = f32[4,256,512]{2,1,0:T(8,128)S(1)} collective-permute-done((f32[4,256,512]{2,1,0:T(8,128)}, f32[4,256,512]{2,1,0:T(8,128)S(1)}, u32[]{:S(2)}, u32[]{:S(2)}) %collective-permute-start.3) | collective-permute-done | bytes 2097184 | tf_op jit(solution)/shard_map/ppermute | solution.py:224
  77.3 0.2 shard_map.89
  77.6 22.2 %all_to_all.26 = bf16[16,80,512]{2,1,0:T(8,128)(2,1)S(1)} all-to-all(bf16[16,80,512]{2,1,0:T(8,128)(2,1)S(1)} %bitcast.11), channel_id=1, replica_groups=mesh['y'=4,'core'=2,'x'=4,'zh'=4,'zl'=4] {'y','x'}, dimensions={0} | all-to-all | bytes 2621440 | tf_op jit(solution)/shard_map/all_to_all | solution.py:219
  99.8 0.8 shard_map.90
  100.6 8.4 %all-to-all-start.4 = ((bf16[4,4,16,512]{3,2,1,0:T(8,128)(2,1)}), bf16[4,4,16,512]{3,2,1,0:T(8,128)(2,1)S(1)}, u32[]{:S(2)}, u32[]{:S(2)}) async-start(bf16[4,4,16,512]{3,2,1,0:T(8,128)(2,1)} %get-tuple-element.24), calls=%async_computation.4 | async-start | bytes 524288 | tf_op jit(solution)/shard_map/all_to_all | solution.py:219
  109.1 3.5 %collective-permute-start.4 = (bf16[4,4,16,512]{3,2,1,0:T(8,128)(2,1)S(1)}, bf16[4,4,16,512]{3,2,1,0:T(8,128)(2,1)S(1)}, u32[]{:S(2)}, u32[]{:S(2)}) collective-permute-start(bf16[4,4,16,512]{3,2,1,0:T(8,128)(2,1)S(1)} %get-tuple-element.27.refs_1_), channel_id=1, source_target_pairs={{0,64},{64,0},{1,65},{65,1},{2,66},{66,2},{3,67},{67,3},{4,68},{68... | collective-permute-start | bytes 786440 | tf_op jit(solution)/shard_map/ppermute | solution.py:224
  112.6 1.1 collective-permute-done.4.refs_2_
  113.7 1.0 shard_map.92
  114.7 10.4 %all-to-all-done.4.in_ref = bf16[4,4,16,512]{3,2,1,0:T(8,128)(2,1)S(1)} async-done(((bf16[4,4,16,512]{3,2,1,0:T(8,128)(2,1)}), bf16[4,4,16,512]{3,2,1,0:T(8,128)(2,1)S(1)}, u32[]{:S(2)}, u32[]{:S(2)}) %all-to-all-start.4) | async-done | bytes 262176 | tf_op jit(solution)/shard_map/all_to_all | solution.py:219
  125.2 0.7 shard_map.91
  (19 shorter events, 0.1 us)
Async XLA Ops:
  0.6 11.8 %copy-start = (bf16[128,2048]{1,0:T(8,128)(2,1)S(1)}, bf16[128,2048]{1,0:T(8,128)(2,1)}, u32[]{:S(2)}) copy-start(bf16[128,2048]{1,0:T(8,128)(2,1)} %refs_0_.1) | copy-start | bytes 1572868
  0.6 59.4 %copy-start.9 = (f32[2048]{0:T(1024)S(1)}, f32[2048]{0:T(1024)}, u32[]{:S(2)}) copy-start(f32[2048]{0:T(1024)} %param.6) | copy-start | bytes 24580
  3.4 29.2 %all-to-all-start = ((bf16[16,176,128]{2,1,0:T(8,128)(2,1)}), bf16[16,176,128]{2,1,0:T(8,128)(2,1)S(1)}, u32[]{:S(2)}, u32[]{:S(2)}) async-start(bf16[16,176,128]{2,1,0:T(8,128)(2,1)} %bitcast.17), calls=%async_computation | async-start | bytes 1441792 | tf_op jit(solution)/shard_map/all_to_all | solution.py:219
  12.5 45.2 %collective-permute-start.1 = (bf16[128,2048]{1,0:T(8,128)(2,1)S(1)}, bf16[128,2048]{1,0:T(8,128)(2,1)S(1)}, u32[]{:S(2)}, u32[]{:S(2)}) collective-permute-start(bf16[128,2048]{1,0:T(8,128)(2,1)S(1)} %copy-done), channel_id=1, source_target_pairs={{0,32},{16,48},{32,0},{48,16},{1,33},{17,49},{33,1},{49,17},{2,34}... | collective-permute-start | bytes 1572872 | tf_op jit(solution)/shard_map/ppermute | solution.py:224
  17.2 41.2 %collective-permute-start = (bf16[128,2048]{1,0:T(8,128)(2,1)S(1)}, bf16[128,2048]{1,0:T(8,128)(2,1)S(1)}, u32[]{:S(2)}, u32[]{:S(2)}) collective-permute-start(bf16[128,2048]{1,0:T(8,128)(2,1)S(1)} %copy-done), channel_id=1, source_target_pairs={{0,16},{16,32},{32,48},{48,0},{1,17},{17,33},{33,49},{49,1},{2,18}... | collective-permute-start | bytes 1572872 | tf_op jit(solution)/shard_map/ppermute | solution.py:224
  19.4 39.8 %collective-permute-start.2 = (bf16[128,2048]{1,0:T(8,128)(2,1)S(1)}, bf16[128,2048]{1,0:T(8,128)(2,1)S(1)}, u32[]{:S(2)}, u32[]{:S(2)}) collective-permute-start(bf16[128,2048]{1,0:T(8,128)(2,1)S(1)} %copy-done), channel_id=1, source_target_pairs={{0,48},{16,0},{32,16},{48,32},{1,49},{17,1},{33,17},{49,33},{2,50}... | collective-permute-start | bytes 1572872 | tf_op jit(solution)/shard_map/ppermute | solution.py:224
  32.9 0.8 copy-start.7
  45.4 23.8 %all-to-all-start.2 = ((bf16[16,4,512]{2,1,0:T(4,128)(2,1)}), bf16[16,4,512]{2,1,0:T(4,128)(2,1)S(1)}, u32[]{:S(2)}, u32[]{:S(2)}) async-start(bf16[16,4,512]{2,1,0:T(4,128)(2,1)} %shard_map.87), calls=%async_computation.2 | async-start | bytes 131072 | tf_op jit(solution)/shard_map/all_to_all | solution.py:219
  57.7 0.8 copy-start.1
  58.5 0.8 copy-start.3
  59.3 0.8 copy-start.5
  60.1 1.0 copy-start.2
  61.1 1.0 copy-start.4
  62.2 1.0 copy-start.6
  63.2 1.0 copy-start.8
  65.8 1.3 %copy-start.11 = (f32[4,256,512]{2,1,0:T(8,128)}, f32[4,256,512]{2,1,0:T(8,128)S(1)}, u32[]{:S(2)}) copy-start(f32[4,256,512]{2,1,0:T(8,128)S(1)} %get-tuple-element.22) | copy-start | bytes 6291460
  69.2 8.1 %collective-permute-start.3 = (f32[4,256,512]{2,1,0:T(8,128)}, f32[4,256,512]{2,1,0:T(8,128)S(1)}, u32[]{:S(2)}, u32[]{:S(2)}) collective-permute-start(f32[4,256,512]{2,1,0:T(8,128)} %copy-done.11), channel_id=1, source_target_pairs={{0,64},{64,0},{1,65},{65,1},{2,66},{66,2},{3,67},{67,3},{4,68},{68... | collective-permute-start | bytes 6291464 | tf_op jit(solution)/shard_map/ppermute | solution.py:224
  77.5 47.6 %copy-start.10 = (s32[128]{0:T(128)S(1)}, s32[128]{0:T(128)}, u32[]{:S(2)}) copy-start(s32[128]{0:T(128)} %param.9) | copy-start | bytes 1540
  100.6 24.5 %all-to-all-start.4 = ((bf16[4,4,16,512]{3,2,1,0:T(8,128)(2,1)}), bf16[4,4,16,512]{3,2,1,0:T(8,128)(2,1)S(1)}, u32[]{:S(2)}, u32[]{:S(2)}) async-start(bf16[4,4,16,512]{3,2,1,0:T(8,128)(2,1)} %get-tuple-element.24), calls=%async_computation.4 | async-start | bytes 524288 | tf_op jit(solution)/shard_map/all_to_all | solution.py:219
  109.1 4.7 %collective-permute-start.4 = (bf16[4,4,16,512]{3,2,1,0:T(8,128)(2,1)S(1)}, bf16[4,4,16,512]{3,2,1,0:T(8,128)(2,1)S(1)}, u32[]{:S(2)}, u32[]{:S(2)}) collective-permute-start(bf16[4,4,16,512]{3,2,1,0:T(8,128)(2,1)S(1)} %get-tuple-element.27.refs_1_), channel_id=1, source_target_pairs={{0,64},{64,0},{1,65},{65,1},{2,66},{66,2},{3,67},{67,3},{4,68},{68... | collective-permute-start | bytes 786440 | tf_op jit(solution)/shard_map/ppermute | solution.py:224

commit v4 on v3

--- a/solution.py
+++ b/solution.py
@@ -115,34 +115,57 @@
             out_ref[to, j * few : (j + 1) * few] = total
 
 
-def multiply(x_ref, core_ref, gain_ref, scale_ref, right_ref, *refs):
-    own_ref, other_ref, total_ref = refs[-3:]
-    lefts = refs[:-3]
-    n_x, n_y = len(lefts), own_ref.shape[0]
+def multiply(x_ref, core_ref, gain_in, scale_in, right_in, *refs):
+    lefts, refs = refs[:-10], refs[-10:]
+    own_out, other_out, gain_ref, scale_ref, right_ref, left_ref, total_ref, half_ref, in_sems, out_sems = refs
+    n_x, n_y = len(lefts), own_out.shape[0]
     toks, width = lefts[0].shape
     tile = width // n_y
-    columns = []
+    pairs = [(gain_in, gain_ref), (scale_in, scale_ref), (right_in, right_ref)]
+    pairs += [(left, left_ref.at[j]) for j, left in enumerate(lefts)]
+    copies = [pltpu.make_async_copy(a, b, in_sems.at[i]) for i, (a, b) in enumerate(pairs)]
+    for copy in copies:
+        copy.start()
+    for copy in copies:
+        copy.wait()
+    columns, right = [], []
     for j in range(n_x):
         x = lax.rem(x_ref[0] + n_x - j, n_x)
-        columns.append(column(scale_ref[:1, pl.ds(pl.multiple_of(x * LANES, LANES), LANES)]))
+        row = scale_ref[:1, pl.ds(pl.multiple_of(x * LANES, LANES), LANES)]
+        columns.append(jnp.concatenate([column(row)] * (tile // LANES), axis=1))
+        right.append(right_ref[x])
+    right = jnp.concatenate(right, axis=0)
+    rows = tile // 2
+    own_rows = pl.ds(pl.multiple_of(core_ref[0] * rows, rows), rows)
+    other_rows = pl.ds(pl.multiple_of((1 - core_ref[0]) * rows, rows), rows)
+    sent = []
     for y in range(n_y):
-        at = slice(y * tile, (y + 1) * tile)
-        normed, right = [], []
-        for j, left_ref in enumerate(lefts):
-            x = lax.rem(x_ref[0] + n_x - j, n_x)
-            scales = jnp.concatenate([columns[j]] * (tile // LANES), axis=1)
-            left = left_ref[:, at].astype(jnp.float32) * scales * gain_ref[:, at]
+        at, slot = slice(y * tile, (y + 1) * tile), y % 2
+        normed = []
+        for j in range(n_x):
+            left = left_ref[j, :, at].astype(jnp.float32) * columns[j] * gain_ref[:, at]
             normed.append(left.astype(jnp.bfloat16))
-            right.append(right_ref[x])
-        total_ref[...] = lax.dot_general(
+        if y >= 2:
+            for copy in sent[y - 2]:
+                copy.wait()
+        total_ref[slot] = lax.dot_general(
             jnp.concatenate(normed, axis=0),
-            jnp.concatenate(right, axis=0),
+            right,
             (((0,), (0,)), ((), ())),
             preferred_element_type=jnp.float32,
         )
-        rows = tile // 2
-        for out_ref, core in ((own_ref, core_ref[0]), (other_ref, 1 - core_ref[0])):
-            out_ref[y] = total_ref[pl.ds(pl.multiple_of(core * rows, rows), rows), :]
+        half_ref[slot] = total_ref[slot, other_rows, :].astype(jnp.bfloat16)
+        sent.append(
+            (
+                pltpu.make_async_copy(total_ref.at[slot, own_rows], own_out.at[y], out_sems.at[slot, 0]),
+                pltpu.make_async_copy(half_ref.at[slot], other_out.at[y], out_sems.at[slot, 1]),
+            )
+        )
+        for copy in sent[y]:
+            copy.start()
+    for pair in sent[-2:]:
+        for copy in pair:
+            copy.wait()
 
 
 def add_cores(own_ref, got_ref, union_ref, out_ref):
@@ -151,7 +174,7 @@
     for y in range(n_y):
         for x in range(n_x):
             at = slice(x * rows, (x + 1) * rows)
-            out_ref[y, x, :rows] = (own_ref[y, at] + got_ref[y, at]).astype(jnp.bfloat16)
+            out_ref[y, x, :rows] = (own_ref[y, at] + got_ref[y, at].astype(jnp.float32)).astype(jnp.bfloat16)
             out_ref[y, x, rows:] = union_ref[0]
 
 
@@ -277,14 +300,25 @@
     )
 
     half = shape((n_y, width // (n_y * n_core), cols), f32)
-    own, other = call(
+    anywhere = pl.BlockSpec(memory_space=pl.ANY)
+    own, other = pl.pallas_call(
         multiply,
-        (half, half),
-        (at_x, at_core, gain, scale, right, *left),
-        2,
-        [pltpu.VMEM((width // n_y, cols), f32)],
-        cost=128 * 1024 * 1024,
-    )
+        out_shape=(half, shape(half.shape, bf16)),
+        in_specs=[SMEM, SMEM] + [anywhere] * (3 + n_x),
+        out_specs=(anywhere, anywhere),
+        scratch_shapes=[
+            pltpu.VMEM(gain.shape, f32),
+            pltpu.VMEM(scale.shape, f32),
+            pltpu.VMEM(right.shape, bf16),
+            pltpu.VMEM((n_x, toks, width), bf16),
+            pltpu.VMEM((2, width // n_y, cols), f32),
+            pltpu.VMEM((2, width // (n_y * n_core), cols), bf16),
+            pltpu.SemaphoreType.DMA((3 + n_x,)),
+            pltpu.SemaphoreType.DMA((2, 2)),
+        ],
+        cost_estimate=pl.CostEstimate(flops=0, bytes_accessed=128 * 1024 * 1024, transcendentals=0),
+        compiler_params=pltpu.CompilerParams(vmem_limit_bytes=60 * 1024 * 1024),
+    )(at_x, at_core, gain, scale, right, *left)
     other, outliers = lax.optimization_barrier((other, outliers))
     got = shift(other, "core", 1)
     rows = width // (n_y * n_core * n_x * n_zh)

time: 128 us -> 125 us (0.977)
  local copies, waits for them, and re-layouts: 8.71 us -> 3.5 us
  Pallas kernels: 8.06 us -> 11.8 us
  starting transfers between devices: 48.6 us -> 45.5 us
  waiting for transfers between devices: 26.4 us -> 27.9 us
    pallas_call x0 -> x1, Pallas kernels: none -> 5.29 us  [per_device(): pl.pallas_call(multiply, out_shape=(half, shape(half.shape, bf16)), in_sp...]
    unnamed x24 -> x16, local copies, waits for them, and re-layouts: 8.71 us -> 3.5 us
    all_to_all x3, starting transfers between devices: 29.7 us -> 26.6 us  [exchange(): return lax.all_to_all(v, axes, split_axis=0, concat_axis=0, tiled=True)]
    all_to_all x3, waiting for transfers between devices: 21.3 us -> 24.3 us  [exchange(): return lax.all_to_all(v, axes, split_axis=0, concat_axis=0, tiled=True)]
    pallas_call x8 -> x7, Pallas kernels: 5.32 us -> 3.74 us  [call(): pl.pallas_call(body, out_shape=out_shape, in_specs=[SMEM] * scalars + [VM...]
    ppermute x5, waiting for transfers between devices: 5.1 us -> 3.6 us  [shift(): return lax.ppermute(v, axis, [(i, (i + by) % count) for i in range(count)])]
  transfers between devices with their start and end apart: 8 -> 8, of which waited for: 5 -> 5; matrix products, arithmetic and copies ran while one was open for 0% -> 0% of each run, Pallas kernels for 3% -> 6%
where the time goes in v4:
time: 125 us; the launch traced here: 123 us
  starting transfers between devices  45.5 us (36%)
  blocking collectives  33.3 us (27%)
  waiting for transfers between devices  27.9 us (22%)
  Pallas kernels  11.8 us (9%)
  local copies, waits for them, and re-layouts  3.5 us (3%)
    all_to_all x2, blocking collectives, exchange(): return lax.all_to_all(v, axes, split_axis=0, concat_axis=0, tiled=True)  33.3 us
    all_to_all x3, starting transfers between devices, exchange(): return lax.all_to_all(v, axes, split_axis=0, concat_axis=0, tiled=True)  26.6 us
    all_to_all x3, waiting for transfers between devices, exchange(): return lax.all_to_all(v, axes, split_axis=0, concat_axis=0, tiled=True)  24.3 us
    ppermute x5, starting transfers between devices, shift(): return lax.ppermute(v, axis, [(i, (i + by) % count) for i in range(count)])  18.9 us
    pallas_call x1, Pallas kernels, per_device(): pl.pallas_call(multiply, out_shape=(half, shape(half.shape, bf16)), in_sp...  5.29 us
    pallas_call x7, Pallas kernels, call(): pl.pallas_call(body, out_shape=out_shape, in_specs=[SMEM] * scalars + [VM...  3.74 us
    ppermute x5, waiting for transfers between devices, shift(): return lax.ppermute(v, axis, [(i, (i + by) % count) for i in range(count)])  3.6 us
    unnamed x16, local copies, waits for them, and re-layouts  3.5 us
  transfers between devices with their start and end apart: 8, of which 5 were waited for; matrix products, arithmetic and copies ran while one was open for 0% of the time, Pallas kernels for 6%

profile of v4, /device:TPU:1, one launch (start us, length us, event | category | flops | bytes accessed | tf_op | source)
XLA Modules:
  0.0 122.9 jit_solution(15805150213516956775)
XLA Ops:
  0.6 0.0 copy-start.4
  0.6 2.7 %shard_map.84 = bf16[4,4,176,128]{3,2,1,0:T(8,128)(2,1)} custom-call(s32[1]{0:T(128)} %bitcast.5.zl_ref.refs_0_, bf16[128,2048]{1,0:T(8,128)(2,1)} %refs_0_.1, bf16[128,256]{1,0:T(8,128)(2,1)} %key_in.1, bf16[128,256]{1,0:T(8,128)(2,1)} %value_in.1, s32[1,128]{1,0:T(1,128)} %bitcast.13, f32[1,2048]{1,0:T(1,128)} %bitcast.16), custom_call_target="tpu_custom_call" | custom-call | tf_op jit(solution)/shard_map/pallas_call | solution.py:265
  3.4 9.0 %all-to-all-start = ((bf16[16,176,128]{2,1,0:T(8,128)(2,1)}), bf16[16,176,128]{2,1,0:T(8,128)(2,1)S(1)}, u32[]{:S(2)}, u32[]{:S(2)}) async-start(bf16[16,176,128]{2,1,0:T(8,128)(2,1)} %bitcast.15), calls=%async_computation | async-start | bytes 1441792 | tf_op jit(solution)/shard_map/all_to_all | solution.py:242
  12.4 4.8 %collective-permute-start.1 = (bf16[128,2048]{1,0:T(8,128)(2,1)S(1)}, bf16[128,2048]{1,0:T(8,128)(2,1)S(1)}, u32[]{:S(2)}, u32[]{:S(2)}) collective-permute-start(bf16[128,2048]{1,0:T(8,128)(2,1)S(1)} %copy-done.4), channel_id=1, source_target_pairs={{0,32},{16,48},{32,0},{48,16},{1,33},{17,49},{33,1},{49,17},{2,34}... | collective-permute-start | bytes 1572872 | tf_op jit(solution)/shard_map/ppermute | solution.py:247
  17.2 2.2 %collective-permute-start = (bf16[128,2048]{1,0:T(8,128)(2,1)S(1)}, bf16[128,2048]{1,0:T(8,128)(2,1)S(1)}, u32[]{:S(2)}, u32[]{:S(2)}) collective-permute-start(bf16[128,2048]{1,0:T(8,128)(2,1)S(1)} %copy-done.4), channel_id=1, source_target_pairs={{0,16},{16,32},{32,48},{48,0},{1,17},{17,33},{33,49},{49,1},{2,18}... | collective-permute-start | bytes 1572872 | tf_op jit(solution)/shard_map/ppermute | solution.py:247
  19.4 4.3 %collective-permute-start.2 = (bf16[128,2048]{1,0:T(8,128)(2,1)S(1)}, bf16[128,2048]{1,0:T(8,128)(2,1)S(1)}, u32[]{:S(2)}, u32[]{:S(2)}) collective-permute-start(bf16[128,2048]{1,0:T(8,128)(2,1)S(1)} %copy-done.4), channel_id=1, source_target_pairs={{0,48},{16,0},{32,16},{48,32},{1,49},{17,1},{33,17},{49,33},{2,50}... | collective-permute-start | bytes 1572872 | tf_op jit(solution)/shard_map/ppermute | solution.py:247
  23.7 8.8 %all-to-all-done = bf16[16,176,128]{2,1,0:T(8,128)(2,1)S(1)} async-done(((bf16[16,176,128]{2,1,0:T(8,128)(2,1)}), bf16[16,176,128]{2,1,0:T(8,128)(2,1)S(1)}, u32[]{:S(2)}, u32[]{:S(2)}) %all-to-all-start) | async-done | bytes 720928 | tf_op jit(solution)/shard_map/all_to_all | solution.py:242
  32.6 0.3 shard_map.85
  32.9 0.0 copy-start.1
  32.9 0.8 copy-done.1
  33.7 11.1 %all_to_all.25.refs_0_ = f32[8,4,512]{2,1,0:T(4,128)S(1)} all-to-all(f32[8,4,512]{2,1,0:T(4,128)S(1)} %get-tuple-element.21), channel_id=1, replica_groups=mesh['y'=4,'core'=2,'x'=4,'zh'=4,'zl'=4] {'y','core'}, dimensions={0} | all-to-all | bytes 131072 | tf_op jit(solution)/shard_map/all_to_all | solution.py:242
  44.8 0.6 shard_map.87
  45.4 12.2 %all-to-all-start.2 = ((bf16[16,4,512]{2,1,0:T(4,128)(2,1)}), bf16[16,4,512]{2,1,0:T(4,128)(2,1)S(1)}, u32[]{:S(2)}, u32[]{:S(2)}) async-start(bf16[16,4,512]{2,1,0:T(4,128)(2,1)} %shard_map.87), calls=%async_computation.2 | async-start | bytes 131072 | tf_op jit(solution)/shard_map/all_to_all | solution.py:242
  57.7 0.0 copy-start.6
  57.7 0.0 collective-permute-done.2.refs_3_
  57.7 0.7 copy-done.5
  58.4 0.2 copy-done.6
  58.6 0.2 copy-done.7
  58.8 5.3 %shard_map.86 = (f32[4,256,512]{2,1,0:T(8,128)}, bf16[4,256,512]{2,1,0:T(8,128)(2,1)}) custom-call(s32[1]{0:T(128)} %bitcast.2.x_ref, s32[1]{0:T(128)} %bitcast.3.core_ref.refs_0_, f32[1,2048]{1,0:T(1,128)} %bitcast.17, f32[8,512]{1,0:T(8,128)} %copy-done.2, bf16[4,128,512]{2,1,0:T(8,128)(2,1)} %copy-done.1, bf16[128,2048]{1,0:T(8,128)(2,1)} %refs_0_.1, ...), custom_call_target="tpu_custom_call" | custom-call | bytes 134217728 | tf_op jit(solution)/shard_map/pallas_call | solution.py:304
  64.1 5.1 %all-to-all-done.2.refs_0_ = bf16[16,4,512]{2,1,0:T(4,128)(2,1)S(1)} async-done(((bf16[16,4,512]{2,1,0:T(4,128)(2,1)}), bf16[16,4,512]{2,1,0:T(4,128)(2,1)S(1)}, u32[]{:S(2)}, u32[]{:S(2)}) %all-to-all-start.2) | async-done | bytes 65568 | tf_op jit(solution)/shard_map/all_to_all | solution.py:242
  69.2 4.1 %collective-permute-start.3 = (bf16[4,256,512]{2,1,0:T(8,128)(2,1)}, bf16[4,256,512]{2,1,0:T(8,128)(2,1)S(1)}, u32[]{:S(2)}, u32[]{:S(2)}) collective-permute-start(bf16[4,256,512]{2,1,0:T(8,128)(2,1)} %get-tuple-element.22), channel_id=1, source_target_pairs={{0,64},{64,0},{1,65},{65,1},{2,66},{66,2},{3,67},{67,3},{4,68},{68... | collective-permute-start | bytes 3145736 | tf_op jit(solution)/shard_map/ppermute | solution.py:247
  73.4 2.5 %collective-permute-done.3.got_ref = bf16[4,256,512]{2,1,0:T(8,128)(2,1)S(1)} collective-permute-done((bf16[4,256,512]{2,1,0:T(8,128)(2,1)}, bf16[4,256,512]{2,1,0:T(8,128)(2,1)S(1)}, u32[]{:S(2)}, u32[]{:S(2)}) %collective-permute-start.3) | collective-permute-done | bytes 1048608 | tf_op jit(solution)/shard_map/ppermute | solution.py:247
  75.9 1.6 %copy-done = f32[4,256,512]{2,1,0:T(8,128)S(1)} copy-done((f32[4,256,512]{2,1,0:T(8,128)S(1)}, f32[4,256,512]{2,1,0:T(8,128)}, u32[]{:S(2)}) %copy-start) | copy-done | bytes 2097176
  77.4 0.2 shard_map.89
  77.6 22.2 %all_to_all.26 = bf16[16,80,512]{2,1,0:T(8,128)(2,1)S(1)} all-to-all(bf16[16,80,512]{2,1,0:T(8,128)(2,1)S(1)} %bitcast.11), channel_id=1, replica_groups=mesh['y'=4,'core'=2,'x'=4,'zh'=4,'zl'=4] {'y','x'}, dimensions={0} | all-to-all | bytes 2621440 | tf_op jit(solution)/shard_map/all_to_all | solution.py:242
  99.9 0.8 shard_map.90
  100.7 5.3 %all-to-all-start.4 = ((bf16[4,4,16,512]{3,2,1,0:T(8,128)(2,1)}), bf16[4,4,16,512]{3,2,1,0:T(8,128)(2,1)S(1)}, u32[]{:S(2)}, u32[]{:S(2)}) async-start(bf16[4,4,16,512]{3,2,1,0:T(8,128)(2,1)} %get-tuple-element.24), calls=%async_computation.4 | async-start | bytes 524288 | tf_op jit(solution)/shard_map/all_to_all | solution.py:242
  106.0 3.5 %collective-permute-start.4 = (bf16[4,4,16,512]{3,2,1,0:T(8,128)(2,1)S(1)}, bf16[4,4,16,512]{3,2,1,0:T(8,128)(2,1)S(1)}, u32[]{:S(2)}, u32[]{:S(2)}) collective-permute-start(bf16[4,4,16,512]{3,2,1,0:T(8,128)(2,1)S(1)} %get-tuple-element.27.refs_1_), channel_id=1, source_target_pairs={{0,64},{64,0},{1,65},{65,1},{2,66},{66,2},{3,67},{67,3},{4,68},{68... | collective-permute-start | bytes 786440 | tf_op jit(solution)/shard_map/ppermute | solution.py:247
  109.6 1.1 collective-permute-done.4.refs_2_
  110.7 1.0 shard_map.92
  111.7 10.4 %all-to-all-done.4.in_ref = bf16[4,4,16,512]{3,2,1,0:T(8,128)(2,1)S(1)} async-done(((bf16[4,4,16,512]{3,2,1,0:T(8,128)(2,1)}), bf16[4,4,16,512]{3,2,1,0:T(8,128)(2,1)S(1)}, u32[]{:S(2)}, u32[]{:S(2)}) %all-to-all-start.4) | async-done | bytes 262176 | tf_op jit(solution)/shard_map/all_to_all | solution.py:242
  122.2 0.7 shard_map.91
  (11 shorter events, 0.0 us)
Async XLA Ops:
  0.6 11.8 %copy-start.4 = (bf16[128,2048]{1,0:T(8,128)(2,1)S(1)}, bf16[128,2048]{1,0:T(8,128)(2,1)}, u32[]{:S(2)}) copy-start(bf16[128,2048]{1,0:T(8,128)(2,1)} %refs_0_.1) | copy-start | bytes 1572868
  3.4 29.2 %all-to-all-start = ((bf16[16,176,128]{2,1,0:T(8,128)(2,1)}), bf16[16,176,128]{2,1,0:T(8,128)(2,1)S(1)}, u32[]{:S(2)}, u32[]{:S(2)}) async-start(bf16[16,176,128]{2,1,0:T(8,128)(2,1)} %bitcast.15), calls=%async_computation | async-start | bytes 1441792 | tf_op jit(solution)/shard_map/all_to_all | solution.py:242
  12.4 45.2 %collective-permute-start.1 = (bf16[128,2048]{1,0:T(8,128)(2,1)S(1)}, bf16[128,2048]{1,0:T(8,128)(2,1)S(1)}, u32[]{:S(2)}, u32[]{:S(2)}) collective-permute-start(bf16[128,2048]{1,0:T(8,128)(2,1)S(1)} %copy-done.4), channel_id=1, source_target_pairs={{0,32},{16,48},{32,0},{48,16},{1,33},{17,49},{33,1},{49,17},{2,34}... | collective-permute-start | bytes 1572872 | tf_op jit(solution)/shard_map/ppermute | solution.py:247
  17.2 40.4 %collective-permute-start = (bf16[128,2048]{1,0:T(8,128)(2,1)S(1)}, bf16[128,2048]{1,0:T(8,128)(2,1)S(1)}, u32[]{:S(2)}, u32[]{:S(2)}) collective-permute-start(bf16[128,2048]{1,0:T(8,128)(2,1)S(1)} %copy-done.4), channel_id=1, source_target_pairs={{0,16},{16,32},{32,48},{48,0},{1,17},{17,33},{33,49},{49,1},{2,18}... | collective-permute-start | bytes 1572872 | tf_op jit(solution)/shard_map/ppermute | solution.py:247
  19.4 38.3 %collective-permute-start.2 = (bf16[128,2048]{1,0:T(8,128)(2,1)S(1)}, bf16[128,2048]{1,0:T(8,128)(2,1)S(1)}, u32[]{:S(2)}, u32[]{:S(2)}) collective-permute-start(bf16[128,2048]{1,0:T(8,128)(2,1)S(1)} %copy-done.4), channel_id=1, source_target_pairs={{0,48},{16,0},{32,16},{48,32},{1,49},{17,1},{33,17},{49,33},{2,50}... | collective-permute-start | bytes 1572872 | tf_op jit(solution)/shard_map/ppermute | solution.py:247
  32.9 0.8 copy-start.1
  33.7 11.1 %copy-start.2 = (f32[8,512]{1,0:T(8,128)}, f32[8,512]{1,0:T(8,128)S(1)}, u32[]{:S(2)}) copy-start(f32[8,512]{1,0:T(8,128)S(1)} %get-tuple-element.17.scale_in) | copy-start | bytes 49156
  45.4 23.8 %all-to-all-start.2 = ((bf16[16,4,512]{2,1,0:T(4,128)(2,1)}), bf16[16,4,512]{2,1,0:T(4,128)(2,1)S(1)}, u32[]{:S(2)}, u32[]{:S(2)}) async-start(bf16[16,4,512]{2,1,0:T(4,128)(2,1)} %shard_map.87), calls=%async_computation.2 | async-start | bytes 131072 | tf_op jit(solution)/shard_map/all_to_all | solution.py:242
  57.7 0.8 copy-start.5
  57.7 0.9 copy-start.6
  57.7 1.1 copy-start.7
  69.2 6.6 %collective-permute-start.3 = (bf16[4,256,512]{2,1,0:T(8,128)(2,1)}, bf16[4,256,512]{2,1,0:T(8,128)(2,1)S(1)}, u32[]{:S(2)}, u32[]{:S(2)}) collective-permute-start(bf16[4,256,512]{2,1,0:T(8,128)(2,1)} %get-tuple-element.22), channel_id=1, source_target_pairs={{0,64},{64,0},{1,65},{65,1},{2,66},{66,2},{3,67},{67,3},{4,68},{68... | collective-permute-start | bytes 3145736 | tf_op jit(solution)/shard_map/ppermute | solution.py:247
  75.8 1.6 %copy-start = (f32[4,256,512]{2,1,0:T(8,128)S(1)}, f32[4,256,512]{2,1,0:T(8,128)}, u32[]{:S(2)}) copy-start(f32[4,256,512]{2,1,0:T(8,128)} %get-tuple-element.19.own_ref) | copy-start | bytes 6291460
  99.9 22.3 %copy-start.3 = (s32[128]{0:T(128)S(1)}, s32[128]{0:T(128)}, u32[]{:S(2)}) copy-start(s32[128]{0:T(128)} %param.9) | copy-start | bytes 1540
  100.7 21.5 %all-to-all-start.4 = ((bf16[4,4,16,512]{3,2,1,0:T(8,128)(2,1)}), bf16[4,4,16,512]{3,2,1,0:T(8,128)(2,1)S(1)}, u32[]{:S(2)}, u32[]{:S(2)}) async-start(bf16[4,4,16,512]{3,2,1,0:T(8,128)(2,1)} %get-tuple-element.24), calls=%async_computation.4 | async-start | bytes 524288 | tf_op jit(solution)/shard_map/all_to_all | solution.py:242
  106.0 4.7 %collective-permute-start.4 = (bf16[4,4,16,512]{3,2,1,0:T(8,128)(2,1)S(1)}, bf16[4,4,16,512]{3,2,1,0:T(8,128)(2,1)S(1)}, u32[]{:S(2)}, u32[]{:S(2)}) collective-permute-start(bf16[4,4,16,512]{3,2,1,0:T(8,128)(2,1)S(1)} %get-tuple-element.27.refs_1_), channel_id=1, source_target_pairs={{0,64},{64,0},{1,65},{65,1},{2,66},{66,2},{3,67},{67,3},{4,68},{68... | collective-permute-start | bytes 786440 | tf_op jit(solution)/shard_map/ppermute | solution.py:247

commit v5 on v4

--- a/solution.py
+++ b/solution.py
@@ -122,9 +122,17 @@
     toks, width = lefts[0].shape
     tile = width // n_y
     pairs = [(gain_in, gain_ref), (scale_in, scale_ref), (right_in, right_ref)]
-    pairs += [(left, left_ref.at[j]) for j, left in enumerate(lefts)]
-    copies = [pltpu.make_async_copy(a, b, in_sems.at[i]) for i, (a, b) in enumerate(pairs)]
-    for copy in copies:
+    copies = [pltpu.make_async_copy(a, b, in_sems.at[n_y, i]) for i, (a, b) in enumerate(pairs)]
+    quarters = []
+    for y in range(n_y):
+        at = pl.ds(y * tile, tile)
+        quarters.append(
+            [
+                pltpu.make_async_copy(left.at[:, at], left_ref.at[j, :, at], in_sems.at[y, j])
+                for j, left in enumerate(lefts)
+            ]
+        )
+    for copy in copies + sum(quarters, []):
         copy.start()
     for copy in copies:
         copy.wait()
@@ -141,6 +149,8 @@
     sent = []
     for y in range(n_y):
         at, slot = slice(y * tile, (y + 1) * tile), y % 2
+        for copy in quarters[y]:
+            copy.wait()
         normed = []
         for j in range(n_x):
             left = left_ref[j, :, at].astype(jnp.float32) * columns[j] * gain_ref[:, at]
@@ -168,6 +178,15 @@
             copy.wait()
 
 
+def fetch(source, out_ref, sems):
+    count = out_ref.shape[0]
+    copies = [pltpu.make_async_copy(source.at[y], out_ref.at[y], sems.at[y]) for y in range(count)]
+    for copy in copies:
+        copy.start()
+    for copy in copies:
+        copy.wait()
+
+
 def add_cores(own_ref, got_ref, union_ref, out_ref):
     n_y, n_x, rows, _ = out_ref.shape
     rows -= union_ref.shape[1]
@@ -313,7 +332,7 @@
             pltpu.VMEM((n_x, toks, width), bf16),
             pltpu.VMEM((2, width // n_y, cols), f32),
             pltpu.VMEM((2, width // (n_y * n_core), cols), bf16),
-            pltpu.SemaphoreType.DMA((3 + n_x,)),
+            pltpu.SemaphoreType.DMA((n_y + 1, n_x)),
             pltpu.SemaphoreType.DMA((2, 2)),
         ],
         cost_estimate=pl.CostEstimate(flops=0, bytes_accessed=128 * 1024 * 1024, transcendentals=0),
@@ -321,6 +340,15 @@
     )(at_x, at_core, gain, scale, right, *left)
     other, outliers = lax.optimization_barrier((other, outliers))
     got = shift(other, "core", 1)
+    own = pl.pallas_call(
+        fetch,
+        out_shape=half,
+        in_specs=[anywhere],
+        out_specs=VMEM,
+        scratch_shapes=[pltpu.SemaphoreType.DMA((n_y,))],
+        cost_estimate=pl.CostEstimate(flops=0, bytes_accessed=16 * 1024 * 1024, transcendentals=0),
+        compiler_params=PARAMS,
+    )(own)
     rows = width // (n_y * n_core * n_x * n_zh)
     lines = n_zh * rows + n_zl * few
     pieces = call(add_cores, shape((n_y, n_x, lines, cols), bf16), (own, got, outliers))

time: 125 us -> 123 us (0.984)
  waiting for transfers between devices: 27.9 us -> 26.6 us
    ppermute x5, waiting for transfers between devices: 3.6 us -> 1.82 us  [shift(): return lax.ppermute(v, axis, [(i, (i + by) % count) for i in range(count)])]
where the time goes in v5:
time: 123 us; the launch traced here: 121 us
  starting transfers between devices  45 us (37%)
  blocking collectives  33.3 us (27%)
  waiting for transfers between devices  26.6 us (22%)
  Pallas kernels  11.5 us (9%)
  local copies, waits for them, and re-layouts  3.5 us (3%)
    all_to_all x2, blocking collectives, exchange(): return lax.all_to_all(v, axes, split_axis=0, concat_axis=0, tiled=True)  33.3 us
    all_to_all x3, starting transfers between devices, exchange(): return lax.all_to_all(v, axes, split_axis=0, concat_axis=0, tiled=True)  26.1 us
    all_to_all x3, waiting for transfers between devices, exchange(): return lax.all_to_all(v, axes, split_axis=0, concat_axis=0, tiled=True)  24.8 us
    ppermute x5, starting transfers between devices, shift(): return lax.ppermute(v, axis, [(i, (i + by) % count) for i in range(count)])  18.9 us
    pallas_call x1, Pallas kernels, per_device(): pl.pallas_call(multiply, out_shape=(half, shape(half.shape, bf16)), in_sp...  4.83 us
    pallas_call x7, Pallas kernels, call(): pl.pallas_call(body, out_shape=out_shape, in_specs=[SMEM] * scalars + [VM...  3.74 us
    unnamed x16, local copies, waits for them, and re-layouts  3.5 us
    pallas_call x1, Pallas kernels, per_device(): pl.pallas_call(prepare, out_shape=shape((n_x, n_zl, toks + per + AUX, LAN...  2.75 us
  transfers between devices with their start and end apart: 8, of which 5 were waited for; matrix products, arithmetic and copies ran while one was open for 0% of the time, Pallas kernels for 6%

profile of v5, /device:TPU:1, one launch (start us, length us, event | category | flops | bytes accessed | tf_op | source)
XLA Modules:
  0.0 120.8 jit_solution(17797806489728883881)
XLA Ops:
  0.6 0.0 copy-start.4
  0.6 2.7 %shard_map.84 = bf16[4,4,176,128]{3,2,1,0:T(8,128)(2,1)} custom-call(s32[1]{0:T(128)} %bitcast.5.zl_ref.refs_0_, bf16[128,2048]{1,0:T(8,128)(2,1)} %refs_0_.1, bf16[128,256]{1,0:T(8,128)(2,1)} %key_in.1, bf16[128,256]{1,0:T(8,128)(2,1)} %value_in.1, s32[1,128]{1,0:T(1,128)} %bitcast.13, f32[1,2048]{1,0:T(1,128)} %bitcast.16), custom_call_target="tpu_custom_call" | custom-call | tf_op jit(solution)/shard_map/pallas_call | solution.py:284
  3.4 9.0 %all-to-all-start = ((bf16[16,176,128]{2,1,0:T(8,128)(2,1)}), bf16[16,176,128]{2,1,0:T(8,128)(2,1)S(1)}, u32[]{:S(2)}, u32[]{:S(2)}) async-start(bf16[16,176,128]{2,1,0:T(8,128)(2,1)} %bitcast.15), calls=%async_computation | async-start | bytes 1441792 | tf_op jit(solution)/shard_map/all_to_all | solution.py:261
  12.4 4.8 %collective-permute-start.1 = (bf16[128,2048]{1,0:T(8,128)(2,1)S(1)}, bf16[128,2048]{1,0:T(8,128)(2,1)S(1)}, u32[]{:S(2)}, u32[]{:S(2)}) collective-permute-start(bf16[128,2048]{1,0:T(8,128)(2,1)S(1)} %copy-done.4), channel_id=1, source_target_pairs={{0,32},{16,48},{32,0},{48,16},{1,33},{17,49},{33,1},{49,17},{2,34}... | collective-permute-start | bytes 1572872 | tf_op jit(solution)/shard_map/ppermute | solution.py:266
  17.2 2.2 %collective-permute-start = (bf16[128,2048]{1,0:T(8,128)(2,1)S(1)}, bf16[128,2048]{1,0:T(8,128)(2,1)S(1)}, u32[]{:S(2)}, u32[]{:S(2)}) collective-permute-start(bf16[128,2048]{1,0:T(8,128)(2,1)S(1)} %copy-done.4), channel_id=1, source_target_pairs={{0,16},{16,32},{32,48},{48,0},{1,17},{17,33},{33,49},{49,1},{2,18}... | collective-permute-start | bytes 1572872 | tf_op jit(solution)/shard_map/ppermute | solution.py:266
  19.4 4.3 %collective-permute-start.2 = (bf16[128,2048]{1,0:T(8,128)(2,1)S(1)}, bf16[128,2048]{1,0:T(8,128)(2,1)S(1)}, u32[]{:S(2)}, u32[]{:S(2)}) collective-permute-start(bf16[128,2048]{1,0:T(8,128)(2,1)S(1)} %copy-done.4), channel_id=1, source_target_pairs={{0,48},{16,0},{32,16},{48,32},{1,49},{17,1},{33,17},{49,33},{2,50}... | collective-permute-start | bytes 1572872 | tf_op jit(solution)/shard_map/ppermute | solution.py:266
  23.7 8.8 %all-to-all-done = bf16[16,176,128]{2,1,0:T(8,128)(2,1)S(1)} async-done(((bf16[16,176,128]{2,1,0:T(8,128)(2,1)}), bf16[16,176,128]{2,1,0:T(8,128)(2,1)S(1)}, u32[]{:S(2)}, u32[]{:S(2)}) %all-to-all-start) | async-done | bytes 720928 | tf_op jit(solution)/shard_map/all_to_all | solution.py:261
  32.6 0.3 shard_map.85
  32.9 0.0 copy-start.1
  32.9 0.8 copy-done.1
  33.7 11.1 %all_to_all.25.refs_0_ = f32[8,4,512]{2,1,0:T(4,128)S(1)} all-to-all(f32[8,4,512]{2,1,0:T(4,128)S(1)} %get-tuple-element.21), channel_id=1, replica_groups=mesh['y'=4,'core'=2,'x'=4,'zh'=4,'zl'=4] {'y','core'}, dimensions={0} | all-to-all | bytes 131072 | tf_op jit(solution)/shard_map/all_to_all | solution.py:261
  44.8 0.6 shard_map.88
  45.4 12.2 %all-to-all-start.2 = ((bf16[16,4,512]{2,1,0:T(4,128)(2,1)}), bf16[16,4,512]{2,1,0:T(4,128)(2,1)S(1)}, u32[]{:S(2)}, u32[]{:S(2)}) async-start(bf16[16,4,512]{2,1,0:T(4,128)(2,1)} %shard_map.88), calls=%async_computation.2 | async-start | bytes 131072 | tf_op jit(solution)/shard_map/all_to_all | solution.py:261
  57.7 0.0 copy-start.6
  57.7 0.7 copy-done.5
  58.4 0.2 copy-done.6
  58.6 0.2 copy-done.7
  58.8 4.8 %shard_map.86 = (f32[4,256,512]{2,1,0:T(8,128)}, bf16[4,256,512]{2,1,0:T(8,128)(2,1)}) custom-call(s32[1]{0:T(128)} %bitcast.2.x_ref, s32[1]{0:T(128)} %bitcast.3.core_ref.refs_0_, f32[1,2048]{1,0:T(1,128)} %bitcast.17, f32[8,512]{1,0:T(8,128)} %copy-done.2, bf16[4,128,512]{2,1,0:T(8,128)(2,1)} %copy-done.1, bf16[128,2048]{1,0:T(8,128)(2,1)} %refs_0_.1, ...), custom_call_target="tpu_custom_call" | custom-call | bytes 134217728 | tf_op jit(solution)/shard_map/pallas_call | solution.py:323
  63.6 5.6 %all-to-all-done.2.refs_0_ = bf16[16,4,512]{2,1,0:T(4,128)(2,1)S(1)} async-done(((bf16[16,4,512]{2,1,0:T(4,128)(2,1)}), bf16[16,4,512]{2,1,0:T(4,128)(2,1)S(1)}, u32[]{:S(2)}, u32[]{:S(2)}) %all-to-all-start.2) | async-done | bytes 65568 | tf_op jit(solution)/shard_map/all_to_all | solution.py:261
  69.2 4.1 %collective-permute-start.3 = (bf16[4,256,512]{2,1,0:T(8,128)(2,1)}, bf16[4,256,512]{2,1,0:T(8,128)(2,1)S(1)}, u32[]{:S(2)}, u32[]{:S(2)}) collective-permute-start(bf16[4,256,512]{2,1,0:T(8,128)(2,1)} %get-tuple-element.22), channel_id=1, source_target_pairs={{0,64},{64,0},{1,65},{65,1},{2,66},{66,2},{3,67},{67,3},{4,68},{68... | collective-permute-start | bytes 3145736 | tf_op jit(solution)/shard_map/ppermute | solution.py:266
  73.4 1.6 %copy-done = f32[4,256,512]{2,1,0:T(8,128)S(1)} copy-done((f32[4,256,512]{2,1,0:T(8,128)S(1)}, f32[4,256,512]{2,1,0:T(8,128)}, u32[]{:S(2)}) %copy-start) | copy-done | bytes 2097176
  75.0 0.2 shard_map.87.own_ref
  75.2 0.7 collective-permute-done.3.got_ref
  75.8 0.2 shard_map.90
  76.0 22.2 %all_to_all.26 = bf16[16,80,512]{2,1,0:T(8,128)(2,1)S(1)} all-to-all(bf16[16,80,512]{2,1,0:T(8,128)(2,1)S(1)} %bitcast.11), channel_id=1, replica_groups=mesh['y'=4,'core'=2,'x'=4,'zh'=4,'zl'=4] {'y','x'}, dimensions={0} | all-to-all | bytes 2621440 | tf_op jit(solution)/shard_map/all_to_all | solution.py:261
  98.3 0.8 shard_map.91
  99.1 4.9 %all-to-all-start.4 = ((bf16[4,4,16,512]{3,2,1,0:T(8,128)(2,1)}), bf16[4,4,16,512]{3,2,1,0:T(8,128)(2,1)S(1)}, u32[]{:S(2)}, u32[]{:S(2)}) async-start(bf16[4,4,16,512]{3,2,1,0:T(8,128)(2,1)} %get-tuple-element.24), calls=%async_computation.4 | async-start | bytes 524288 | tf_op jit(solution)/shard_map/all_to_all | solution.py:261
  104.0 3.5 %collective-permute-start.4 = (bf16[4,4,16,512]{3,2,1,0:T(8,128)(2,1)S(1)}, bf16[4,4,16,512]{3,2,1,0:T(8,128)(2,1)S(1)}, u32[]{:S(2)}, u32[]{:S(2)}) collective-permute-start(bf16[4,4,16,512]{3,2,1,0:T(8,128)(2,1)S(1)} %get-tuple-element.27.refs_1_), channel_id=1, source_target_pairs={{0,64},{64,0},{1,65},{65,1},{2,66},{66,2},{3,67},{67,3},{4,68},{68... | collective-permute-start | bytes 786440 | tf_op jit(solution)/shard_map/ppermute | solution.py:266
  107.5 1.1 collective-permute-done.4.refs_2_
  108.6 1.0 shard_map.93
  109.7 10.4 %all-to-all-done.4.in_ref = bf16[4,4,16,512]{3,2,1,0:T(8,128)(2,1)S(1)} async-done(((bf16[4,4,16,512]{3,2,1,0:T(8,128)(2,1)}), bf16[4,4,16,512]{3,2,1,0:T(8,128)(2,1)S(1)}, u32[]{:S(2)}, u32[]{:S(2)}) %all-to-all-start.4) | async-done | bytes 262176 | tf_op jit(solution)/shard_map/all_to_all | solution.py:261
  120.1 0.7 shard_map.92
  (12 shorter events, 0.0 us)
Async XLA Ops:
  0.6 11.8 %copy-start.4 = (bf16[128,2048]{1,0:T(8,128)(2,1)S(1)}, bf16[128,2048]{1,0:T(8,128)(2,1)}, u32[]{:S(2)}) copy-start(bf16[128,2048]{1,0:T(8,128)(2,1)} %refs_0_.1) | copy-start | bytes 1572868
  3.4 29.2 %all-to-all-start = ((bf16[16,176,128]{2,1,0:T(8,128)(2,1)}), bf16[16,176,128]{2,1,0:T(8,128)(2,1)S(1)}, u32[]{:S(2)}, u32[]{:S(2)}) async-start(bf16[16,176,128]{2,1,0:T(8,128)(2,1)} %bitcast.15), calls=%async_computation | async-start | bytes 1441792 | tf_op jit(solution)/shard_map/all_to_all | solution.py:261
  12.4 45.2 %collective-permute-start.1 = (bf16[128,2048]{1,0:T(8,128)(2,1)S(1)}, bf16[128,2048]{1,0:T(8,128)(2,1)S(1)}, u32[]{:S(2)}, u32[]{:S(2)}) collective-permute-start(bf16[128,2048]{1,0:T(8,128)(2,1)S(1)} %copy-done.4), channel_id=1, source_target_pairs={{0,32},{16,48},{32,0},{48,16},{1,33},{17,49},{33,1},{49,17},{2,34}... | collective-permute-start | bytes 1572872 | tf_op jit(solution)/shard_map/ppermute | solution.py:266
  17.2 40.4 %collective-permute-start = (bf16[128,2048]{1,0:T(8,128)(2,1)S(1)}, bf16[128,2048]{1,0:T(8,128)(2,1)S(1)}, u32[]{:S(2)}, u32[]{:S(2)}) collective-permute-start(bf16[128,2048]{1,0:T(8,128)(2,1)S(1)} %copy-done.4), channel_id=1, source_target_pairs={{0,16},{16,32},{32,48},{48,0},{1,17},{17,33},{33,49},{49,1},{2,18}... | collective-permute-start | bytes 1572872 | tf_op jit(solution)/shard_map/ppermute | solution.py:266
  19.4 38.3 %collective-permute-start.2 = (bf16[128,2048]{1,0:T(8,128)(2,1)S(1)}, bf16[128,2048]{1,0:T(8,128)(2,1)S(1)}, u32[]{:S(2)}, u32[]{:S(2)}) collective-permute-start(bf16[128,2048]{1,0:T(8,128)(2,1)S(1)} %copy-done.4), channel_id=1, source_target_pairs={{0,48},{16,0},{32,16},{48,32},{1,49},{17,1},{33,17},{49,33},{2,50}... | collective-permute-start | bytes 1572872 | tf_op jit(solution)/shard_map/ppermute | solution.py:266
  32.9 0.8 copy-start.1
  33.7 11.1 %copy-start.2 = (f32[8,512]{1,0:T(8,128)}, f32[8,512]{1,0:T(8,128)S(1)}, u32[]{:S(2)}) copy-start(f32[8,512]{1,0:T(8,128)S(1)} %get-tuple-element.17.scale_in) | copy-start | bytes 49156
  45.4 23.8 %all-to-all-start.2 = ((bf16[16,4,512]{2,1,0:T(4,128)(2,1)}), bf16[16,4,512]{2,1,0:T(4,128)(2,1)S(1)}, u32[]{:S(2)}, u32[]{:S(2)}) async-start(bf16[16,4,512]{2,1,0:T(4,128)(2,1)} %shard_map.88), calls=%async_computation.2 | async-start | bytes 131072 | tf_op jit(solution)/shard_map/all_to_all | solution.py:261
  57.7 0.8 copy-start.5
  57.7 0.9 copy-start.6
  57.7 1.1 copy-start.7
  69.2 6.6 %collective-permute-start.3 = (bf16[4,256,512]{2,1,0:T(8,128)(2,1)}, bf16[4,256,512]{2,1,0:T(8,128)(2,1)S(1)}, u32[]{:S(2)}, u32[]{:S(2)}) collective-permute-start(bf16[4,256,512]{2,1,0:T(8,128)(2,1)} %get-tuple-element.22), channel_id=1, source_target_pairs={{0,64},{64,0},{1,65},{65,1},{2,66},{66,2},{3,67},{67,3},{4,68},{68... | collective-permute-start | bytes 3145736 | tf_op jit(solution)/shard_map/ppermute | solution.py:266
  73.4 1.6 %copy-start = (f32[4,256,512]{2,1,0:T(8,128)S(1)}, f32[4,256,512]{2,1,0:T(8,128)}, u32[]{:S(2)}) copy-start(f32[4,256,512]{2,1,0:T(8,128)} %get-tuple-element.19.source) | copy-start | bytes 6291460
  76.0 44.1 %copy-start.3 = (s32[128]{0:T(128)S(1)}, s32[128]{0:T(128)}, u32[]{:S(2)}) copy-start(s32[128]{0:T(128)} %param.9) | copy-start | bytes 1540
  99.1 21.0 %all-to-all-start.4 = ((bf16[4,4,16,512]{3,2,1,0:T(8,128)(2,1)}), bf16[4,4,16,512]{3,2,1,0:T(8,128)(2,1)S(1)}, u32[]{:S(2)}, u32[]{:S(2)}) async-start(bf16[4,4,16,512]{3,2,1,0:T(8,128)(2,1)} %get-tuple-element.24), calls=%async_computation.4 | async-start | bytes 524288 | tf_op jit(solution)/shard_map/all_to_all | solution.py:261
  104.0 4.7 %collective-permute-start.4 = (bf16[4,4,16,512]{3,2,1,0:T(8,128)(2,1)S(1)}, bf16[4,4,16,512]{3,2,1,0:T(8,128)(2,1)S(1)}, u32[]{:S(2)}, u32[]{:S(2)}) collective-permute-start(bf16[4,4,16,512]{3,2,1,0:T(8,128)(2,1)S(1)} %get-tuple-element.27.refs_1_), channel_id=1, source_target_pairs={{0,64},{64,0},{1,65},{65,1},{2,66},{66,2},{3,67},{67,3},{4,68},{68... | collective-permute-start | bytes 786440 | tf_op jit(solution)/shard_map/ppermute | solution.py:266

commit v6 on v5

--- a/solution.py
+++ b/solution.py
@@ -7,7 +7,7 @@
 
 AXES = ("y", "core", "x", "zh", "zl")
 LANES = 128
-AUX = 16
+AUX = 8
 VMEM = pl.BlockSpec(memory_space=pltpu.VMEM)
 SMEM = pl.BlockSpec(memory_space=pltpu.SMEM)
 PARAMS = pltpu.CompilerParams(vmem_limit_bytes=20 * 1024 * 1024)
@@ -56,19 +56,21 @@
     gains = jnp.sum(jnp.where(hit, gain_ref[...], 0.0), axis=1, keepdims=True)
     copies[0].wait()
     hidden = hidden_ref[...]
-    hidden_f = hidden.astype(jnp.float32)
-    squares = jnp.sum(hidden_f * hidden_f, axis=1, keepdims=True)
-    picked = lax.dot_general(
-        jnp.where(hit, 1.0, 0.0).astype(jnp.bfloat16),
+    both = lax.dot_general(
+        jnp.concatenate([jnp.where(hit, 1.0, 0.0).astype(jnp.bfloat16), hidden], axis=0),
         hidden,
         (((1,), (1,)), ((), ())),
         preferred_element_type=jnp.float32,
-    ).astype(jnp.bfloat16)
+    )
+    picked = both[:n_union].astype(jnp.bfloat16)
+    row = lax.broadcasted_iota(jnp.int32, (toks, LANES), 0)
     lane = lax.broadcasted_iota(jnp.int32, (toks, LANES), 1)
-    table = jnp.zeros((toks, LANES), jnp.float32)
+    squares = jnp.sum(jnp.where(row == lane, both[n_union:], 0.0), axis=0, keepdims=True)
+    gains = jnp.broadcast_to(gains, (n_union, LANES)).T[:1]
+    table = jnp.zeros((AUX, LANES), jnp.float32)
     for place, part in enumerate(split3(squares) + split3(gains)):
-        table = jnp.where(lane == place, part, table)
-    extra = table.T[:AUX].astype(jnp.bfloat16)
+        table = jnp.where(row[:AUX] == place, part, table)
+    extra = table.astype(jnp.bfloat16)
     for x in range(n_x):
         for z in range(n_zl):
             packed_ref[x, z, toks : toks + per] = picked[per * z : per * (z + 1)]
@@ -95,7 +97,7 @@
         right = jnp.concatenate([in_ref[x, z, :toks] for z in range(n_zl)], axis=1)
         total = total + jnp.dot(normed, right, preferred_element_type=jnp.float32)
         out_ref[x] = right
-        table = jnp.zeros((AUX // 2, LANES), jnp.float32) + scale
+        table = jnp.zeros((AUX, LANES), jnp.float32) + scale
         scale_ref[:, x * LANES : (x + 1) * LANES] = table
     count, few, _ = union_ref.shape
     for i in range(count):
@@ -296,7 +298,7 @@
         lambda *refs: unpack(float(width * n_zl), *refs),
         (
             shape((n_x, toks, cols), bf16),
-            shape((AUX // 2, n_x * LANES), f32),
+            shape((AUX, n_x * LANES), f32),
             shape((n_y * n_core, few, cols), f32),
         ),
         (at_zl, packed.reshape((n_x, n_zl) + packed.shape[1:])),

time: 123 us -> 123 us (level)
  no operation moved by 1% of the time
where the time goes in v6:
time: 123 us; the launch traced here: 120 us
  starting transfers between devices  45 us (37%)
  blocking collectives  33.3 us (27%)
  waiting for transfers between devices  25.9 us (21%)
  Pallas kernels  11.6 us (9%)
  local copies, waits for them, and re-layouts  3.5 us (3%)
    all_to_all x2, blocking collectives, exchange(): return lax.all_to_all(v, axes, split_axis=0, concat_axis=0, tiled=True)  33.3 us
    all_to_all x3, starting transfers between devices, exchange(): return lax.all_to_all(v, axes, split_axis=0, concat_axis=0, tiled=True)  26.1 us
    all_to_all x3, waiting for transfers between devices, exchange(): return lax.all_to_all(v, axes, split_axis=0, concat_axis=0, tiled=True)  24.1 us
    ppermute x5, starting transfers between devices, shift(): return lax.ppermute(v, axis, [(i, (i + by) % count) for i in range(count)])  18.9 us
    pallas_call x1, Pallas kernels, per_device(): pl.pallas_call(multiply, out_shape=(half, shape(half.shape, bf16)), in_sp...  4.82 us
    pallas_call x7, Pallas kernels, call(): pl.pallas_call(body, out_shape=out_shape, in_specs=[SMEM] * scalars + [VM...  3.74 us
    unnamed x16, local copies, waits for them, and re-layouts  3.5 us
    pallas_call x1, Pallas kernels, per_device(): pl.pallas_call(prepare, out_shape=shape((n_x, n_zl, toks + per + AUX, LAN...  2.88 us
  transfers between devices with their start and end apart: 8, of which 5 were waited for; matrix products, arithmetic and copies ran while one was open for 0% of the time, Pallas kernels for 6%

profile of v6, /device:TPU:1, one launch (start us, length us, event | category | flops | bytes accessed | tf_op | source)
XLA Modules:
  0.0 120.3 jit_solution(12392335330790571627)
XLA Ops:
  0.6 0.0 copy-start.4
  0.6 2.9 %shard_map.84 = bf16[4,4,168,128]{3,2,1,0:T(8,128)(2,1)} custom-call(s32[1]{0:T(128)} %bitcast.5.zl_ref.refs_0_, bf16[128,2048]{1,0:T(8,128)(2,1)} %refs_0_.1, bf16[128,256]{1,0:T(8,128)(2,1)} %key_in.1, bf16[128,256]{1,0:T(8,128)(2,1)} %value_in.1, s32[1,128]{1,0:T(1,128)} %bitcast.13, f32[1,2048]{1,0:T(1,128)} %bitcast.16), custom_call_target="tpu_custom_call" | custom-call | tf_op jit(solution)/shard_map/pallas_call | solution.py:286
  3.5 9.0 %all-to-all-start = ((bf16[16,168,128]{2,1,0:T(8,128)(2,1)}), bf16[16,168,128]{2,1,0:T(8,128)(2,1)S(1)}, u32[]{:S(2)}, u32[]{:S(2)}) async-start(bf16[16,168,128]{2,1,0:T(8,128)(2,1)} %bitcast.15), calls=%async_computation | async-start | bytes 1376256 | tf_op jit(solution)/shard_map/all_to_all | solution.py:263
  12.6 4.8 %collective-permute-start.1 = (bf16[128,2048]{1,0:T(8,128)(2,1)S(1)}, bf16[128,2048]{1,0:T(8,128)(2,1)S(1)}, u32[]{:S(2)}, u32[]{:S(2)}) collective-permute-start(bf16[128,2048]{1,0:T(8,128)(2,1)S(1)} %copy-done.4), channel_id=1, source_target_pairs={{0,32},{16,48},{32,0},{48,16},{1,33},{17,49},{33,1},{49,17},{2,34}... | collective-permute-start | bytes 1572872 | tf_op jit(solution)/shard_map/ppermute | solution.py:268
  17.4 2.2 %collective-permute-start = (bf16[128,2048]{1,0:T(8,128)(2,1)S(1)}, bf16[128,2048]{1,0:T(8,128)(2,1)S(1)}, u32[]{:S(2)}, u32[]{:S(2)}) collective-permute-start(bf16[128,2048]{1,0:T(8,128)(2,1)S(1)} %copy-done.4), channel_id=1, source_target_pairs={{0,16},{16,32},{32,48},{48,0},{1,17},{17,33},{33,49},{49,1},{2,18}... | collective-permute-start | bytes 1572872 | tf_op jit(solution)/shard_map/ppermute | solution.py:268
  19.6 4.3 %collective-permute-start.2 = (bf16[128,2048]{1,0:T(8,128)(2,1)S(1)}, bf16[128,2048]{1,0:T(8,128)(2,1)S(1)}, u32[]{:S(2)}, u32[]{:S(2)}) collective-permute-start(bf16[128,2048]{1,0:T(8,128)(2,1)S(1)} %copy-done.4), channel_id=1, source_target_pairs={{0,48},{16,0},{32,16},{48,32},{1,49},{17,1},{33,17},{49,33},{2,50}... | collective-permute-start | bytes 1572872 | tf_op jit(solution)/shard_map/ppermute | solution.py:268
  23.9 8.1 %all-to-all-done = bf16[16,168,128]{2,1,0:T(8,128)(2,1)S(1)} async-done(((bf16[16,168,128]{2,1,0:T(8,128)(2,1)}), bf16[16,168,128]{2,1,0:T(8,128)(2,1)S(1)}, u32[]{:S(2)}, u32[]{:S(2)}) %all-to-all-start) | async-done | bytes 688160 | tf_op jit(solution)/shard_map/all_to_all | solution.py:263
  32.0 0.3 shard_map.85
  32.3 0.0 copy-start.1
  32.3 0.8 copy-done.1
  33.1 11.1 %all_to_all.25.refs_0_ = f32[8,4,512]{2,1,0:T(4,128)S(1)} all-to-all(f32[8,4,512]{2,1,0:T(4,128)S(1)} %get-tuple-element.21), channel_id=1, replica_groups=mesh['y'=4,'core'=2,'x'=4,'zh'=4,'zl'=4] {'y','core'}, dimensions={0} | all-to-all | bytes 131072 | tf_op jit(solution)/shard_map/all_to_all | solution.py:263
  44.2 0.6 shard_map.88
  44.9 12.2 %all-to-all-start.2 = ((bf16[16,4,512]{2,1,0:T(4,128)(2,1)}), bf16[16,4,512]{2,1,0:T(4,128)(2,1)S(1)}, u32[]{:S(2)}, u32[]{:S(2)}) async-start(bf16[16,4,512]{2,1,0:T(4,128)(2,1)} %shard_map.88), calls=%async_computation.2 | async-start | bytes 131072 | tf_op jit(solution)/shard_map/all_to_all | solution.py:263
  57.1 0.0 copy-start.6
  57.1 0.7 copy-done.5
  57.9 0.2 copy-done.6
  58.1 0.2 copy-done.7
  58.2 4.8 %shard_map.86 = (f32[4,256,512]{2,1,0:T(8,128)}, bf16[4,256,512]{2,1,0:T(8,128)(2,1)}) custom-call(s32[1]{0:T(128)} %bitcast.2.x_ref, s32[1]{0:T(128)} %bitcast.3.core_ref.refs_0_, f32[1,2048]{1,0:T(1,128)} %bitcast.17, f32[8,512]{1,0:T(8,128)} %copy-done.2, bf16[4,128,512]{2,1,0:T(8,128)(2,1)} %copy-done.1, bf16[128,2048]{1,0:T(8,128)(2,1)} %refs_0_.1, ...), custom_call_target="tpu_custom_call" | custom-call | bytes 134217728 | tf_op jit(solution)/shard_map/pallas_call | solution.py:325
  63.1 5.6 %all-to-all-done.2.refs_0_ = bf16[16,4,512]{2,1,0:T(4,128)(2,1)S(1)} async-done(((bf16[16,4,512]{2,1,0:T(4,128)(2,1)}), bf16[16,4,512]{2,1,0:T(4,128)(2,1)S(1)}, u32[]{:S(2)}, u32[]{:S(2)}) %all-to-all-start.2) | async-done | bytes 65568 | tf_op jit(solution)/shard_map/all_to_all | solution.py:263
  68.7 4.1 %collective-permute-start.3 = (bf16[4,256,512]{2,1,0:T(8,128)(2,1)}, bf16[4,256,512]{2,1,0:T(8,128)(2,1)S(1)}, u32[]{:S(2)}, u32[]{:S(2)}) collective-permute-start(bf16[4,256,512]{2,1,0:T(8,128)(2,1)} %get-tuple-element.22), channel_id=1, source_target_pairs={{0,64},{64,0},{1,65},{65,1},{2,66},{66,2},{3,67},{67,3},{4,68},{68... | collective-permute-start | bytes 3145736 | tf_op jit(solution)/shard_map/ppermute | solution.py:268
  72.8 1.6 %copy-done = f32[4,256,512]{2,1,0:T(8,128)S(1)} copy-done((f32[4,256,512]{2,1,0:T(8,128)S(1)}, f32[4,256,512]{2,1,0:T(8,128)}, u32[]{:S(2)}) %copy-start) | copy-done | bytes 2097176
  74.4 0.2 shard_map.87.own_ref
  74.6 0.7 collective-permute-done.3.got_ref
  75.3 0.2 shard_map.90
  75.5 22.2 %all_to_all.26 = bf16[16,80,512]{2,1,0:T(8,128)(2,1)S(1)} all-to-all(bf16[16,80,512]{2,1,0:T(8,128)(2,1)S(1)} %bitcast.11), channel_id=1, replica_groups=mesh['y'=4,'core'=2,'x'=4,'zh'=4,'zl'=4] {'y','x'}, dimensions={0} | all-to-all | bytes 2621440 | tf_op jit(solution)/shard_map/all_to_all | solution.py:263
  97.7 0.8 shard_map.91
  98.5 4.9 %all-to-all-start.4 = ((bf16[4,4,16,512]{3,2,1,0:T(8,128)(2,1)}), bf16[4,4,16,512]{3,2,1,0:T(8,128)(2,1)S(1)}, u32[]{:S(2)}, u32[]{:S(2)}) async-start(bf16[4,4,16,512]{3,2,1,0:T(8,128)(2,1)} %get-tuple-element.24), calls=%async_computation.4 | async-start | bytes 524288 | tf_op jit(solution)/shard_map/all_to_all | solution.py:263
  103.4 3.5 %collective-permute-start.4 = (bf16[4,4,16,512]{3,2,1,0:T(8,128)(2,1)S(1)}, bf16[4,4,16,512]{3,2,1,0:T(8,128)(2,1)S(1)}, u32[]{:S(2)}, u32[]{:S(2)}) collective-permute-start(bf16[4,4,16,512]{3,2,1,0:T(8,128)(2,1)S(1)} %get-tuple-element.27.refs_1_), channel_id=1, source_target_pairs={{0,64},{64,0},{1,65},{65,1},{2,66},{66,2},{3,67},{67,3},{4,68},{68... | collective-permute-start | bytes 786440 | tf_op jit(solution)/shard_map/ppermute | solution.py:268
  107.0 1.1 collective-permute-done.4.refs_2_
  108.1 1.0 shard_map.93
  109.1 10.4 %all-to-all-done.4.in_ref = bf16[4,4,16,512]{3,2,1,0:T(8,128)(2,1)S(1)} async-done(((bf16[4,4,16,512]{3,2,1,0:T(8,128)(2,1)}), bf16[4,4,16,512]{3,2,1,0:T(8,128)(2,1)S(1)}, u32[]{:S(2)}, u32[]{:S(2)}) %all-to-all-start.4) | async-done | bytes 262176 | tf_op jit(solution)/shard_map/all_to_all | solution.py:263
  119.5 0.7 shard_map.92
  (12 shorter events, 0.0 us)
Async XLA Ops:
  0.6 11.9 %copy-start.4 = (bf16[128,2048]{1,0:T(8,128)(2,1)S(1)}, bf16[128,2048]{1,0:T(8,128)(2,1)}, u32[]{:S(2)}) copy-start(bf16[128,2048]{1,0:T(8,128)(2,1)} %refs_0_.1) | copy-start | bytes 1572868
  3.5 28.5 %all-to-all-start = ((bf16[16,168,128]{2,1,0:T(8,128)(2,1)}), bf16[16,168,128]{2,1,0:T(8,128)(2,1)S(1)}, u32[]{:S(2)}, u32[]{:S(2)}) async-start(bf16[16,168,128]{2,1,0:T(8,128)(2,1)} %bitcast.15), calls=%async_computation | async-start | bytes 1376256 | tf_op jit(solution)/shard_map/all_to_all | solution.py:263
  12.6 44.5 %collective-permute-start.1 = (bf16[128,2048]{1,0:T(8,128)(2,1)S(1)}, bf16[128,2048]{1,0:T(8,128)(2,1)S(1)}, u32[]{:S(2)}, u32[]{:S(2)}) collective-permute-start(bf16[128,2048]{1,0:T(8,128)(2,1)S(1)} %copy-done.4), channel_id=1, source_target_pairs={{0,32},{16,48},{32,0},{48,16},{1,33},{17,49},{33,1},{49,17},{2,34}... | collective-permute-start | bytes 1572872 | tf_op jit(solution)/shard_map/ppermute | solution.py:268
  17.4 39.7 %collective-permute-start = (bf16[128,2048]{1,0:T(8,128)(2,1)S(1)}, bf16[128,2048]{1,0:T(8,128)(2,1)S(1)}, u32[]{:S(2)}, u32[]{:S(2)}) collective-permute-start(bf16[128,2048]{1,0:T(8,128)(2,1)S(1)} %copy-done.4), channel_id=1, source_target_pairs={{0,16},{16,32},{32,48},{48,0},{1,17},{17,33},{33,49},{49,1},{2,18}... | collective-permute-start | bytes 1572872 | tf_op jit(solution)/shard_map/ppermute | solution.py:268
  19.6 37.6 %collective-permute-start.2 = (bf16[128,2048]{1,0:T(8,128)(2,1)S(1)}, bf16[128,2048]{1,0:T(8,128)(2,1)S(1)}, u32[]{:S(2)}, u32[]{:S(2)}) collective-permute-start(bf16[128,2048]{1,0:T(8,128)(2,1)S(1)} %copy-done.4), channel_id=1, source_target_pairs={{0,48},{16,0},{32,16},{48,32},{1,49},{17,1},{33,17},{49,33},{2,50}... | collective-permute-start | bytes 1572872 | tf_op jit(solution)/shard_map/ppermute | solution.py:268
  32.3 0.8 copy-start.1
  33.1 11.1 %copy-start.2 = (f32[8,512]{1,0:T(8,128)}, f32[8,512]{1,0:T(8,128)S(1)}, u32[]{:S(2)}) copy-start(f32[8,512]{1,0:T(8,128)S(1)} %get-tuple-element.17.scale_in) | copy-start | bytes 49156
  44.9 23.8 %all-to-all-start.2 = ((bf16[16,4,512]{2,1,0:T(4,128)(2,1)}), bf16[16,4,512]{2,1,0:T(4,128)(2,1)S(1)}, u32[]{:S(2)}, u32[]{:S(2)}) async-start(bf16[16,4,512]{2,1,0:T(4,128)(2,1)} %shard_map.88), calls=%async_computation.2 | async-start | bytes 131072 | tf_op jit(solution)/shard_map/all_to_all | solution.py:263
  57.1 0.8 copy-start.5
  57.1 0.9 copy-start.6
  57.1 1.1 copy-start.7
  68.7 6.6 %collective-permute-start.3 = (bf16[4,256,512]{2,1,0:T(8,128)(2,1)}, bf16[4,256,512]{2,1,0:T(8,128)(2,1)S(1)}, u32[]{:S(2)}, u32[]{:S(2)}) collective-permute-start(bf16[4,256,512]{2,1,0:T(8,128)(2,1)} %get-tuple-element.22), channel_id=1, source_target_pairs={{0,64},{64,0},{1,65},{65,1},{2,66},{66,2},{3,67},{67,3},{4,68},{68... | collective-permute-start | bytes 3145736 | tf_op jit(solution)/shard_map/ppermute | solution.py:268
  72.8 1.6 %copy-start = (f32[4,256,512]{2,1,0:T(8,128)S(1)}, f32[4,256,512]{2,1,0:T(8,128)}, u32[]{:S(2)}) copy-start(f32[4,256,512]{2,1,0:T(8,128)} %get-tuple-element.19.source) | copy-start | bytes 6291460
  75.5 44.1 %copy-start.3 = (s32[128]{0:T(128)S(1)}, s32[128]{0:T(128)}, u32[]{:S(2)}) copy-start(s32[128]{0:T(128)} %param.9) | copy-start | bytes 1540
  98.5 21.0 %all-to-all-start.4 = ((bf16[4,4,16,512]{3,2,1,0:T(8,128)(2,1)}), bf16[4,4,16,512]{3,2,1,0:T(8,128)(2,1)S(1)}, u32[]{:S(2)}, u32[]{:S(2)}) async-start(bf16[4,4,16,512]{3,2,1,0:T(8,128)(2,1)} %get-tuple-element.24), calls=%async_computation.4 | async-start | bytes 524288 | tf_op jit(solution)/shard_map/all_to_all | solution.py:263
  103.4 4.7 %collective-permute-start.4 = (bf16[4,4,16,512]{3,2,1,0:T(8,128)(2,1)S(1)}, bf16[4,4,16,512]{3,2,1,0:T(8,128)(2,1)S(1)}, u32[]{:S(2)}, u32[]{:S(2)}) collective-permute-start(bf16[4,4,16,512]{3,2,1,0:T(8,128)(2,1)S(1)} %get-tuple-element.27.refs_1_), channel_id=1, source_target_pairs={{0,64},{64,0},{1,65},{65,1},{2,66},{66,2},{3,67},{67,3},{4,68},{68... | collective-permute-start | bytes 786440 | tf_op jit(solution)/shard_map/ppermute | solution.py:268

commit v7 on v6

--- a/solution.py
+++ b/solution.py
@@ -112,6 +112,19 @@
         total = in_ref[j].astype(jnp.float32)
         for i in range(1, groups):
             total = total + in_ref[i * rest + j].astype(jnp.float32)
+        total = total.astype(jnp.bfloat16)
+        for to in range(out_ref.shape[0]):
+            out_ref[to, j * few : (j + 1) * few] = total
+
+
+def sum_last(groups, in_ref, out_ref):
+    count = in_ref.shape[0]
+    rest = count // groups
+    few = in_ref.shape[1]
+    for j in range(rest):
+        total = in_ref[j * groups].astype(jnp.float32)
+        for i in range(1, groups):
+            total = total + in_ref[j * groups + i].astype(jnp.float32)
         total = total.astype(jnp.bfloat16)
         for to in range(out_ref.shape[0]):
             out_ref[to, j * few : (j + 1) * few] = total
@@ -313,9 +326,9 @@
         shape((n_zh * n_zl, few, cols), bf16),
         (outliers,),
     )
-    outliers = exchange(outliers, ("zh", "zl"))
+    outliers = exchange(outliers, ("zl", "zh"))
     outliers = call(
-        lambda *refs: sum_spread(n_zh, *refs),
+        lambda *refs: sum_last(n_zh, *refs),
         shape((1, n_zl * few, cols), bf16),
         (outliers,),
     )

time: 123 us -> 123 us (level)
  no operation moved by 1% of the time
where the time goes in v7:
time: 123 us; the launch traced here: 120 us
  starting transfers between devices  44.9 us (37%)
  blocking collectives  33.3 us (27%)
  waiting for transfers between devices  26 us (21%)
  Pallas kernels  11.6 us (9%)
  local copies, waits for them, and re-layouts  3.5 us (3%)
    all_to_all x2, blocking collectives, exchange(): return lax.all_to_all(v, axes, split_axis=0, concat_axis=0, tiled=True)  33.3 us
    all_to_all x3, starting transfers between devices, exchange(): return lax.all_to_all(v, axes, split_axis=0, concat_axis=0, tiled=True)  25.7 us
    all_to_all x3, waiting for transfers between devices, exchange(): return lax.all_to_all(v, axes, split_axis=0, concat_axis=0, tiled=True)  24.2 us
    ppermute x5, starting transfers between devices, shift(): return lax.ppermute(v, axis, [(i, (i + by) % count) for i in range(count)])  19.2 us
    pallas_call x1, Pallas kernels, per_device(): pl.pallas_call(multiply, out_shape=(half, shape(half.shape, bf16)), in_sp...  4.82 us
    pallas_call x7, Pallas kernels, call(): pl.pallas_call(body, out_shape=out_shape, in_specs=[SMEM] * scalars + [VM...  3.74 us
    unnamed x16, local copies, waits for them, and re-layouts  3.5 us
    pallas_call x1, Pallas kernels, per_device(): pl.pallas_call(prepare, out_shape=shape((n_x, n_zl, toks + per + AUX, LAN...  2.88 us
  transfers between devices with their start and end apart: 8, of which 5 were waited for; matrix products, arithmetic and copies ran while one was open for 0% of the time, Pallas kernels for 6%

profile of v7, /device:TPU:1, one launch (start us, length us, event | category | flops | bytes accessed | tf_op | source)
XLA Modules:
  0.0 120.3 jit_solution(6991954323091842481)
XLA Ops:
  0.6 0.0 copy-start.4
  0.6 2.9 %shard_map.84 = bf16[4,4,168,128]{3,2,1,0:T(8,128)(2,1)} custom-call(s32[1]{0:T(128)} %bitcast.5.zl_ref.refs_0_, bf16[128,2048]{1,0:T(8,128)(2,1)} %refs_0_.1, bf16[128,256]{1,0:T(8,128)(2,1)} %key_in.1, bf16[128,256]{1,0:T(8,128)(2,1)} %value_in.1, s32[1,128]{1,0:T(1,128)} %bitcast.13, f32[1,2048]{1,0:T(1,128)} %bitcast.16), custom_call_target="tpu_custom_call" | custom-call | tf_op jit(solution)/shard_map/pallas_call | solution.py:299
  3.5 9.0 %all-to-all-start = ((bf16[16,168,128]{2,1,0:T(8,128)(2,1)}), bf16[16,168,128]{2,1,0:T(8,128)(2,1)S(1)}, u32[]{:S(2)}, u32[]{:S(2)}) async-start(bf16[16,168,128]{2,1,0:T(8,128)(2,1)} %bitcast.15), calls=%async_computation | async-start | bytes 1376256 | tf_op jit(solution)/shard_map/all_to_all | solution.py:276
  12.6 4.8 %collective-permute-start.1 = (bf16[128,2048]{1,0:T(8,128)(2,1)S(1)}, bf16[128,2048]{1,0:T(8,128)(2,1)S(1)}, u32[]{:S(2)}, u32[]{:S(2)}) collective-permute-start(bf16[128,2048]{1,0:T(8,128)(2,1)S(1)} %copy-done.4), channel_id=1, source_target_pairs={{0,32},{16,48},{32,0},{48,16},{1,33},{17,49},{33,1},{49,17},{2,34}... | collective-permute-start | bytes 1572872 | tf_op jit(solution)/shard_map/ppermute | solution.py:281
  17.4 2.2 %collective-permute-start = (bf16[128,2048]{1,0:T(8,128)(2,1)S(1)}, bf16[128,2048]{1,0:T(8,128)(2,1)S(1)}, u32[]{:S(2)}, u32[]{:S(2)}) collective-permute-start(bf16[128,2048]{1,0:T(8,128)(2,1)S(1)} %copy-done.4), channel_id=1, source_target_pairs={{0,16},{16,32},{32,48},{48,0},{1,17},{17,33},{33,49},{49,1},{2,18}... | collective-permute-start | bytes 1572872 | tf_op jit(solution)/shard_map/ppermute | solution.py:281
  19.6 4.3 %collective-permute-start.2 = (bf16[128,2048]{1,0:T(8,128)(2,1)S(1)}, bf16[128,2048]{1,0:T(8,128)(2,1)S(1)}, u32[]{:S(2)}, u32[]{:S(2)}) collective-permute-start(bf16[128,2048]{1,0:T(8,128)(2,1)S(1)} %copy-done.4), channel_id=1, source_target_pairs={{0,48},{16,0},{32,16},{48,32},{1,49},{17,1},{33,17},{49,33},{2,50}... | collective-permute-start | bytes 1572872 | tf_op jit(solution)/shard_map/ppermute | solution.py:281
  23.9 8.1 %all-to-all-done = bf16[16,168,128]{2,1,0:T(8,128)(2,1)S(1)} async-done(((bf16[16,168,128]{2,1,0:T(8,128)(2,1)}), bf16[16,168,128]{2,1,0:T(8,128)(2,1)S(1)}, u32[]{:S(2)}, u32[]{:S(2)}) %all-to-all-start) | async-done | bytes 688160 | tf_op jit(solution)/shard_map/all_to_all | solution.py:276
  32.0 0.3 shard_map.85
  32.3 0.0 copy-start.1
  32.3 0.8 copy-done.1
  33.1 11.1 %all_to_all.25.refs_0_ = f32[8,4,512]{2,1,0:T(4,128)S(1)} all-to-all(f32[8,4,512]{2,1,0:T(4,128)S(1)} %get-tuple-element.21), channel_id=1, replica_groups=mesh['y'=4,'core'=2,'x'=4,'zh'=4,'zl'=4] {'y','core'}, dimensions={0} | all-to-all | bytes 131072 | tf_op jit(solution)/shard_map/all_to_all | solution.py:276
  44.2 0.6 shard_map.88
  44.9 12.2 %all-to-all-start.2 = ((bf16[16,4,512]{2,1,0:T(4,128)(2,1)}), bf16[16,4,512]{2,1,0:T(4,128)(2,1)S(1)}, u32[]{:S(2)}, u32[]{:S(2)}) async-start(bf16[16,4,512]{2,1,0:T(4,128)(2,1)} %shard_map.88), calls=%async_computation.2 | async-start | bytes 131072 | tf_op jit(solution)/shard_map/all_to_all | solution.py:276
  57.1 0.7 copy-done.5
  57.9 0.2 copy-done.6
  58.1 0.2 copy-done.7
  58.2 4.8 %shard_map.86 = (f32[4,256,512]{2,1,0:T(8,128)}, bf16[4,256,512]{2,1,0:T(8,128)(2,1)}) custom-call(s32[1]{0:T(128)} %bitcast.2.x_ref, s32[1]{0:T(128)} %bitcast.3.core_ref.refs_0_, f32[1,2048]{1,0:T(1,128)} %bitcast.17, f32[8,512]{1,0:T(8,128)} %copy-done.2, bf16[4,128,512]{2,1,0:T(8,128)(2,1)} %copy-done.1, bf16[128,2048]{1,0:T(8,128)(2,1)} %refs_0_.1, ...), custom_call_target="tpu_custom_call" | custom-call | bytes 134217728 | tf_op jit(solution)/shard_map/pallas_call | solution.py:338
  63.1 5.7 %all-to-all-done.2.refs_0_ = bf16[16,4,512]{2,1,0:T(4,128)(2,1)S(1)} async-done(((bf16[16,4,512]{2,1,0:T(4,128)(2,1)}), bf16[16,4,512]{2,1,0:T(4,128)(2,1)S(1)}, u32[]{:S(2)}, u32[]{:S(2)}) %all-to-all-start.2) | async-done | bytes 65568 | tf_op jit(solution)/shard_map/all_to_all | solution.py:276
  68.8 4.4 %collective-permute-start.3 = (bf16[4,256,512]{2,1,0:T(8,128)(2,1)}, bf16[4,256,512]{2,1,0:T(8,128)(2,1)S(1)}, u32[]{:S(2)}, u32[]{:S(2)}) collective-permute-start(bf16[4,256,512]{2,1,0:T(8,128)(2,1)} %get-tuple-element.22), channel_id=1, source_target_pairs={{0,64},{64,0},{1,65},{65,1},{2,66},{66,2},{3,67},{67,3},{4,68},{68... | collective-permute-start | bytes 3145736 | tf_op jit(solution)/shard_map/ppermute | solution.py:281
  73.2 1.6 %copy-done = f32[4,256,512]{2,1,0:T(8,128)S(1)} copy-done((f32[4,256,512]{2,1,0:T(8,128)S(1)}, f32[4,256,512]{2,1,0:T(8,128)}, u32[]{:S(2)}) %copy-start) | copy-done | bytes 2097176
  74.8 0.2 shard_map.87.own_ref
  75.0 0.7 collective-permute-done.3.got_ref
  75.7 0.2 shard_map.90
  75.9 0.0 copy-start.3
  75.9 22.2 %all_to_all.26 = bf16[16,80,512]{2,1,0:T(8,128)(2,1)S(1)} all-to-all(bf16[16,80,512]{2,1,0:T(8,128)(2,1)S(1)} %bitcast.11), channel_id=1, replica_groups=mesh['y'=4,'core'=2,'x'=4,'zh'=4,'zl'=4] {'y','x'}, dimensions={0} | all-to-all | bytes 2621440 | tf_op jit(solution)/shard_map/all_to_all | solution.py:276
  98.1 0.8 shard_map.91
  99.0 4.5 %all-to-all-start.4 = ((bf16[4,4,16,512]{3,2,1,0:T(8,128)(2,1)}), bf16[4,4,16,512]{3,2,1,0:T(8,128)(2,1)S(1)}, u32[]{:S(2)}, u32[]{:S(2)}) async-start(bf16[4,4,16,512]{3,2,1,0:T(8,128)(2,1)} %get-tuple-element.24), calls=%async_computation.4 | async-start | bytes 524288 | tf_op jit(solution)/shard_map/all_to_all | solution.py:276
  103.4 3.5 %collective-permute-start.4 = (bf16[4,4,16,512]{3,2,1,0:T(8,128)(2,1)S(1)}, bf16[4,4,16,512]{3,2,1,0:T(8,128)(2,1)S(1)}, u32[]{:S(2)}, u32[]{:S(2)}) collective-permute-start(bf16[4,4,16,512]{3,2,1,0:T(8,128)(2,1)S(1)} %get-tuple-element.27.refs_1_), channel_id=1, source_target_pairs={{0,64},{64,0},{1,65},{65,1},{2,66},{66,2},{3,67},{67,3},{4,68},{68... | collective-permute-start | bytes 786440 | tf_op jit(solution)/shard_map/ppermute | solution.py:281
  107.0 1.1 collective-permute-done.4.refs_2_
  108.1 1.0 shard_map.93
  109.1 10.4 %all-to-all-done.4.in_ref = bf16[4,4,16,512]{3,2,1,0:T(8,128)(2,1)S(1)} async-done(((bf16[4,4,16,512]{3,2,1,0:T(8,128)(2,1)}), bf16[4,4,16,512]{3,2,1,0:T(8,128)(2,1)S(1)}, u32[]{:S(2)}, u32[]{:S(2)}) %all-to-all-start.4) | async-done | bytes 262176 | tf_op jit(solution)/shard_map/all_to_all | solution.py:276
  119.5 0.7 shard_map.92
  (12 shorter events, 0.0 us)
Async XLA Ops:
  0.6 11.9 %copy-start.4 = (bf16[128,2048]{1,0:T(8,128)(2,1)S(1)}, bf16[128,2048]{1,0:T(8,128)(2,1)}, u32[]{:S(2)}) copy-start(bf16[128,2048]{1,0:T(8,128)(2,1)} %refs_0_.1) | copy-start | bytes 1572868
  3.5 28.5 %all-to-all-start = ((bf16[16,168,128]{2,1,0:T(8,128)(2,1)}), bf16[16,168,128]{2,1,0:T(8,128)(2,1)S(1)}, u32[]{:S(2)}, u32[]{:S(2)}) async-start(bf16[16,168,128]{2,1,0:T(8,128)(2,1)} %bitcast.15), calls=%async_computation | async-start | bytes 1376256 | tf_op jit(solution)/shard_map/all_to_all | solution.py:276
  12.6 44.5 %collective-permute-start.1 = (bf16[128,2048]{1,0:T(8,128)(2,1)S(1)}, bf16[128,2048]{1,0:T(8,128)(2,1)S(1)}, u32[]{:S(2)}, u32[]{:S(2)}) collective-permute-start(bf16[128,2048]{1,0:T(8,128)(2,1)S(1)} %copy-done.4), channel_id=1, source_target_pairs={{0,32},{16,48},{32,0},{48,16},{1,33},{17,49},{33,1},{49,17},{2,34}... | collective-permute-start | bytes 1572872 | tf_op jit(solution)/shard_map/ppermute | solution.py:281
  17.4 39.7 %collective-permute-start = (bf16[128,2048]{1,0:T(8,128)(2,1)S(1)}, bf16[128,2048]{1,0:T(8,128)(2,1)S(1)}, u32[]{:S(2)}, u32[]{:S(2)}) collective-permute-start(bf16[128,2048]{1,0:T(8,128)(2,1)S(1)} %copy-done.4), channel_id=1, source_target_pairs={{0,16},{16,32},{32,48},{48,0},{1,17},{17,33},{33,49},{49,1},{2,18}... | collective-permute-start | bytes 1572872 | tf_op jit(solution)/shard_map/ppermute | solution.py:281
  19.6 37.6 %collective-permute-start.2 = (bf16[128,2048]{1,0:T(8,128)(2,1)S(1)}, bf16[128,2048]{1,0:T(8,128)(2,1)S(1)}, u32[]{:S(2)}, u32[]{:S(2)}) collective-permute-start(bf16[128,2048]{1,0:T(8,128)(2,1)S(1)} %copy-done.4), channel_id=1, source_target_pairs={{0,48},{16,0},{32,16},{48,32},{1,49},{17,1},{33,17},{49,33},{2,50}... | collective-permute-start | bytes 1572872 | tf_op jit(solution)/shard_map/ppermute | solution.py:281
  32.3 0.8 copy-start.1
  33.1 11.1 %copy-start.2 = (f32[8,512]{1,0:T(8,128)}, f32[8,512]{1,0:T(8,128)S(1)}, u32[]{:S(2)}) copy-start(f32[8,512]{1,0:T(8,128)S(1)} %get-tuple-element.17.scale_in) | copy-start | bytes 49156
  44.9 23.9 %all-to-all-start.2 = ((bf16[16,4,512]{2,1,0:T(4,128)(2,1)}), bf16[16,4,512]{2,1,0:T(4,128)(2,1)S(1)}, u32[]{:S(2)}, u32[]{:S(2)}) async-start(bf16[16,4,512]{2,1,0:T(4,128)(2,1)} %shard_map.88), calls=%async_computation.2 | async-start | bytes 131072 | tf_op jit(solution)/shard_map/all_to_all | solution.py:276
  57.1 0.8 copy-start.5
  57.1 0.9 copy-start.6
  57.1 1.1 copy-start.7
  68.8 6.9 %collective-permute-start.3 = (bf16[4,256,512]{2,1,0:T(8,128)(2,1)}, bf16[4,256,512]{2,1,0:T(8,128)(2,1)S(1)}, u32[]{:S(2)}, u32[]{:S(2)}) collective-permute-start(bf16[4,256,512]{2,1,0:T(8,128)(2,1)} %get-tuple-element.22), channel_id=1, source_target_pairs={{0,64},{64,0},{1,65},{65,1},{2,66},{66,2},{3,67},{67,3},{4,68},{68... | collective-permute-start | bytes 3145736 | tf_op jit(solution)/shard_map/ppermute | solution.py:281
  73.2 1.6 %copy-start = (f32[4,256,512]{2,1,0:T(8,128)S(1)}, f32[4,256,512]{2,1,0:T(8,128)}, u32[]{:S(2)}) copy-start(f32[4,256,512]{2,1,0:T(8,128)} %get-tuple-element.19.source) | copy-start | bytes 6291460
  75.9 43.6 %copy-start.3 = (s32[128]{0:T(128)S(1)}, s32[128]{0:T(128)}, u32[]{:S(2)}) copy-start(s32[128]{0:T(128)} %param.9) | copy-start | bytes 1540
  99.0 20.6 %all-to-all-start.4 = ((bf16[4,4,16,512]{3,2,1,0:T(8,128)(2,1)}), bf16[4,4,16,512]{3,2,1,0:T(8,128)(2,1)S(1)}, u32[]{:S(2)}, u32[]{:S(2)}) async-start(bf16[4,4,16,512]{3,2,1,0:T(8,128)(2,1)} %get-tuple-element.24), calls=%async_computation.4 | async-start | bytes 524288 | tf_op jit(solution)/shard_map/all_to_all | solution.py:276
  103.4 4.7 %collective-permute-start.4 = (bf16[4,4,16,512]{3,2,1,0:T(8,128)(2,1)S(1)}, bf16[4,4,16,512]{3,2,1,0:T(8,128)(2,1)S(1)}, u32[]{:S(2)}, u32[]{:S(2)}) collective-permute-start(bf16[4,4,16,512]{3,2,1,0:T(8,128)(2,1)S(1)} %get-tuple-element.27.refs_1_), channel_id=1, source_target_pairs={{0,64},{64,0},{1,65},{65,1},{2,66},{66,2},{3,67},{67,3},{4,68},{68... | collective-permute-start | bytes 786440 | tf_op jit(solution)/shard_map/ppermute | solution.py:281

commit v8 on v6

--- a/solution.py
+++ b/solution.py
@@ -101,7 +101,7 @@
         scale_ref[:, x * LANES : (x + 1) * LANES] = table
     count, few, _ = union_ref.shape
     for i in range(count):
-        union_ref[i] = total[i * few : (i + 1) * few]
+        union_ref[i] = total[i * few : (i + 1) * few].astype(union_ref.dtype)
 
 
 def sum_spread(groups, in_ref, out_ref):
@@ -299,7 +299,7 @@
         (
             shape((n_x, toks, cols), bf16),
             shape((AUX, n_x * LANES), f32),
-            shape((n_y * n_core, few, cols), f32),
+            shape((n_y * n_core, few, cols), bf16),
         ),
         (at_zl, packed.reshape((n_x, n_zl) + packed.shape[1:])),
         1,

time: 123 us -> 122 us (level)
  no operation moved by 1% of the time
where the time goes in v8:
time: 122 us; the launch traced here: 120 us
  starting transfers between devices  45 us (37%)
  blocking collectives  33.2 us (27%)
  waiting for transfers between devices  25.9 us (21%)
  Pallas kernels  11.6 us (10%)
  local copies, waits for them, and re-layouts  3.5 us (3%)
    all_to_all x2, blocking collectives, exchange(): return lax.all_to_all(v, axes, split_axis=0, concat_axis=0, tiled=True)  33.2 us
    all_to_all x3, starting transfers between devices, exchange(): return lax.all_to_all(v, axes, split_axis=0, concat_axis=0, tiled=True)  26.1 us
    all_to_all x3, waiting for transfers between devices, exchange(): return lax.all_to_all(v, axes, split_axis=0, concat_axis=0, tiled=True)  24.1 us
    ppermute x5, starting transfers between devices, shift(): return lax.ppermute(v, axis, [(i, (i + by) % count) for i in range(count)])  18.9 us
    pallas_call x1, Pallas kernels, per_device(): pl.pallas_call(multiply, out_shape=(half, shape(half.shape, bf16)), in_sp...  4.82 us
    pallas_call x7, Pallas kernels, call(): pl.pallas_call(body, out_shape=out_shape, in_specs=[SMEM] * scalars + [VM...  3.74 us
    unnamed x16, local copies, waits for them, and re-layouts  3.5 us
    pallas_call x1, Pallas kernels, per_device(): pl.pallas_call(prepare, out_shape=shape((n_x, n_zl, toks + per + AUX, LAN...  2.88 us
  transfers between devices with their start and end apart: 8, of which 5 were waited for; matrix products, arithmetic and copies ran while one was open for 0% of the time, Pallas kernels for 6%

profile of v8, /device:TPU:1, one launch (start us, length us, event | category | flops | bytes accessed | tf_op | source)
XLA Modules:
  0.0 120.1 jit_solution(4589021968636942005)
XLA Ops:
  0.6 0.0 copy-start.4
  0.6 2.9 %shard_map.84 = bf16[4,4,168,128]{3,2,1,0:T(8,128)(2,1)} custom-call(s32[1]{0:T(128)} %bitcast.5.zl_ref.refs_0_, bf16[128,2048]{1,0:T(8,128)(2,1)} %refs_0_.1, bf16[128,256]{1,0:T(8,128)(2,1)} %key_in.1, bf16[128,256]{1,0:T(8,128)(2,1)} %value_in.1, s32[1,128]{1,0:T(1,128)} %bitcast.13, f32[1,2048]{1,0:T(1,128)} %bitcast.16), custom_call_target="tpu_custom_call" | custom-call | tf_op jit(solution)/shard_map/pallas_call | solution.py:286
  3.5 9.0 %all-to-all-start = ((bf16[16,168,128]{2,1,0:T(8,128)(2,1)}), bf16[16,168,128]{2,1,0:T(8,128)(2,1)S(1)}, u32[]{:S(2)}, u32[]{:S(2)}) async-start(bf16[16,168,128]{2,1,0:T(8,128)(2,1)} %bitcast.15), calls=%async_computation | async-start | bytes 1376256 | tf_op jit(solution)/shard_map/all_to_all | solution.py:263
  12.6 4.8 %collective-permute-start.1 = (bf16[128,2048]{1,0:T(8,128)(2,1)S(1)}, bf16[128,2048]{1,0:T(8,128)(2,1)S(1)}, u32[]{:S(2)}, u32[]{:S(2)}) collective-permute-start(bf16[128,2048]{1,0:T(8,128)(2,1)S(1)} %copy-done.4), channel_id=1, source_target_pairs={{0,32},{16,48},{32,0},{48,16},{1,33},{17,49},{33,1},{49,17},{2,34}... | collective-permute-start | bytes 1572872 | tf_op jit(solution)/shard_map/ppermute | solution.py:268
  17.4 2.2 %collective-permute-start = (bf16[128,2048]{1,0:T(8,128)(2,1)S(1)}, bf16[128,2048]{1,0:T(8,128)(2,1)S(1)}, u32[]{:S(2)}, u32[]{:S(2)}) collective-permute-start(bf16[128,2048]{1,0:T(8,128)(2,1)S(1)} %copy-done.4), channel_id=1, source_target_pairs={{0,16},{16,32},{32,48},{48,0},{1,17},{17,33},{33,49},{49,1},{2,18}... | collective-permute-start | bytes 1572872 | tf_op jit(solution)/shard_map/ppermute | solution.py:268
  19.6 4.3 %collective-permute-start.2 = (bf16[128,2048]{1,0:T(8,128)(2,1)S(1)}, bf16[128,2048]{1,0:T(8,128)(2,1)S(1)}, u32[]{:S(2)}, u32[]{:S(2)}) collective-permute-start(bf16[128,2048]{1,0:T(8,128)(2,1)S(1)} %copy-done.4), channel_id=1, source_target_pairs={{0,48},{16,0},{32,16},{48,32},{1,49},{17,1},{33,17},{49,33},{2,50}... | collective-permute-start | bytes 1572872 | tf_op jit(solution)/shard_map/ppermute | solution.py:268
  23.9 8.1 %all-to-all-done = bf16[16,168,128]{2,1,0:T(8,128)(2,1)S(1)} async-done(((bf16[16,168,128]{2,1,0:T(8,128)(2,1)}), bf16[16,168,128]{2,1,0:T(8,128)(2,1)S(1)}, u32[]{:S(2)}, u32[]{:S(2)}) %all-to-all-start) | async-done | bytes 688160 | tf_op jit(solution)/shard_map/all_to_all | solution.py:263
  32.0 0.3 shard_map.85
  32.3 0.8 copy-done.1
  33.1 11.0 %all_to_all.25.refs_0_ = bf16[8,4,512]{2,1,0:T(4,128)(2,1)S(1)} all-to-all(bf16[8,4,512]{2,1,0:T(4,128)(2,1)S(1)} %get-tuple-element.21), channel_id=1, replica_groups=mesh['y'=4,'core'=2,'x'=4,'zh'=4,'zl'=4] {'y','core'}, dimensions={0} | all-to-all | bytes 65536 | tf_op jit(solution)/shard_map/all_to_all | solution.py:263
  44.1 0.6 shard_map.88
  44.7 12.2 %all-to-all-start.2 = ((bf16[16,4,512]{2,1,0:T(4,128)(2,1)}), bf16[16,4,512]{2,1,0:T(4,128)(2,1)S(1)}, u32[]{:S(2)}, u32[]{:S(2)}) async-start(bf16[16,4,512]{2,1,0:T(4,128)(2,1)} %shard_map.88), calls=%async_computation.2 | async-start | bytes 131072 | tf_op jit(solution)/shard_map/all_to_all | solution.py:263
  57.0 0.0 copy-start.6
  57.0 0.7 copy-done.5
  57.7 0.2 copy-done.6
  57.9 0.2 copy-done.7
  58.1 4.8 %shard_map.86 = (f32[4,256,512]{2,1,0:T(8,128)}, bf16[4,256,512]{2,1,0:T(8,128)(2,1)}) custom-call(s32[1]{0:T(128)} %bitcast.2.x_ref, s32[1]{0:T(128)} %bitcast.3.core_ref.refs_0_, f32[1,2048]{1,0:T(1,128)} %bitcast.17, f32[8,512]{1,0:T(8,128)} %copy-done.2, bf16[4,128,512]{2,1,0:T(8,128)(2,1)} %copy-done.1, bf16[128,2048]{1,0:T(8,128)(2,1)} %refs_0_.1, ...), custom_call_target="tpu_custom_call" | custom-call | bytes 134217728 | tf_op jit(solution)/shard_map/pallas_call | solution.py:325
  62.9 5.6 %all-to-all-done.2.refs_0_ = bf16[16,4,512]{2,1,0:T(4,128)(2,1)S(1)} async-done(((bf16[16,4,512]{2,1,0:T(4,128)(2,1)}), bf16[16,4,512]{2,1,0:T(4,128)(2,1)S(1)}, u32[]{:S(2)}, u32[]{:S(2)}) %all-to-all-start.2) | async-done | bytes 65568 | tf_op jit(solution)/shard_map/all_to_all | solution.py:263
  68.5 4.1 %collective-permute-start.3 = (bf16[4,256,512]{2,1,0:T(8,128)(2,1)}, bf16[4,256,512]{2,1,0:T(8,128)(2,1)S(1)}, u32[]{:S(2)}, u32[]{:S(2)}) collective-permute-start(bf16[4,256,512]{2,1,0:T(8,128)(2,1)} %get-tuple-element.22), channel_id=1, source_target_pairs={{0,64},{64,0},{1,65},{65,1},{2,66},{66,2},{3,67},{67,3},{4,68},{68... | collective-permute-start | bytes 3145736 | tf_op jit(solution)/shard_map/ppermute | solution.py:268
  72.6 1.6 %copy-done = f32[4,256,512]{2,1,0:T(8,128)S(1)} copy-done((f32[4,256,512]{2,1,0:T(8,128)S(1)}, f32[4,256,512]{2,1,0:T(8,128)}, u32[]{:S(2)}) %copy-start) | copy-done | bytes 2097176
  74.2 0.2 shard_map.87.own_ref
  74.4 0.7 collective-permute-done.3.got_ref
  75.1 0.2 shard_map.90
  75.3 0.0 copy-start.3
  75.3 22.2 %all_to_all.26 = bf16[16,80,512]{2,1,0:T(8,128)(2,1)S(1)} all-to-all(bf16[16,80,512]{2,1,0:T(8,128)(2,1)S(1)} %bitcast.11), channel_id=1, replica_groups=mesh['y'=4,'core'=2,'x'=4,'zh'=4,'zl'=4] {'y','x'}, dimensions={0} | all-to-all | bytes 2621440 | tf_op jit(solution)/shard_map/all_to_all | solution.py:263
  97.5 0.8 shard_map.91
  98.4 4.9 %all-to-all-start.4 = ((bf16[4,4,16,512]{3,2,1,0:T(8,128)(2,1)}), bf16[4,4,16,512]{3,2,1,0:T(8,128)(2,1)S(1)}, u32[]{:S(2)}, u32[]{:S(2)}) async-start(bf16[4,4,16,512]{3,2,1,0:T(8,128)(2,1)} %get-tuple-element.24), calls=%async_computation.4 | async-start | bytes 524288 | tf_op jit(solution)/shard_map/all_to_all | solution.py:263
  103.3 3.5 %collective-permute-start.4 = (bf16[4,4,16,512]{3,2,1,0:T(8,128)(2,1)S(1)}, bf16[4,4,16,512]{3,2,1,0:T(8,128)(2,1)S(1)}, u32[]{:S(2)}, u32[]{:S(2)}) collective-permute-start(bf16[4,4,16,512]{3,2,1,0:T(8,128)(2,1)S(1)} %get-tuple-element.27.refs_1_), channel_id=1, source_target_pairs={{0,64},{64,0},{1,65},{65,1},{2,66},{66,2},{3,67},{67,3},{4,68},{68... | collective-permute-start | bytes 786440 | tf_op jit(solution)/shard_map/ppermute | solution.py:268
  106.8 1.1 collective-permute-done.4.refs_2_
  107.9 1.0 shard_map.93
  108.9 10.4 %all-to-all-done.4.in_ref = bf16[4,4,16,512]{3,2,1,0:T(8,128)(2,1)S(1)} async-done(((bf16[4,4,16,512]{3,2,1,0:T(8,128)(2,1)}), bf16[4,4,16,512]{3,2,1,0:T(8,128)(2,1)S(1)}, u32[]{:S(2)}, u32[]{:S(2)}) %all-to-all-start.4) | async-done | bytes 262176 | tf_op jit(solution)/shard_map/all_to_all | solution.py:263
  119.3 0.7 shard_map.92
  (12 shorter events, 0.0 us)
Async XLA Ops:
  0.6 11.9 %copy-start.4 = (bf16[128,2048]{1,0:T(8,128)(2,1)S(1)}, bf16[128,2048]{1,0:T(8,128)(2,1)}, u32[]{:S(2)}) copy-start(bf16[128,2048]{1,0:T(8,128)(2,1)} %refs_0_.1) | copy-start | bytes 1572868
  3.5 28.5 %all-to-all-start = ((bf16[16,168,128]{2,1,0:T(8,128)(2,1)}), bf16[16,168,128]{2,1,0:T(8,128)(2,1)S(1)}, u32[]{:S(2)}, u32[]{:S(2)}) async-start(bf16[16,168,128]{2,1,0:T(8,128)(2,1)} %bitcast.15), calls=%async_computation | async-start | bytes 1376256 | tf_op jit(solution)/shard_map/all_to_all | solution.py:263
  12.6 44.4 %collective-permute-start.1 = (bf16[128,2048]{1,0:T(8,128)(2,1)S(1)}, bf16[128,2048]{1,0:T(8,128)(2,1)S(1)}, u32[]{:S(2)}, u32[]{:S(2)}) collective-permute-start(bf16[128,2048]{1,0:T(8,128)(2,1)S(1)} %copy-done.4), channel_id=1, source_target_pairs={{0,32},{16,48},{32,0},{48,16},{1,33},{17,49},{33,1},{49,17},{2,34}... | collective-permute-start | bytes 1572872 | tf_op jit(solution)/shard_map/ppermute | solution.py:268
  17.4 39.6 %collective-permute-start = (bf16[128,2048]{1,0:T(8,128)(2,1)S(1)}, bf16[128,2048]{1,0:T(8,128)(2,1)S(1)}, u32[]{:S(2)}, u32[]{:S(2)}) collective-permute-start(bf16[128,2048]{1,0:T(8,128)(2,1)S(1)} %copy-done.4), channel_id=1, source_target_pairs={{0,16},{16,32},{32,48},{48,0},{1,17},{17,33},{33,49},{49,1},{2,18}... | collective-permute-start | bytes 1572872 | tf_op jit(solution)/shard_map/ppermute | solution.py:268
  19.6 37.4 %collective-permute-start.2 = (bf16[128,2048]{1,0:T(8,128)(2,1)S(1)}, bf16[128,2048]{1,0:T(8,128)(2,1)S(1)}, u32[]{:S(2)}, u32[]{:S(2)}) collective-permute-start(bf16[128,2048]{1,0:T(8,128)(2,1)S(1)} %copy-done.4), channel_id=1, source_target_pairs={{0,48},{16,0},{32,16},{48,32},{1,49},{17,1},{33,17},{49,33},{2,50}... | collective-permute-start | bytes 1572872 | tf_op jit(solution)/shard_map/ppermute | solution.py:268
  32.3 0.8 copy-start.1
  33.1 11.0 %copy-start.2 = (f32[8,512]{1,0:T(8,128)}, f32[8,512]{1,0:T(8,128)S(1)}, u32[]{:S(2)}) copy-start(f32[8,512]{1,0:T(8,128)S(1)} %get-tuple-element.17.scale_in) | copy-start | bytes 49156
  44.7 23.8 %all-to-all-start.2 = ((bf16[16,4,512]{2,1,0:T(4,128)(2,1)}), bf16[16,4,512]{2,1,0:T(4,128)(2,1)S(1)}, u32[]{:S(2)}, u32[]{:S(2)}) async-start(bf16[16,4,512]{2,1,0:T(4,128)(2,1)} %shard_map.88), calls=%async_computation.2 | async-start | bytes 131072 | tf_op jit(solution)/shard_map/all_to_all | solution.py:263
  57.0 0.8 copy-start.5
  57.0 0.9 copy-start.6
  57.0 1.1 copy-start.7
  68.5 6.6 %collective-permute-start.3 = (bf16[4,256,512]{2,1,0:T(8,128)(2,1)}, bf16[4,256,512]{2,1,0:T(8,128)(2,1)S(1)}, u32[]{:S(2)}, u32[]{:S(2)}) collective-permute-start(bf16[4,256,512]{2,1,0:T(8,128)(2,1)} %get-tuple-element.22), channel_id=1, source_target_pairs={{0,64},{64,0},{1,65},{65,1},{2,66},{66,2},{3,67},{67,3},{4,68},{68... | collective-permute-start | bytes 3145736 | tf_op jit(solution)/shard_map/ppermute | solution.py:268
  72.6 1.6 %copy-start = (f32[4,256,512]{2,1,0:T(8,128)S(1)}, f32[4,256,512]{2,1,0:T(8,128)}, u32[]{:S(2)}) copy-start(f32[4,256,512]{2,1,0:T(8,128)} %get-tuple-element.19.source) | copy-start | bytes 6291460
  75.3 44.0 %copy-start.3 = (s32[128]{0:T(128)S(1)}, s32[128]{0:T(128)}, u32[]{:S(2)}) copy-start(s32[128]{0:T(128)} %param.9) | copy-start | bytes 1540
  98.4 21.0 %all-to-all-start.4 = ((bf16[4,4,16,512]{3,2,1,0:T(8,128)(2,1)}), bf16[4,4,16,512]{3,2,1,0:T(8,128)(2,1)S(1)}, u32[]{:S(2)}, u32[]{:S(2)}) async-start(bf16[4,4,16,512]{3,2,1,0:T(8,128)(2,1)} %get-tuple-element.24), calls=%async_computation.4 | async-start | bytes 524288 | tf_op jit(solution)/shard_map/all_to_all | solution.py:263
  103.3 4.7 %collective-permute-start.4 = (bf16[4,4,16,512]{3,2,1,0:T(8,128)(2,1)S(1)}, bf16[4,4,16,512]{3,2,1,0:T(8,128)(2,1)S(1)}, u32[]{:S(2)}, u32[]{:S(2)}) collective-permute-start(bf16[4,4,16,512]{3,2,1,0:T(8,128)(2,1)S(1)} %get-tuple-element.27.refs_1_), channel_id=1, source_target_pairs={{0,64},{64,0},{1,65},{65,1},{2,66},{66,2},{3,67},{67,3},{4,68},{68... | collective-permute-start | bytes 786440 | tf_op jit(solution)/shard_map/ppermute | solution.py:268
